TPU v7x, 32 devices: a whole 2x2x4 slice. The times are simulated.
32 devices in a mesh: dp: 8 (over z, x), cls: 4 (over y, core).
Axes of the slice: x: 2, y: 2, z: 4, core: 2. Of those that a mesh axis runs over, the one named last changes fastest.
Arguments:
- images: bfloat16 [1024, 64, 512], P('dp'), may hold values from -12 to 12
- pose_slot: int32 [1024], P('dp'), may hold values from 0 to 1023, as said below
- references: bfloat16 [256, 64, 512], P('cls'), may hold values from -4 to 4
- rotation_response: float32 [36, 512], replicated, may hold values from -1 to 1
- shell_weight: float32 [64], replicated, may hold values from 0.003 to 0.03
- class_lists: int32 [1024, 2], P('dp'), may hold values from 0 to 255, as said below
- class_counts: int32 [256], P('cls'), may hold values from 0 to 19999
Outputs:
- class_gradient: float32 [4, 64, 64, 512], P('cls', 'dp')
- log_evidence: float32 [1024], P('dp')
Inputs may be any that keep to these rules, and one draw needn't show every extreme that they name: `pose_slot`: the particles of each micrograph block of 128 rows land exactly 16 in every pose block of 128 positions; each position is taken once. `class_lists`: each row names 2 different classes. Within each pose block of 128 rows every class that the block names is named by exactly 2 of its rows.
All inputs are finite; a program needn't handle non-finite values.
Results may differ from a plain program's by a relative error of at most 0.04.
Values may be sent and summed in bfloat16 or wider, within the bound.
A program may use at most 192 MiB of HBM per device.

v0:
```python
import math

import jax
import jax.numpy as jnp
from jax import lax
from jax.sharding import PartitionSpec as P

NSHELL = 64
NANG = 256
LIST = 2
MOST = 2


def combined_all(part, axis, combine):
    gathered = jax.tree.map(lambda a: lax.all_gather(a, axis), part)

    def take(source):
        return jax.tree.map(lambda a: lax.dynamic_index_in_dim(a, source, 0, False), gathered)

    return lax.fori_loop(
        1, lax.axis_size(axis), lambda source, state: combine(state, take(source)), take(0)
    )


def angular_tables(points):
    positions = jnp.arange(points, dtype=jnp.int32)
    product = positions[:, None] * positions[None, :] % points
    angles = product.astype(jnp.float32) * (2.0 * math.pi / points)
    cosine = jnp.cos(angles) / math.sqrt(points)
    sine_part = jnp.sin(angles) / math.sqrt(points)
    upper_half = jnp.concatenate([cosine, -sine_part], axis=1)
    lower_half = jnp.concatenate([sine_part, cosine], axis=1)
    return jnp.concatenate([upper_half, lower_half], axis=0)


def combine(earlier_part, later_part):
    larger = jnp.maximum(earlier_part[0], later_part[0])
    merged = earlier_part[1] * jnp.exp(earlier_part[0] - larger) + later_part[1] * jnp.exp(
        later_part[0] - larger
    )
    return (larger, merged)


def local(
    images, pose_slot, references, rotation_response, shell_weight, class_lists, class_counts
):
    dp_count = lax.axis_size("dp")
    column = lax.axis_index("cls")
    blocksize = images.shape[0]
    per_pair = blocksize // dp_count
    row_width = 2 * NANG
    full_table = angular_tables(NANG)
    forward = full_table.astype(jnp.bfloat16)
    inverse = full_table.T
    target_block = pose_slot // blocksize
    target_row = pose_slot % blocksize
    dest_onehot = (target_block[:, None] == jnp.arange(dp_count, dtype=jnp.int32)[None, :]).astype(
        jnp.int32
    )
    before_dest = jnp.cumsum(dest_onehot, axis=0) - dest_onehot
    within = jnp.sum(before_dest * dest_onehot, axis=1)
    position = target_block * per_pair + within
    rows_index = jnp.arange(blocksize, dtype=jnp.int32)
    send_order = jnp.sum(
        jnp.where(position[None, :] == rows_index[:, None], rows_index[None, :], 0), axis=1
    )
    slot_tags = target_row[send_order].astype(jnp.bfloat16).reshape(dp_count, per_pair)

    def transform(field_rows):
        leading = field_rows.shape[:-1]
        result = jnp.dot(
            field_rows.reshape(-1, row_width), forward, preferred_element_type=jnp.float32
        )
        return result.astype(jnp.bfloat16).reshape(leading + (row_width,))

    outgoing = images[send_order].reshape(dp_count, per_pair, NSHELL, row_width)
    arrived, arrived_tags = (
        lax.all_to_all(outgoing, "dp", split_axis=0, concat_axis=0, tiled=True),
        lax.all_to_all(slot_tags, "dp", split_axis=0, concat_axis=0, tiled=True),
    )
    flat_tags = arrived_tags.reshape(blocksize).astype(jnp.int32)
    source_row = jnp.sum(
        jnp.where(flat_tags[None, :] == rows_index[:, None], rows_index[None, :], 0), axis=1
    )
    image_hat = transform(arrived.reshape((blocksize,) + arrived.shape[2:])[source_row])
    ref_hat = transform(references)
    col_classes = references.shape[0]
    weighted = (ref_hat.astype(jnp.float32) * shell_weight[None, :, None]).astype(jnp.bfloat16)

    def contract(left_op, right_op):
        return jnp.einsum("pjm,kjm->pkm", left_op, right_op, preferred_element_type=jnp.float32)

    image_re = image_hat[..., :NANG]
    image_im = image_hat[..., NANG:]
    ref_re = weighted[..., :NANG]
    ref_im = weighted[..., NANG:]
    cross_term = jnp.concatenate(
        [
            contract(image_re, ref_re) + contract(image_im, ref_im),
            contract(image_im, ref_re) - contract(image_re, ref_im),
        ],
        axis=-1,
    )
    log_prior = jnp.log1p(class_counts.astype(jnp.float32))
    dense_scores = (
        jnp.einsum("pkn,rn->pkr", cross_term, rotation_response, precision=lax.Precision.HIGHEST)
        + log_prior[None, :, None]
    )
    local_class = class_lists - column * col_classes
    inside = (local_class >= 0) & (local_class < col_classes)
    picker = (
        local_class[..., None] == jnp.arange(col_classes, dtype=jnp.int32)[None, None, :]
    ).astype(jnp.float32)
    scores = jnp.einsum("pak,pkr->par", picker, dense_scores, precision=lax.Precision.HIGHEST)
    scores = jnp.where(inside[..., None], scores, -1e30)
    top_local = jnp.max(scores, axis=(1, 2))
    total_local = jnp.sum(
        jnp.where(inside[..., None], jnp.exp(scores - top_local[:, None, None]), 0.0), axis=(1, 2)
    )
    top_score, total_sum = combined_all((top_local, total_local), "cls", combine)
    posterior = (
        jnp.where(inside[..., None], jnp.exp(scores - top_score[:, None, None]), 0.0)
        / total_sum[:, None, None]
    )
    evidence = top_score + jnp.log(total_sum)
    rot_re = rotation_response[:, :NANG]
    rot_im = rotation_response[:, NANG:]
    coef_table = jnp.concatenate([rot_re, -rot_im, rot_re * rot_re + rot_im * rot_im], axis=1)
    coef_rows = jnp.einsum("par,rn->pan", posterior, coef_table, precision=lax.Precision.HIGHEST)
    post_sum = jnp.sum(posterior, axis=2)
    own_ref = ref_hat.astype(jnp.float32)
    entries = blocksize * LIST
    flat_local = local_class.reshape(entries)
    flat_inside = inside.reshape(entries)
    class_onehot = (
        flat_local[:, None] == jnp.arange(col_classes, dtype=jnp.int32)[None, :]
    ).astype(jnp.int32)
    before_class = jnp.cumsum(class_onehot, axis=0) - class_onehot
    slot_rank = jnp.sum(before_class * class_onehot, axis=1)
    slot_id = jnp.where(flat_inside, flat_local * MOST + slot_rank, -1)
    slot_count = col_classes * MOST
    chooser = slot_id[None, :] == jnp.arange(slot_count, dtype=jnp.int32)[:, None]
    particle = jnp.arange(entries, dtype=jnp.int32) // LIST
    slot_particle = jnp.sum(jnp.where(chooser, particle[None, :], 0), axis=1)
    chooser_f = chooser.astype(jnp.float32)
    slot_coef = jnp.dot(
        chooser_f, coef_rows.reshape(entries, 3 * NANG), precision=lax.Precision.HIGHEST
    ).reshape(col_classes, MOST, 1, 3 * NANG)
    slot_weight = jnp.dot(
        chooser_f, post_sum.reshape(entries), precision=lax.Precision.HIGHEST
    ).reshape(col_classes, MOST)
    source = (
        image_hat[slot_particle].reshape(col_classes, MOST, NSHELL, row_width).astype(jnp.float32)
    )
    class_ref = own_ref[:, None]
    coef_re = slot_coef[..., :NANG]
    coef_im = slot_coef[..., NANG : 2 * NANG]
    volume = slot_coef[..., 2 * NANG :]
    grad_re = (
        source[..., :NANG] * coef_re - source[..., NANG:] * coef_im - volume * class_ref[..., :NANG]
    )
    grad_im = (
        source[..., :NANG] * coef_im + source[..., NANG:] * coef_re - volume * class_ref[..., NANG:]
    )
    buffer = jnp.concatenate([grad_re, grad_im], axis=-1).reshape(
        dp_count, col_classes // dp_count, MOST, NSHELL, row_width
    )
    weights_out = slot_weight.reshape(dp_count, col_classes // dp_count, MOST)
    grad_rows = lax.all_to_all(
        buffer.astype(jnp.bfloat16), "dp", split_axis=0, concat_axis=0, tiled=True
    ).astype(buffer.dtype)
    weight_rows = lax.all_to_all(
        weights_out.astype(jnp.bfloat16), "dp", split_axis=0, concat_axis=0, tiled=True
    ).astype(weights_out.dtype)
    numer_sum = jnp.sum(grad_rows, axis=(0, 2))
    scaled = numer_sum / (1.0 + jnp.sum(weight_rows, axis=(0, 2)))[:, None, None]
    result = jnp.dot(scaled.reshape(-1, row_width), inverse, precision=lax.Precision.HIGHEST)
    gradient = result.reshape(numer_sum.shape)
    return (gradient[None], evidence)


def solution(mesh):
    return jax.shard_map(
        local,
        mesh=mesh,
        in_specs=(
            P("dp", None, None),
            P("dp"),
            P("cls", None, None),
            P(),
            P(),
            P("dp", None),
            P("cls"),
        ),
        out_specs=(P("cls", "dp", None, None), P("dp")),
        check_vma=False,
    )
```

profile of v0, /device:TPU:0, one launch (start us, length us, event | category | flops | bytes accessed | tf_op | source)
XLA Modules:
  0.0 597.0 jit_solution(9419831516727389686)
XLA Ops:
  0.6 0.7 and_select_fusion.1
  1.4 0.2 reduce_window_sum.26
  1.6 0.2 select_reduce_fusion.4
  1.9 1.2 gather_fusion.1
  3.1 0.7 convert_element_type.133
  3.8 7.3 %all-to-all-start.1 = ((bf16[8,1,16]{2,1,0:T(2,128)(2,1)}), bf16[8,1,16]{2,1,0:T(2,128)(2,1)S(1)}, u32[]{:S(2)}, u32[]{:S(2)}) async-start(bf16[8,1,16]{2,1,0:T(2,128)(2,1)} %convert_element_type.133), calls=%async_computation.1 | async-start | bytes 8192 | tf_op jit(solution)/shard_map/all_to_all | solution.py:79
  11.1 9.9 %gather_fusion = bf16[128,64,512]{2,1,0:T(8,128)(2,1)} fusion(bf16[128,64,512]{2,1,0:T(8,128)(2,1)} %param.9, s32[1024]{0:T(1024)S(1)} %pad_clamp_fusion.2), kind=kCustom, calls=%fused_computation | custom fusion | bytes 16777728 | tf_op jit(solution)/shard_map/gather | solution.py:76
  21.0 6.4 %all-to-all-start = ((bf16[8,16,64,512]{3,2,1,0:T(8,128)(2,1)}), bf16[8,16,64,512]{3,2,1,0:T(8,128)(2,1)}, u32[]{:S(2)}, u32[]{:S(2)}) async-start(bf16[8,16,64,512]{3,2,1,0:T(8,128)(2,1)} %bitcast.114), calls=%async_computation | async-start | bytes 16777216 | tf_op jit(solution)/shard_map/all_to_all | solution.py:78
  27.5 0.1 eq.144
  27.7 0.5 copy-done.11
  28.1 0.1 reshape.233
  28.3 1.0 fusion.29
  29.3 1.1 sine_multiply_fusion
  30.4 8.0 %convert_bitcast_fusion = f32[4096,512]{0,1:T(8,128)} fusion(bf16[4096,512]{1,0:T(8,128)(2,1)} %bitcast.117, f32[256,256]{1,0:T(8,128)S(1)} %get-tuple-element.170, f32[256,256]{1,0:T(8,128)S(1)} %get-tuple-element.169, f32[256,256]{1,0:T(8,128)S(1)} %fusion.29), kind=kOutput, calls=%fused_computation.15 | convolution fusion | flops 2153775104 | bytes 13369344 | tf_op jit(solution)/shard_map/dot_general | solution.py:71
  38.4 9.0 %copy.55 = f32[4096,512]{1,0:T(8,128)} copy(f32[4096,512]{0,1:T(8,128)} %convert_bitcast_fusion) | data formatting | bytes 16777216 | tf_op jit(solution)/shard_map/convert_element_type | solution.py:88
  47.4 16.3 %copy.56 = f32[64,64,512]{1,0,2:T(8,128)} copy(f32[64,64,512]{2,1,0:T(8,128)} %bitcast.109) | data formatting | bytes 16777216 | tf_op jit(solution)/shard_map/convert_element_type | solution.py:88
  63.7 0.1 copy.49
  63.8 0.6 reduce-window.6
  64.4 0.2 slice_reduce_fusion
  64.7 0.2 reshape.232
  64.8 0.5 multiply_add_fusion.2
  65.6 0.6 pad_clamp_fusion
  66.2 0.6 convert_log-plus-one_fusion
  66.8 0.8 broadcast_compare_fusion
  67.6 0.7 fusion.50
  68.2 8.8 %slice_bitcast_fusion.1 = (f32[64,64,256]{2,1,0:T(8,128)}, f32[64,64,256]{2,1,0:T(8,128)}) fusion(f32[64,1,64,512]{3,2,0,1:T(8,128)} %bitcast.110), kind=kLoop, calls=%fused_computation.22 | loop fusion | bytes 16777216 | tf_op jit(solution)/shard_map/mul | solution.py:160
  77.1 2.3 copy-done
  79.4 4.4 multiply_convert_fusion
  84.1 125.8 %all-to-all-done = bf16[8,16,64,512]{3,2,1,0:T(8,128)(2,1)} async-done(((bf16[8,16,64,512]{3,2,1,0:T(8,128)(2,1)}), bf16[8,16,64,512]{3,2,1,0:T(8,128)(2,1)}, u32[]{:S(2)}, u32[]{:S(2)}) %all-to-all-start) | async-done | bytes 8388640 | tf_op jit(solution)/shard_map/all_to_all | solution.py:78
  209.9 10.0 %gather_fusion.2 = bf16[128,64,512]{2,1,0:T(8,128)(2,1)} fusion(bf16[128,64,512]{2,1,0:T(8,128)(2,1)} %bitcast.5, s32[1024]{0:T(1024)S(1)} %pad_clamp_fusion.1), kind=kCustom, calls=%fused_computation.2 | custom fusion | bytes 16777728 | tf_op jit(solution)/shard_map/gather | solution.py:85
  219.9 8.8 %convolution_convert_fusion = bf16[8192,512]{1,0:T(8,128)(2,1)S(1)} fusion(bf16[8192,512]{1,0:T(8,128)(2,1)} %bitcast.116, f32[256,256]{1,0:T(8,128)S(1)} %get-tuple-element.170, f32[256,256]{1,0:T(8,128)S(1)} %get-tuple-element.169, f32[256,256]{1,0:T(8,128)S(1)} %fusion.29), kind=kOutput, calls=%fused_computation.13 | convolution fusion | flops 4301258752 | bytes 17563648 | tf_op jit(solution)/shard_map/dot_general | solution.py:71
  228.7 3.8 fusion.49
  232.5 1.9 copy-done.4
  234.4 7.4 %copy.69 = bf16[128,64,256]{0,1,2:T(8,128)(2,1)} copy(bf16[128,64,256]{2,1,0:T(8,128)(2,1)} %get-tuple-element.157) | data formatting | bytes 8388608
  241.8 7.4 %copy.70 = bf16[128,64,256]{0,1,2:T(8,128)(2,1)} copy(bf16[128,64,256]{2,1,0:T(8,128)(2,1)} %get-tuple-element.158) | data formatting | bytes 8388608
  249.2 8.0 %fusion.52 = f32[256,64,128]{2,1,0:T(8,128)} fusion(bf16[64,64,512]{1,0,2:T(8,128)(2,1)} %multiply_convert_fusion, bf16[128,64,256]{0,1,2:T(8,128)(2,1)} %copy.69), kind=kOutput, calls=%fused_computation.127 | convolution fusion | flops 268435456 | bytes 16777216 | tf_op jit(solution)/shard_map/pjm,kjm->pkm/dot_general | solution.py:91
  257.2 6.6 %fusion.53 = f32[256,64,128]{2,1,0:T(8,128)} fusion(bf16[64,64,512]{1,0,2:T(8,128)(2,1)} %multiply_convert_fusion, bf16[128,64,256]{0,1,2:T(8,128)(2,1)S(1)} %copy-done.2), kind=kOutput, calls=%fused_computation.128 | convolution fusion | flops 268435456 | bytes 16777216 | tf_op jit(solution)/shard_map/pjm,kjm->pkm/dot_general | solution.py:91
  263.9 9.2 %add_bitcast_fusion = f32[128,64,256]{0,1,2:T(8,128)} fusion(f32[256,64,128]{2,1,0:T(8,128)} %fusion.52, bf16[64,64,512]{1,0,2:T(8,128)(2,1)} %multiply_convert_fusion, bf16[128,64,256]{0,1,2:T(8,128)(2,1)S(1)} %copy-done.2), kind=kOutput, calls=%fused_computation.19 | convolution fusion | flops 270532608 | bytes 25165824 | tf_op jit(solution)/shard_map/pjm,kjm->pkm/dot_general | solution.py:91
  273.1 9.2 %subtract_bitcast_fusion = f32[128,64,256]{0,1,2:T(8,128)} fusion(f32[256,64,128]{2,1,0:T(8,128)} %fusion.53, bf16[64,64,512]{1,0,2:T(8,128)(2,1)} %multiply_convert_fusion, bf16[128,64,256]{0,1,2:T(8,128)(2,1)S(1)} %copy-done.1), kind=kOutput, calls=%fused_computation.18 | convolution fusion | flops 270532608 | bytes 25165824 | tf_op jit(solution)/shard_map/pjm,kjm->pkm/dot_general | solution.py:91
  282.4 10.2 %pad_maximum_fusion = f32[128,64,512]{0,1,2:T(8,128)} fusion(f32[128,64,256]{0,1,2:T(8,128)} %subtract_bitcast_fusion, f32[128,64,256]{0,1,2:T(8,128)S(1)} %copy-done.3), kind=kLoop, calls=%fused_computation.10 | loop fusion | flops 4194304 | bytes 33554432 | tf_op jit(solution)/shard_map/concatenate | solution.py:97
  292.6 17.6 %copy.59 = f32[128,64,512]{2,1,0:T(8,128)} copy(f32[128,64,512]{0,1,2:T(8,128)} %pad_maximum_fusion) | data formatting | bytes 33554432 | tf_op jit(solution)/shard_map/concatenate | solution.py:97
  310.2 24.0 %fusion.30 = f32[128,64,36]{1,2,0:T(8,128)S(1)} fusion(f32[128,64,512]{2,1,0:T(8,128)} %copy.59, f32[36,512]{1,0:T(8,128)S(1)} %copy-done.16), kind=kOutput, calls=%fused_computation.65 | convolution fusion | flops 1811939328 | bytes 18030592 | tf_op jit(solution)/shard_map/pkn,rn->pkr/dot_general | solution.py:106
  334.2 2.6 fusion.51
  336.8 2.1 select_reduce_fusion
  339.0 5.0 all-gather.3
  344.0 5.0 all-gather.2
  349.0 0.3 while.17
  349.3 0.6 fusion.48
  350.0 0.8 fusion.19
  350.8 0.6 copy.61
  351.4 0.5 reshape.290
  352.0 0.4 convolution_bitcast_fusion.1
  352.8 10.0 %gather_fusion.3 = bf16[128,64,512]{2,1,0:T(8,128)(2,1)} fusion(bf16[128,64,512]{2,1,0:T(8,128)(2,1)} %bitcast.113, s32[1024]{0:T(1024)} %pad_clamp_fusion), kind=kCustom, calls=%fused_computation.3 | custom fusion | bytes 16777728 | tf_op jit(solution)/shard_map/gather | solution.py:153
  362.7 11.6 %convert.14 = f32[64,2,64,512]{3,2,1,0:T(8,128)} convert(bf16[64,2,64,512]{3,2,1,0:T(8,128)(2,1)} %bitcast.111) | non-fusion elementwise | flops 4194304 | bytes 25165824 | tf_op jit(solution)/shard_map/convert_element_type | solution.py:153
  374.5 0.5 fusion.23
  375.0 0.6 convert_element_type.125
  375.6 3.7 all-to-all-start.3
  379.3 12.8 %subtract_convert_fusion.1 = (bf16[64,2,64,256]{3,2,1,0:T(8,128)(2,1)}, bf16[64,2,64,256]{3,2,1,0:T(8,128)(2,1)}) fusion(f32[64,2,64,512]{3,2,1,0:T(8,128)} %convert.14, f32[64,64,256]{2,1,0:T(8,128)} %get-tuple-element.155, f32[64,2,256]{2,1,0:T(2,128)S(1)} %copy.64, f32[64,2,256]{2,1,0:T(2,128)S(1)} %copy.63, f32[64,2,256]{2,1,0:T(2,128)S(1)} %copy.62, ...), kind=kLoop, calls=%fused_computation.17 | loop fusion | flops 25165824 | bytes 33947648 | tf_op jit(solution)/shard_map/convert.6
  392.1 7.7 %pad_maximum_fusion.1 = bf16[64,2,64,512]{3,2,1,0:T(8,128)(2,1)} fusion(bf16[64,2,64,256]{3,2,1,0:T(8,128)(2,1)} %get-tuple-element.154, bf16[64,2,64,256]{3,2,1,0:T(8,128)(2,1)} %get-tuple-element.153), kind=kLoop, calls=%fused_computation.14 | loop fusion | flops 16777216 | bytes 16777216 | tf_op jit(solution)/shard_map/concatenate | solution.py:165
  399.8 6.3 %all-to-all-start.2 = ((bf16[8,8,2,64,512]{4,3,2,1,0:T(8,128)(2,1)}), bf16[8,8,2,64,512]{4,3,2,1,0:T(8,128)(2,1)}, u32[]{:S(2)}, u32[]{:S(2)}) async-start(bf16[8,8,2,64,512]{4,3,2,1,0:T(8,128)(2,1)} %bitcast.115), calls=%async_computation.2 | async-start | bytes 16777216 | tf_op jit(solution)/shard_map/all_to_all | solution.py:169
  406.1 0.5 log_add_fusion
  406.7 182.3 %all-to-all-done.2 = bf16[8,8,2,64,512]{4,3,2,1,0:T(8,128)(2,1)} async-done(((bf16[8,8,2,64,512]{4,3,2,1,0:T(8,128)(2,1)}), bf16[8,8,2,64,512]{4,3,2,1,0:T(8,128)(2,1)}, u32[]{:S(2)}, u32[]{:S(2)}) %all-to-all-start.2) | async-done | bytes 8388640 | tf_op jit(solution)/shard_map/all_to_all | solution.py:169
  589.0 4.9 convert_reduce_fusion
  593.9 2.9 convolution_bitcast_fusion
  (89 shorter events, 1.5 us)
Async XLA Ops:
  3.8 17.2 %all-to-all-start.1 = ((bf16[8,1,16]{2,1,0:T(2,128)(2,1)}), bf16[8,1,16]{2,1,0:T(2,128)(2,1)S(1)}, u32[]{:S(2)}, u32[]{:S(2)}) async-start(bf16[8,1,16]{2,1,0:T(2,128)(2,1)} %convert_element_type.133), calls=%async_computation.1 | async-start | bytes 8192 | tf_op jit(solution)/shard_map/all_to_all | solution.py:79
  21.0 6.4 %copy-start.24 = (s32[128,2]{0,1:T(2,128)S(1)}, s32[128,2]{0,1:T(2,128)}, u32[]{:S(2)}) copy-start(s32[128,2]{0,1:T(2,128)} %param.14) | copy-start | bytes 3076
  21.0 188.9 %all-to-all-start = ((bf16[8,16,64,512]{3,2,1,0:T(8,128)(2,1)}), bf16[8,16,64,512]{3,2,1,0:T(8,128)(2,1)}, u32[]{:S(2)}, u32[]{:S(2)}) async-start(bf16[8,16,64,512]{3,2,1,0:T(8,128)(2,1)} %bitcast.114), calls=%async_computation | async-start | bytes 16777216 | tf_op jit(solution)/shard_map/all_to_all | solution.py:78
  27.5 0.6 copy-start.11
  29.3 190.6 %copy-start.5 = (f32[256,256]{1,0:T(8,128)}, f32[256,256]{1,0:T(8,128)S(1)}, u32[]{:S(2)}) copy-start(f32[256,256]{1,0:T(8,128)S(1)} %fusion.29) | copy-start | bytes 786436
  30.3 189.5 %copy-start.7 = (f32[256,256]{1,0:T(8,128)}, f32[256,256]{1,0:T(8,128)S(1)}, u32[]{:S(2)}) copy-start(f32[256,256]{1,0:T(8,128)S(1)} %get-tuple-element.169) | copy-start | bytes 786436
  30.3 189.5 %copy-start.9 = (f32[256,256]{1,0:T(8,128)}, f32[256,256]{1,0:T(8,128)S(1)}, u32[]{:S(2)}) copy-start(f32[256,256]{1,0:T(8,128)S(1)} %get-tuple-element.170) | copy-start | bytes 786436
  47.4 18.8 %copy-start.27 = (s32[64]{0:T(128)S(1)}, s32[64]{0:T(128)}, u32[]{:S(2)}) copy-start(s32[64]{0:T(128)} %param.15) | copy-start | bytes 772
  47.4 20.2 %copy-start.15 = (f32[36,512]{1,0:T(8,128)S(1)}, f32[36,512]{1,0:T(8,128)}, u32[]{:S(2)}) copy-start(f32[36,512]{1,0:T(8,128)} %param.12) | copy-start | bytes 221188
  47.4 29.7 %copy-start.25 = (f32[64]{0:T(128)S(1)}, f32[64]{0:T(128)}, u32[]{:S(2)}) copy-start(f32[64]{0:T(128)} %param.13) | copy-start | bytes 772
  63.8 13.3 %copy-start.13 = (pred[128,2]{1,0:T(8,128)(4,1)}, pred[128,2]{1,0:T(8,128)(4,1)S(1)}, u32[]{:S(2)}) copy-start(pred[128,2]{1,0:T(8,128)(4,1)S(1)} %copy.49) | copy-start | bytes 772
  65.5 11.6 %copy-start.21 = (s32[256]{0:T(256)}, s32[256]{0:T(256)S(1)}, u32[]{:S(2)}) copy-start(s32[256]{0:T(256)S(1)} %add_select_fusion.1) | copy-start | bytes 3076
  68.2 11.1 %copy-start = (f32[64,64,512]{1,0,2:T(8,128)S(1)}, f32[64,64,512]{1,0,2:T(8,128)}, u32[]{:S(2)}) copy-start(f32[64,64,512]{1,0,2:T(8,128)} %copy.56) | copy-start | bytes 25165828
  228.7 5.7 copy-start.4
  249.2 8.1 %copy-start.2 = (bf16[128,64,256]{0,1,2:T(8,128)(2,1)S(1)}, bf16[128,64,256]{0,1,2:T(8,128)(2,1)}, u32[]{:S(2)}) copy-start(bf16[128,64,256]{0,1,2:T(8,128)(2,1)} %copy.70) | copy-start | bytes 12582916
  263.9 9.3 %copy-start.1 = (bf16[128,64,256]{0,1,2:T(8,128)(2,1)S(1)}, bf16[128,64,256]{0,1,2:T(8,128)(2,1)}, u32[]{:S(2)}) copy-start(bf16[128,64,256]{0,1,2:T(8,128)(2,1)} %copy.69) | copy-start | bytes 12582916
  273.1 9.2 %copy-start.3 = (f32[128,64,256]{0,1,2:T(8,128)S(1)}, f32[128,64,256]{0,1,2:T(8,128)}, u32[]{:S(2)}) copy-start(f32[128,64,256]{0,1,2:T(8,128)} %add_bitcast_fusion) | copy-start | bytes 25165828
  292.6 17.6 %copy-start.16 = (f32[36,512]{1,0:T(8,128)S(1)}, f32[36,512]{1,0:T(8,128)}, u32[]{:S(2)}) copy-start(f32[36,512]{1,0:T(8,128)} %param.12) | copy-start | bytes 221188
  310.1 24.1 %copy-start.12 = (s32[128,2]{1,0:T(8,128)S(1)}, s32[128,2]{1,0:T(8,128)}, u32[]{:S(2)}) copy-start(s32[128,2]{1,0:T(8,128)} %copy-done.11) | copy-start | bytes 3076
  310.1 24.1 %copy-start.14 = (pred[128,2]{1,0:T(8,128)(4,1)S(1)}, pred[128,2]{1,0:T(8,128)(4,1)}, u32[]{:S(2)}) copy-start(pred[128,2]{1,0:T(8,128)(4,1)} %copy-done.13) | copy-start | bytes 772
  310.1 24.1 %copy-start.26 = (f32[64]{0:T(128)S(1)}, f32[64]{0:T(128)}, u32[]{:S(2)}) copy-start(f32[64]{0:T(128)} %convert_log-plus-one_fusion) | copy-start | bytes 772
  310.1 39.8 %copy-start.17 = (f32[36,256]{1,0:T(8,128)S(1)}, f32[36,256]{1,0:T(8,128)}, u32[]{:S(2)}) copy-start(f32[36,256]{1,0:T(8,128)} %get-tuple-element.162) | copy-start | bytes 110596
  310.2 39.8 %copy-start.18 = (f32[36,256]{1,0:T(8,128)S(1)}, f32[36,256]{1,0:T(8,128)}, u32[]{:S(2)}) copy-start(f32[36,256]{1,0:T(8,128)} %get-tuple-element.163) | copy-start | bytes 110596
  310.2 39.8 %copy-start.19 = (f32[36,256]{1,0:T(8,128)S(1)}, f32[36,256]{1,0:T(8,128)}, u32[]{:S(2)}) copy-start(f32[36,256]{1,0:T(8,128)} %get-tuple-element.164) | copy-start | bytes 110596
  310.2 41.8 %copy-start.22 = (s32[256]{0:T(256)S(1)}, s32[256]{0:T(256)}, u32[]{:S(2)}) copy-start(s32[256]{0:T(256)} %copy-done.21) | copy-start | bytes 3076
  310.2 41.8 %copy-start.23 = (s32[64,2]{0,1:T(2,128)S(1)}, s32[64,2]{0,1:T(2,128)}, u32[]{:S(2)}) copy-start(s32[64,2]{0,1:T(2,128)} %multiply_add_fusion.2) | copy-start | bytes 1540
  362.7 11.8 %copy-start.20 = (pred[8,8,2,256]{3,2,1,0:T(4,128)(4,1)S(1)}, pred[8,8,2,256]{3,2,1,0:T(4,128)(4,1)}, u32[]{:S(2)}) copy-start(pred[8,8,2,256]{3,2,1,0:T(4,128)(4,1)} %broadcast_compare_fusion) | copy-start | bytes 98308
  375.6 24.2 %all-to-all-start.3 = ((bf16[8,8,2]{1,2,0:T(2,128)(2,1)}), bf16[8,8,2]{1,2,0:T(2,128)(2,1)S(1)}, u32[]{:S(2)}, u32[]{:S(2)}) async-start(bf16[8,8,2]{1,2,0:T(2,128)(2,1)} %convert_element_type.125), calls=%async_computation.3 | async-start | bytes 8192 | tf_op jit(solution)/shard_map/all_to_all | solution.py:172
  399.8 189.2 %all-to-all-start.2 = ((bf16[8,8,2,64,512]{4,3,2,1,0:T(8,128)(2,1)}), bf16[8,8,2,64,512]{4,3,2,1,0:T(8,128)(2,1)}, u32[]{:S(2)}, u32[]{:S(2)}) async-start(bf16[8,8,2,64,512]{4,3,2,1,0:T(8,128)(2,1)} %bitcast.115), calls=%async_computation.2 | async-start | bytes 16777216 | tf_op jit(solution)/shard_map/all_to_all | solution.py:169
  406.1 187.8 %copy-start.6 = (f32[256,256]{1,0:T(8,128)S(1)}, f32[256,256]{1,0:T(8,128)}, u32[]{:S(2)}) copy-start(f32[256,256]{1,0:T(8,128)} %copy-done.5) | copy-start | bytes 786436
  406.1 187.8 %copy-start.8 = (f32[256,256]{1,0:T(8,128)S(1)}, f32[256,256]{1,0:T(8,128)}, u32[]{:S(2)}) copy-start(f32[256,256]{1,0:T(8,128)} %copy-done.7) | copy-start | bytes 786436
  406.1 187.8 %copy-start.10 = (f32[256,256]{1,0:T(8,128)S(1)}, f32[256,256]{1,0:T(8,128)}, u32[]{:S(2)}) copy-start(f32[256,256]{1,0:T(8,128)} %copy-done.9) | copy-start | bytes 786436
where the time goes:
time: 601 us; the launch traced here: 597 us
  waiting for transfers between devices  308 us (51%)
  local copies, waits for them, and re-layouts  109 us (18%)
  matrix products  81.2 us (14%)
  other arithmetic  63 us (10%)
  starting transfers between devices  23.6 us (4%)
  blocking collectives  10.1 us (2%)
    all_to_all x1, waiting for transfers between devices, local(): lax.all_to_all(buffer.astype(jnp.bfloat16), 'dp', split_axis=0, concat_ax...  182 us
    all_to_all x1, waiting for transfers between devices, local(): lax.all_to_all(outgoing, 'dp', split_axis=0, concat_axis=0, tiled=True)  126 us
    dot_general x4, matrix products, contract(): jnp.einsum('pjm,kjm->pkm', left_op, right_op, preferred_element_type=jnp....  33.2 us
    convert_element_type x2, local copies, waits for them, and re-layouts, local(): ref_hat.astype(jnp.float32) * shell_weight[None, :, None]  25.3 us
    dot_general x1, matrix products, local(): jnp.einsum('pkn,rn->pkr', cross_term, rotation_response, precision=lax.Pr...  24 us
    unnamed x58, local copies, waits for them, and re-layouts  19.5 us
    concatenate x1, local copies, waits for them, and re-layouts, local(): jnp.concatenate([contract(image_re, ref_re) + contract(image_im, ref_im),...  17.6 us
    dot_general x2, matrix products, transform(): jnp.dot(field_rows.reshape(-1, row_width), forward, preferred_element_typ...  16.8 us
  transfers between devices with their start and end apart: 4, of which 2 were waited for; matrix products, arithmetic and copies ran while one was open for 14% of the time, Pallas kernels for 0%

commit v1 on v0

v1 whole, which is shorter than its diff:
```python
import functools
import math

import jax
import jax.numpy as jnp
import numpy as np
from jax import lax
from jax.experimental import pallas as pl
from jax.experimental.pallas import tpu as pltpu
from jax.sharding import PartitionSpec as P

NSHELL = 64
NANG = 256
LIST = 2
LANES = 128
ROWS = 16
MESH = pl.DeviceIdType.MESH
HIGHEST = lax.Precision.HIGHEST
VMEM_LIMIT = 56 * 1024 * 1024


def angular_tables(points):
    positions = np.arange(points)
    angles = (positions[:, None] * positions[None, :] % points).astype(np.float64) * (
        2.0 * math.pi / points
    )
    cosine = np.cos(angles) / math.sqrt(points)
    sine_part = np.sin(angles) / math.sqrt(points)
    upper_half = np.concatenate([cosine, -sine_part], axis=1)
    lower_half = np.concatenate([sine_part, cosine], axis=1)
    return np.concatenate([upper_half, lower_half], axis=0).astype(np.float32)


def score_kernel(cls_ref, xh_ref, rh_ref, sw_ref, rr_ref, bias_ref, scores_ref, stats_ref, cross):
    step = pl.program_id(0)
    block = bias_ref.shape[0] // LIST
    classes = rh_ref.shape[0]

    @pl.when(step == 0)
    def _():
        cross[...] = jnp.zeros_like(cross)

    def entry(i, carry):
        p = i // LIST
        row = (i % LIST) * block + step * ROWS + p
        k = cls_ref[row]

        @pl.when((k >= 0) & (k < classes))
        def _():
            x_re = xh_ref[p, :, :NANG].astype(jnp.float32)
            x_im = xh_ref[p, :, NANG:].astype(jnp.float32)
            c_re = rh_ref[k, :, :NANG].astype(jnp.float32)
            c_im = rh_ref[k, :, NANG:].astype(jnp.float32)
            sw = sw_ref[...]
            cross[pl.ds(row, 1), :NANG] = jnp.sum(
                (x_re * c_re + x_im * c_im) * sw, axis=0, keepdims=True
            )
            cross[pl.ds(row, 1), NANG:] = jnp.sum(
                (x_im * c_re - x_re * c_im) * sw, axis=0, keepdims=True
            )

        return carry

    lax.fori_loop(0, ROWS * LIST, entry, 0)

    @pl.when(step == pl.num_programs(0) - 1)
    def _():
        scores = (
            lax.dot_general(
                cross[...],
                rr_ref[...],
                (((1,), (1,)), ((), ())),
                precision=HIGHEST,
                preferred_element_type=jnp.float32,
            )
            + bias_ref[...]
        )
        scores_ref[...] = scores
        first, second = scores[:block], scores[block:]
        top = jnp.max(jnp.maximum(first, second), axis=1, keepdims=True)
        total = jnp.sum(jnp.exp(first - top) + jnp.exp(second - top), axis=1, keepdims=True)
        lane = lax.broadcasted_iota(jnp.int32, (block, LANES), 1)
        stats = jnp.where(lane == 0, top, total)
        stats_ref[...] = jnp.transpose(stats)[:8]


def grad_kernel(
    cls_ref, xh_ref, rh_ref, scores_ref, stats_ref, ct_ref,
    part_ref, weight_ref, evid_ref, acc, coef, post_sum, volume,
):
    step = pl.program_id(0)
    block = scores_ref.shape[0] // LIST
    classes = rh_ref.shape[0]

    @pl.when(step == 0)
    def _():
        stats = stats_ref[...]
        tops = stats[:, 0:1, :]
        top = jnp.max(tops, axis=0)
        total = jnp.sum(stats[:, 1:2, :] * jnp.exp(tops - top[None]), axis=0)
        evid_ref[...] = top + jnp.log(total)
        top_col = jnp.transpose(jnp.broadcast_to(top, (LANES, block)))
        total_col = jnp.transpose(jnp.broadcast_to(total, (LANES, block)))
        for a in range(LIST):
            rows = slice(a * block, (a + 1) * block)
            posterior = jnp.exp(scores_ref[rows] - top_col) / total_col
            post_sum[rows] = jnp.broadcast_to(
                jnp.sum(posterior, axis=1, keepdims=True), (block, LANES)
            )
            coef[rows] = jnp.dot(
                posterior, ct_ref[...], precision=HIGHEST, preferred_element_type=jnp.float32
            )
        volume[...] = jnp.zeros_like(volume)
        weight_ref[...] = jnp.zeros_like(weight_ref)

        def clear(k, carry):
            acc[k] = jnp.zeros(acc.shape[1:], jnp.float32)
            return carry

        lax.fori_loop(0, classes, clear, 0)

    def entry(i, carry):
        p = i // LIST
        row = (i % LIST) * block + step * ROWS + p
        k = cls_ref[row]

        @pl.when((k >= 0) & (k < classes))
        def _():
            x_re = xh_ref[p, :, :NANG].astype(jnp.float32)
            x_im = xh_ref[p, :, NANG:].astype(jnp.float32)
            re = coef[pl.ds(row, 1), :NANG]
            im = coef[pl.ds(row, 1), NANG : 2 * NANG]
            acc[k, :, :NANG] += x_re * re - x_im * im
            acc[k, :, NANG:] += x_re * im + x_im * re
            volume[pl.ds(k, 1), :] += coef[pl.ds(row, 1), 2 * NANG :]
            weight_ref[pl.ds(k, 1), :] += post_sum[pl.ds(row, 1), :]

        return carry

    lax.fori_loop(0, ROWS * LIST, entry, 0)

    @pl.when(step == pl.num_programs(0) - 1)
    def _():
        def finish(k, carry):
            vol = volume[pl.ds(k, 1), :]
            for half in (slice(0, NANG), slice(NANG, 2 * NANG)):
                part_ref[k, :, half] = (
                    acc[k, :, half] - vol * rh_ref[k, :, half].astype(jnp.float32)
                ).astype(jnp.bfloat16)
            return carry

        lax.fori_loop(0, classes, finish, 0)


def reduce_kernel(
    lines, groups, p_ref, out_ref, held, from_left, from_right,
    pair_send, pair_recv, right_send, right_recv, left_send, left_recv,
):
    me = lax.axis_index("dp")
    x = lax.rem(me, 2)
    z = lax.div(me, 2)
    partner = me + 1 - 2 * x
    has_left = z > 0
    has_right = z < lines - 1
    per_group = p_ref.shape[3]

    barrier = pltpu.get_barrier_semaphore()
    pl.semaphore_signal(barrier, inc=1, device_id={"dp": partner}, device_id_type=MESH)

    @pl.when(has_left)
    def _():
        pl.semaphore_signal(barrier, inc=1, device_id={"dp": me - 2}, device_id_type=MESH)

    @pl.when(has_right)
    def _():
        pl.semaphore_signal(barrier, inc=1, device_id={"dp": me + 2}, device_id_type=MESH)

    peers = 1 + has_left.astype(jnp.int32) + has_right.astype(jnp.int32)
    pl.semaphore_wait(barrier, peers)

    def where_is(t):
        g, i = lax.div(t, lines), lax.rem(t, lines)
        odd, half = lax.rem(i, 2), lax.div(i, 2)
        return (1 - odd) * (lines - 1 - half) + odd * half, g

    def pair(b, g):
        return pltpu.make_async_remote_copy(
            src_ref=p_ref.at[b, 1 - x, g], dst_ref=held.at[b, g],
            send_sem=pair_send.at[b, g], recv_sem=pair_recv.at[b, g],
            device_id={"dp": partner}, device_id_type=MESH,
        )

    def right(b, g):
        return pltpu.make_async_remote_copy(
            src_ref=held.at[b, g], dst_ref=from_left.at[b, g],
            send_sem=right_send.at[b, g], recv_sem=right_recv.at[b, g],
            device_id={"dp": me + 2}, device_id_type=MESH,
        )

    def left(b, g):
        return pltpu.make_async_remote_copy(
            src_ref=held.at[b, g], dst_ref=from_right.at[b, g],
            send_sem=left_send.at[b, g], recv_sem=left_recv.at[b, g],
            device_id={"dp": me - 2}, device_id_type=MESH,
        )

    def add(b, g, other):
        def one(c, carry):
            held[b, g, c] = (
                held[b, g, c].astype(jnp.float32) + other(c).astype(jnp.float32)
            ).astype(jnp.bfloat16)
            return carry

        lax.fori_loop(0, per_group, one, 0)

    def begin(t, carry):
        pair(*where_is(t)).start()
        return carry

    def relay(t, carry):
        b, g = where_is(t)
        pair(b, g).wait_recv()
        add(b, g, lambda c: p_ref[b, x, g, c])

        @pl.when(z < b)
        def _():
            @pl.when(has_left)
            def _():
                right(b, g).wait_recv()
                add(b, g, lambda c: from_left[b, g, c])

            right(b, g).start()

        @pl.when(z > b)
        def _():
            @pl.when(has_right)
            def _():
                left(b, g).wait_recv()
                add(b, g, lambda c: from_right[b, g, c])

            left(b, g).start()

        return carry

    def finish(g, carry):
        def own(c, inner):
            out_ref[g, c] = held[z, g, c].astype(jnp.float32)
            return inner

        lax.fori_loop(0, per_group, own, 0)

        @pl.when(has_left)
        def _():
            right(z, g).wait_recv()

            def one(c, inner):
                out_ref[g, c] += from_left[z, g, c].astype(jnp.float32)
                return inner

            lax.fori_loop(0, per_group, one, 0)

        @pl.when(has_right)
        def _():
            left(z, g).wait_recv()

            def one(c, inner):
                out_ref[g, c] += from_right[z, g, c].astype(jnp.float32)
                return inner

            lax.fori_loop(0, per_group, one, 0)

        return carry

    def drain(t, carry):
        b, g = where_is(t)
        pair(b, g).wait_send()

        @pl.when(z < b)
        def _():
            right(b, g).wait_send()

        @pl.when(z > b)
        def _():
            left(b, g).wait_send()

        return carry

    lax.fori_loop(0, lines * groups, begin, 0)
    lax.fori_loop(0, lines * groups, relay, 0)
    lax.fori_loop(0, groups, finish, 0)
    lax.fori_loop(0, lines * groups, drain, 0)


def reduce_scatter(part, dp_count):
    classes = part.shape[0]
    lines = dp_count // 2
    owned = classes // dp_count
    groups = math.gcd(4, owned)
    shape = (owned // groups,) + part.shape[1:]
    whole = pltpu.VMEM((lines, groups) + shape, jnp.bfloat16)
    sems = pltpu.SemaphoreType.DMA((lines, groups))
    out = pl.pallas_call(
        functools.partial(reduce_kernel, lines, groups),
        out_shape=jax.ShapeDtypeStruct((groups,) + shape, jnp.float32),
        in_specs=[pl.BlockSpec(memory_space=pltpu.VMEM)],
        out_specs=pl.BlockSpec(memory_space=pltpu.VMEM),
        scratch_shapes=[whole, whole, whole] + [sems] * 6,
        compiler_params=pltpu.CompilerParams(
            collective_id=0, has_side_effects=True, vmem_limit_bytes=VMEM_LIMIT
        ),
        name="reduce_over_dp",
    )(part.reshape((lines, 2, groups) + shape))
    return out.reshape((owned,) + part.shape[1:])


def local(
    images, pose_slot, references, rotation_response, shell_weight, class_lists, class_counts
):
    dp_count = lax.axis_size("dp")
    here = lax.axis_index("dp")
    column = lax.axis_index("cls")
    block = images.shape[0]
    classes = references.shape[0]
    width = 2 * NANG
    entries = block * LIST
    full_table = angular_tables(NANG)
    forward = jnp.asarray(full_table.astype(jnp.bfloat16))
    inverse = jnp.asarray(np.ascontiguousarray(full_table.T))

    def transform(rows):
        out = jnp.dot(rows.reshape(-1, width), forward, preferred_element_type=jnp.float32)
        return out.astype(jnp.bfloat16).reshape(rows.shape)

    tags = jnp.concatenate([pose_slot[None, :], class_lists.T], axis=0)
    all_tags = lax.all_gather(tags, "dp", axis=1, tiled=True)
    image_hat = transform(images)
    ref_hat = transform(references)

    positions = jnp.arange(dp_count * block, dtype=jnp.int32)
    at_slot = pose_slot[:, None] == positions[None, :]
    own_lists = jnp.stack(
        [jnp.sum(jnp.where(at_slot, all_tags[1 + a][None, :], 0), axis=1) for a in range(LIST)]
    )
    local_class = (own_lists - column * classes).reshape(entries)
    log_prior = jnp.log1p(class_counts.astype(jnp.float32))
    picked = local_class[:, None] == jnp.arange(classes, dtype=jnp.int32)[None, :]
    prior = jnp.sum(jnp.where(picked, log_prior[None, :], 0.0), axis=1)
    inside = (local_class >= 0) & (local_class < classes)
    rotations = rotation_response.shape[0]
    lane = jnp.arange(LANES, dtype=jnp.int32)
    bias = jnp.where(inside[:, None] & (lane < rotations)[None, :], prior[:, None], -1e30)
    spread = jnp.broadcast_to(shell_weight[:, None], (NSHELL, NANG))
    rot_re = rotation_response[:, :NANG]
    rot_im = rotation_response[:, NANG:]
    pad = ((0, LANES - rotations), (0, 0))
    response = jnp.pad(rotation_response, pad)
    coef_table = jnp.pad(
        jnp.concatenate([rot_re, -rot_im, rot_re * rot_re + rot_im * rot_im], axis=1), pad
    )

    def whole(shape):
        return pl.BlockSpec(shape, lambda i, c: (0,) * len(shape))

    image_spec = pl.BlockSpec((ROWS, NSHELL, width), lambda i, c: (i, 0, 0))
    params = pltpu.CompilerParams(
        dimension_semantics=("arbitrary",), vmem_limit_bytes=VMEM_LIMIT
    )
    scores, stats = pl.pallas_call(
        score_kernel,
        grid_spec=pltpu.PrefetchScalarGridSpec(
            num_scalar_prefetch=1,
            grid=(block // ROWS,),
            in_specs=[
                image_spec,
                whole((classes, NSHELL, width)),
                whole((NSHELL, NANG)),
                whole((LANES, width)),
                whole((entries, LANES)),
            ],
            out_specs=[whole((entries, LANES)), whole((8, block))],
            scratch_shapes=[pltpu.VMEM((entries, width), jnp.float32)],
        ),
        out_shape=[
            jax.ShapeDtypeStruct((entries, LANES), jnp.float32),
            jax.ShapeDtypeStruct((8, block), jnp.float32),
        ],
        compiler_params=params,
        name="scores",
    )(local_class, image_hat, ref_hat, spread, response, bias)
    all_stats = lax.all_gather(stats, "cls")
    columns = all_stats.shape[0]
    part, weight, evidence = pl.pallas_call(
        grad_kernel,
        grid_spec=pltpu.PrefetchScalarGridSpec(
            num_scalar_prefetch=1,
            grid=(block // ROWS,),
            in_specs=[
                image_spec,
                whole((classes, NSHELL, width)),
                whole((entries, LANES)),
                whole((columns, 8, block)),
                whole((LANES, 3 * NANG)),
            ],
            out_specs=[
                whole((classes, NSHELL, width)),
                whole((classes, LANES)),
                whole((1, block)),
            ],
            scratch_shapes=[
                pltpu.VMEM((classes, NSHELL, width), jnp.float32),
                pltpu.VMEM((entries, 3 * NANG), jnp.float32),
                pltpu.VMEM((entries, LANES), jnp.float32),
                pltpu.VMEM((classes, NANG), jnp.float32),
            ],
        ),
        out_shape=[
            jax.ShapeDtypeStruct((classes, NSHELL, width), jnp.bfloat16),
            jax.ShapeDtypeStruct((classes, LANES), jnp.float32),
            jax.ShapeDtypeStruct((1, block), jnp.float32),
        ],
        compiler_params=params,
        name="gradient",
    )(local_class, image_hat, ref_hat, scores, all_stats, coef_table)

    small = jnp.concatenate([evidence[0], weight[:, 0]])
    all_small = lax.all_gather(small, "dp")
    owned = classes // dp_count
    weights = jnp.sum(all_small[:, block:], axis=0)
    denom = 1.0 + lax.dynamic_slice_in_dim(weights, here * owned, owned, 0)
    mine = here * block + jnp.arange(block, dtype=jnp.int32)
    log_evidence = jnp.sum(
        jnp.where(
            all_tags[0][None, :] == mine[:, None], all_small[:, :block].reshape(1, -1), 0.0
        ),
        axis=1,
    )

    numer = reduce_scatter(part, dp_count)
    scaled = numer / denom[:, None, None]
    result = jnp.dot(scaled.reshape(-1, width), inverse, precision=HIGHEST)
    return (result.reshape((1,) + numer.shape), log_evidence)


def solution(mesh):
    return jax.shard_map(
        local,
        mesh=mesh,
        in_specs=(
            P("dp", None, None),
            P("dp"),
            P("cls", None, None),
            P(),
            P(),
            P("dp", None),
            P("cls"),
        ),
        out_specs=(P("cls", "dp", None, None), P("dp")),
        check_vma=False,
    )
```

time: 601 us -> 200 us (0.33)
  waiting for transfers between devices: 308 us -> 0 us
  Pallas kernels: 0 us -> 93.3 us
  local copies, waits for them, and re-layouts: 109 us -> 21.5 us
  matrix products: 81.2 us -> 20.8 us
  other arithmetic: 63 us -> 6.93 us
  blocking collectives: 10.1 us -> 54.5 us
  starting transfers between devices: 23.6 us -> 0 us
    all_to_all x4 -> x0, waiting for transfers between devices: 308 us -> none  [the longest x1 182 us: local(): lax.all_to_all(buffer.astype(jnp.bfloat16), 'dp', split_axis=0, concat_ax...]
    pallas_call x0 -> x3, Pallas kernels: none -> 93.3 us  [the longest x1 63 us: reduce_scatter(): pl.pallas_call(functools.partial(reduce_kernel, lines, groups), out_shape...]
    dot_general x12 -> x3, matrix products: 81.2 us -> 20.8 us  [the longest x2 18 us: transform(): jnp.dot(rows.reshape(-1, width), forward, preferred_element_type=jnp.floa...]
    gather x4 -> x0, local copies, waits for them, and re-layouts: 31.1 us -> none  [the longest x1 9.96 us: local(): arrived.reshape((blocksize,) + arrived.shape[2:])[source_row]]
    all_gather x2, blocking collectives: 10.1 us -> 34.8 us  [the longest x1 27.8 us: local(): all_tags = lax.all_gather(tags, 'dp', axis=1, tiled=True)]
    all_to_all x4 -> x0, starting transfers between devices: 23.6 us -> none  [the longest x1 7.25 us: local(): lax.all_to_all(slot_tags, 'dp', split_axis=0, concat_axis=0, tiled=True)]
    unnamed x0 -> x1, blocking collectives: none -> 19.7 us
    unnamed x58 -> x14, local copies, waits for them, and re-layouts: 19.5 us -> 0.61 us
  transfers between devices with their start and end apart: 4 -> 0, of which waited for: 2 -> 0; matrix products, arithmetic and copies ran while one was open for 14% -> 0% of each run, Pallas kernels for 0% -> 0%
where the time goes in v1:
time: 200 us; the launch traced here: 198 us
  Pallas kernels  93.3 us (47%)
  blocking collectives  54.5 us (27%)
  local copies, waits for them, and re-layouts  21.5 us (11%)
  matrix products  20.8 us (10%)
  other arithmetic  6.93 us (3%)
    pallas_call x1, Pallas kernels, reduce_scatter(): pl.pallas_call(functools.partial(reduce_kernel, lines, groups), out_shape...  63 us
    all_gather x1, blocking collectives, local(): all_tags = lax.all_gather(tags, 'dp', axis=1, tiled=True)  27.8 us
    unnamed x1, blocking collectives  19.7 us
    convert_element_type x2, local copies, waits for them, and re-layouts, transform(): return out.astype(jnp.bfloat16).reshape(rows.shape)  18.5 us
    dot_general x2, matrix products, transform(): jnp.dot(rows.reshape(-1, width), forward, preferred_element_type=jnp.floa...  18 us
    pallas_call x1, Pallas kernels, local(): pl.pallas_call(grad_kernel, grid_spec=pltpu.PrefetchScalarGridSpec(num_sc...  16.3 us
    pallas_call x1, Pallas kernels, local(): pl.pallas_call(score_kernel, grid_spec=pltpu.PrefetchScalarGridSpec(num_s...  14 us
    all_gather x1, blocking collectives, local(): all_stats = lax.all_gather(stats, 'cls')  7.03 us

profile of v1, /device:TPU:0, one launch (start us, length us, event | category | flops | bytes accessed | tf_op | source)
XLA Modules:
  0.0 198.4 jit_solution(6938388122255470995)
XLA Ops:
  0.6 0.7 pad_add_fusion
  1.3 27.8 %all_gather.15 = s32[3,1024]{1,0:T(4,128)S(1)} all-gather(s32[3,128]{1,0:T(4,128)S(1)} %pad_add_fusion), channel_id=1, replica_groups=mesh['dp'=8,'cls'=4] {'dp'}, dimensions={1}, use_global_device_ids=true | all-gather | bytes 13824 | tf_op jit(solution)/shard_map/all_gather | solution.py:335
  29.1 0.9 select_reduce_fusion.2
  30.0 0.0 copy-start.2
  30.0 0.7 convert_log-plus-one_fusion
  30.7 0.1 select_reduce_fusion.3
  30.8 0.8 and_select_fusion.bias_ref
  31.6 11.4 %fusion = bf16[8192,512]{0,1:T(8,128)(2,1)} fusion(bf16[512,512]{1,0:T(8,128)(2,1)} %constant.32.clone, bf16[8192,512]{1,0:T(8,128)(2,1)} %bitcast.49), kind=kOutput, calls=%fused_computation.1 | convolution fusion | flops 4299161600 | bytes 17301504 | tf_op jit(solution)/shard_map/dot_general | solution.py:331
  43.0 0.0 copy-done.2
  43.0 0.0 copy-start.4
  43.0 12.0 %copy.15 = bf16[8192,512]{1,0:T(8,128)(2,1)} copy(bf16[8192,512]{0,1:T(8,128)(2,1)} %fusion) | data formatting | bytes 16777216 | tf_op jit(solution)/shard_map/convert_element_type | solution.py:332
  55.0 0.0 copy-done.4
  55.0 0.0 copy-start.1
  55.0 0.0 copy-start.3
  55.0 6.6 %fusion.1 = bf16[4096,512]{0,1:T(8,128)(2,1)} fusion(bf16[512,512]{1,0:T(8,128)(2,1)S(1)} %copy-done.4, bf16[4096,512]{1,0:T(8,128)(2,1)} %bitcast.50), kind=kOutput, calls=%fused_computation.3 | convolution fusion | flops 2149580800 | bytes 8912896 | tf_op jit(solution)/shard_map/dot_general | solution.py:331
  61.6 6.5 %copy.16 = bf16[4096,512]{1,0:T(8,128)(2,1)} copy(bf16[4096,512]{0,1:T(8,128)(2,1)} %fusion.1) | data formatting | bytes 8388608 | tf_op jit(solution)/shard_map/convert_element_type | solution.py:332
  68.1 0.0 copy-done.1
  68.1 0.7 pad.8.rr_ref
  68.8 0.0 copy-done.3
  68.8 0.7 broadcast_in_dim.84.sw_ref
  69.5 14.0 %scores.1 = (f32[256,128]{1,0:T(8,128)}, f32[8,128]{1,0:T(8,128)}) custom-call(s32[256]{0:T(256)} %copy-done.2, bf16[128,64,512]{2,1,0:T(8,128)(2,1)} %bitcast.35, bf16[64,64,512]{2,1,0:T(8,128)(2,1)} %bitcast.37, f32[64,256]{1,0:T(8,128)} %broadcast_in_dim.84.sw_ref, f32[128,512]{1,0:T(8,128)} %pad.8.rr_ref, f32[256,128]{1,0:T(8,128)} %and_select_fusion.bias_ref), custom_call_target="tpu_custom_call" | custom-call | tf_op jit(solution)/shard_map/scores/pallas_call | solution.py:368
  83.5 0.0 copy-start.5
  83.5 7.0 %all-gather = f32[32,128]{1,0:T(8,128)} all-gather(f32[8,128]{1,0:T(8,128)} %get-tuple-element.8), channel_id=2, replica_groups=mesh['dp'=8,'cls'=4] {'cls'}, dimensions={0}, use_global_device_ids=true | all-gather | bytes 20480 | tf_op jit(solution)/shard_map/all_gather | solution.py:390
  90.5 0.8 select_maximum_fusion.ct_ref
  91.3 0.0 copy-start
  91.3 16.3 %gradient.1 = (bf16[64,64,512]{2,1,0:T(8,128)(2,1)}, f32[64,128]{1,0:T(8,128)}, f32[1,128]{1,0:T(1,128)}) custom-call(s32[256]{0:T(256)} %copy-done.2, bf16[128,64,512]{2,1,0:T(8,128)(2,1)} %bitcast.36, bf16[64,64,512]{2,1,0:T(8,128)(2,1)} %bitcast.38, f32[256,128]{1,0:T(8,128)} %get-tuple-element.7.scores_ref, f32[4,8,128]{2,1,0:T(8,128)} %bitcast.40, ...), custom_call_target="tpu_custom_call" | custom-call | tf_op jit(solution)/shard_map/gradient/pallas_call | solution.py:392
  107.6 0.9 slice_reduce_fusion
  108.5 0.0 copy-done.5
  108.5 0.6 dynamic-slice
  109.7 0.8 maximum_dynamic-update-slice_fusion
  110.5 19.7 %all-reduce.2 = f32[1536]{0:T(1024)S(1)} all-reduce(f32[1536]{0:T(1024)S(1)} %maximum_dynamic-update-slice_fusion), channel_id=3, replica_groups=mesh['dp'=8,'cls'=4] {'dp'}, use_global_device_ids=true, to_apply=%add.2 | all-reduce | flops 1536 | bytes 12288
  130.2 0.1 reshape.76
  130.3 0.1 dynamic-slice_add_fusion
  130.4 63.0 %reduce_over_dp.1 = f32[4,2,64,512]{3,2,1,0:T(8,128)} custom-call(bf16[4,2,4,2,64,512]{5,4,3,2,1,0:T(8,128)(2,1)} %bitcast.39), custom_call_target="tpu_custom_call" | custom-call | tf_op jit(solution)/shard_map/reduce_over_dp/pallas_call | solution.py:302
  193.4 1.4 bitcast_divide_fusion
  194.8 0.0 copy-done
  194.9 2.8 %convolution_bitcast_fusion = f32[1,8,64,512]{3,2,1,0:T(8,128)} fusion(f32[8,64,512]{2,1,0:T(8,128)S(1)} %bitcast_divide_fusion, f32[512,512,1]{1,0,2:T(8,128)S(1)} %copy-done), kind=kOutput, calls=%fused_computation.4 | convolution fusion | flops 1610612736 | bytes 3145728 | tf_op jit(solution)/shard_map/dot_general | solution.py:440
  197.7 0.7 select_reduce_fusion
  (8 shorter events, 0.1 us)
Async XLA Ops:
  30.0 12.9 %copy-start.2 = (s32[256]{0:T(256)}, s32[256]{0:T(256)S(1)}, u32[]{:S(2)}) copy-start(s32[256]{0:T(256)S(1)} %get-tuple-element.15.cls_ref) | copy-start | bytes 3076
  43.0 12.0 %copy-start.4 = (bf16[512,512]{1,0:T(8,128)(2,1)S(1)}, bf16[512,512]{1,0:T(8,128)(2,1)}, u32[]{:S(2)}) copy-start(bf16[512,512]{1,0:T(8,128)(2,1)} %constant.32.clone) | copy-start | bytes 1572868
  55.0 13.1 %copy-start.1 = (f32[36,512]{1,0:T(8,128)S(1)}, f32[36,512]{1,0:T(8,128)}, u32[]{:S(2)}) copy-start(f32[36,512]{1,0:T(8,128)} %param.12) | copy-start | bytes 221188
  55.0 13.8 %copy-start.3 = (f32[64]{0:T(128)S(1)}, f32[64]{0:T(128)}, u32[]{:S(2)}) copy-start(f32[64]{0:T(128)} %param.13) | copy-start | bytes 772
  83.5 25.0 %copy-start.5 = (u32[32]{0:T(128)S(1)}, u32[32]{0:T(128)}, u32[]{:S(2)}) copy-start(u32[32]{0:T(128)} %constant.40) | copy-start | bytes 388
  91.3 103.5 %copy-start = (f32[512,512,1]{1,0,2:T(8,128)S(1)}, f32[512,512,1]{1,0,2:T(8,128)}, u32[]{:S(2)}) copy-start(f32[512,512,1]{1,0,2:T(8,128)} %constant.44) | copy-start | bytes 3145732

commit v2 on v1

v2 whole, which is shorter than its diff:
```python
import functools
import math

import jax
import jax.numpy as jnp
import numpy as np
from jax import lax
from jax.experimental import pallas as pl
from jax.experimental.pallas import tpu as pltpu
from jax.sharding import PartitionSpec as P

NSHELL = 64
NANG = 256
LIST = 2
LANES = 128
ROWS = 16
MESH = pl.DeviceIdType.MESH
HIGHEST = lax.Precision.HIGHEST
VMEM_LIMIT = 56 * 1024 * 1024


def angular_tables(points):
    positions = np.arange(points)
    angles = (positions[:, None] * positions[None, :] % points).astype(np.float64) * (
        2.0 * math.pi / points
    )
    cosine = np.cos(angles) / math.sqrt(points)
    sine_part = np.sin(angles) / math.sqrt(points)
    upper_half = np.concatenate([cosine, -sine_part], axis=1)
    lower_half = np.concatenate([sine_part, cosine], axis=1)
    return np.concatenate([upper_half, lower_half], axis=0).astype(np.float32)


def everyone(axis):
    me, count = lax.axis_index(axis), lax.axis_size(axis)

    def peer(step):
        return lax.rem(me + step, count)

    return me, count, peer


def greet(axis):
    _, count, peer = everyone(axis)
    barrier = pltpu.get_barrier_semaphore()

    def one(step, carry):
        pl.semaphore_signal(barrier, inc=1, device_id={axis: peer(step)}, device_id_type=MESH)
        return carry

    lax.fori_loop(1, count, one, 0)


def greeted(axis):
    pl.semaphore_wait(pltpu.get_barrier_semaphore(), lax.axis_size(axis) - 1)


def share(axis, src, dst, send, recv):
    me, count, peer = everyone(axis)

    def outgoing(step):
        return pltpu.make_async_remote_copy(
            src_ref=src(peer(step)), dst_ref=dst.at[me],
            send_sem=send.at[peer(step)], recv_sem=recv.at[me],
            device_id={axis: peer(step)}, device_id_type=MESH,
        )

    def incoming(step):
        return pltpu.make_async_remote_copy(
            src_ref=src(peer(step)), dst_ref=dst.at[peer(step)],
            send_sem=send.at[peer(step)], recv_sem=recv.at[peer(step)],
            device_id={axis: peer(step)}, device_id_type=MESH,
        )

    def loop(act):
        def one(step, carry):
            act(step)
            return carry

        lax.fori_loop(1, count, one, 0)

    return (
        lambda: loop(lambda step: outgoing(step).start()),
        lambda: loop(lambda step: incoming(step).wait_recv()),
        lambda: loop(lambda step: outgoing(step).wait_send()),
    )


def transform_kernel(
    image_steps, classes, image_ref, refs_ref, table_ref, tags_ref,
    image_out, refs_out, ids_out, slots_out, all_tags, send, recv,
):
    step = pl.program_id(0)
    start, arrive, sent = share("dp", lambda _: tags_ref, all_tags, send, recv)
    me = lax.axis_index("dp")
    count = lax.axis_size("dp")
    block = tags_ref.shape[1]

    @pl.when(step == 0)
    def _():
        greet("dp")

    @pl.when(step == image_steps // 2)
    def _():
        greeted("dp")
        start()

    def multiply(source, target):
        def one(i, carry):
            some = pl.ds(i * 4, 4)
            out = jnp.dot(
                source[some].reshape(4 * NSHELL, 2 * NANG),
                table_ref[...],
                preferred_element_type=jnp.float32,
            )
            target[some] = out.astype(jnp.bfloat16).reshape(4, NSHELL, 2 * NANG)
            return carry

        lax.fori_loop(0, ROWS // 4, one, 0)

    @pl.when(step < image_steps)
    def _():
        multiply(image_ref, image_out)

    @pl.when(step >= image_steps)
    def _():
        multiply(refs_ref, refs_out)

    @pl.when(step == pl.num_programs(0) - 1)
    def _():
        arrive()
        all_tags[me] = tags_ref[...]
        own = tags_ref[0:1, :].astype(jnp.float32)
        slot = jnp.transpose(jnp.broadcast_to(own, (LANES, block))).astype(jnp.int32)
        lane = lax.broadcasted_iota(jnp.int32, (block, block), 1)

        def look(d, found):
            rows = all_tags[d]
            hit = slot == lane + d * block
            slots_out[pl.ds(d, 1), :] = rows[0:1]
            return tuple(
                total + jnp.where(hit, rows[1 + a : 2 + a], 0) for a, total in enumerate(found)
            )

        found = lax.fori_loop(
            0, count, look, (jnp.zeros((block, block), jnp.int32),) * LIST
        )
        column = lax.axis_index("cls")
        ids_out[...] = jnp.zeros_like(ids_out)
        for a in range(LIST):
            total = jnp.sum(found[a].astype(jnp.float32), axis=1, keepdims=True)
            row = jnp.transpose(jnp.broadcast_to(total, (block, LANES)))[0:1]
            ids_out[a : a + 1, :] = row.astype(jnp.int32) - column * classes
        sent()


def listed(ids_ref, chosen, step, classes):
    count = jnp.int32(0)
    for i in range(ROWS * LIST):
        k = ids_ref[i % LIST, step * ROWS + i // LIST]
        chosen[count] = i
        count = count + jnp.where((k >= 0) & (k < classes), 1, 0)
    return count


def score_kernel(
    ids_ref, xh_ref, rh_ref, sw_ref, rr_ref, prior_ref,
    scores_ref, stats_ref, cross, bias, response, chosen,
):
    step = pl.program_id(0)
    block = ids_ref.shape[1]
    classes = rh_ref.shape[0]
    rotations = rr_ref.shape[0]

    @pl.when(step == 0)
    def _():
        cross[...] = jnp.zeros_like(cross)
        bias[...] = jnp.full_like(bias, -1e30)
        response[...] = jnp.zeros_like(response)
        response[:rotations] = rr_ref[...]

    def entry(n, carry):
        i = chosen[n]
        p = lax.div(i, LIST)
        a = lax.rem(i, LIST)
        row = a * block + step * ROWS + p
        k = ids_ref[a, step * ROWS + p]
        bias[pl.ds(row, 1), :] = prior_ref[pl.ds(k, 1), :]
        re = jnp.zeros((8, NANG), jnp.float32)
        im = jnp.zeros((8, NANG), jnp.float32)
        for j in range(0, NSHELL, ROWS):
            x = xh_ref[p, j : j + ROWS].astype(jnp.float32)
            c = rh_ref[k, j : j + ROWS].astype(jnp.float32)
            sw = sw_ref[j : j + ROWS]
            x_re, x_im, c_re, c_im = x[:, :NANG], x[:, NANG:], c[:, :NANG], c[:, NANG:]
            one = (x_re * c_re + x_im * c_im) * sw
            two = (x_im * c_re - x_re * c_im) * sw
            re = re + one[:8] + one[8:]
            im = im + two[:8] + two[8:]
        cross[pl.ds(row, 1), :NANG] = jnp.sum(re, axis=0, keepdims=True)
        cross[pl.ds(row, 1), NANG:] = jnp.sum(im, axis=0, keepdims=True)
        return carry

    lax.fori_loop(0, listed(ids_ref, chosen, step, classes), entry, 0)

    @pl.when(step == pl.num_programs(0) - 1)
    def _():
        lane = lax.broadcasted_iota(jnp.int32, (block, LANES), 1)
        scores = lax.dot_general(
            cross[...],
            response[...],
            (((1,), (1,)), ((), ())),
            precision=HIGHEST,
            preferred_element_type=jnp.float32,
        ) + bias[...]
        first = jnp.where(lane < rotations, scores[:block], -1e30)
        second = jnp.where(lane < rotations, scores[block:], -1e30)
        scores_ref[:block] = first
        scores_ref[block:] = second
        top = jnp.max(jnp.maximum(first, second), axis=1, keepdims=True)
        total = jnp.sum(jnp.exp(first - top) + jnp.exp(second - top), axis=1, keepdims=True)
        stats = jnp.where(lane == 0, top, total)
        stats_ref[...] = jnp.transpose(stats)[:8]


def posterior_kernel(
    scores_ref, stats_ref, rr_ref, coef_ref, post_ref, evid_ref, all_stats, table, send, recv
):
    start, arrive, sent = share("cls", lambda _: stats_ref, all_stats, send, recv)
    block = scores_ref.shape[0] // LIST
    rotations = rr_ref.shape[0]
    greet("cls")
    table[...] = jnp.zeros_like(table)
    rot_re = rr_ref[:, :NANG]
    rot_im = rr_ref[:, NANG:]
    table[:rotations, :NANG] = rot_re
    table[:rotations, NANG : 2 * NANG] = -rot_im
    table[:rotations, 2 * NANG :] = rot_re * rot_re + rot_im * rot_im
    greeted("cls")
    start()
    all_stats[lax.axis_index("cls")] = stats_ref[...]
    arrive()
    stats = all_stats[...]
    tops = stats[:, 0:1, :]
    top = jnp.max(tops, axis=0)
    total = jnp.sum(stats[:, 1:2, :] * jnp.exp(tops - top[None]), axis=0)
    evid_ref[...] = top + jnp.log(total)
    top_col = jnp.transpose(jnp.broadcast_to(top, (LANES, block)))
    total_col = jnp.transpose(jnp.broadcast_to(total, (LANES, block)))
    for a in range(LIST):
        rows = slice(a * block, (a + 1) * block)
        posterior = jnp.exp(scores_ref[rows] - top_col) / total_col
        post_ref[rows] = jnp.broadcast_to(
            jnp.sum(posterior, axis=1, keepdims=True), (block, LANES)
        )
        coef_ref[rows] = jnp.dot(
            posterior, table[...], precision=HIGHEST, preferred_element_type=jnp.float32
        )
    sent()


def grad_kernel(
    ids_ref, xh_ref, rh_ref, coef, post_sum, part_ref, weight_ref, acc, volume, chosen
):
    step = pl.program_id(0)
    block = ids_ref.shape[1]
    classes = rh_ref.shape[0]

    @pl.when(step == 0)
    def _():
        volume[...] = jnp.zeros_like(volume)
        weight_ref[...] = jnp.zeros_like(weight_ref)

        def clear(k, carry):
            acc[k] = jnp.zeros(acc.shape[1:], jnp.float32)
            return carry

        lax.fori_loop(0, classes, clear, 0)

    def entry(n, carry):
        i = chosen[n]
        p = lax.div(i, LIST)
        a = lax.rem(i, LIST)
        row = a * block + step * ROWS + p
        k = ids_ref[a, step * ROWS + p]
        re = coef[pl.ds(row, 1), :NANG]
        im = coef[pl.ds(row, 1), NANG : 2 * NANG]
        for j in range(0, NSHELL, ROWS):
            x = xh_ref[p, j : j + ROWS].astype(jnp.float32)
            x_re, x_im = x[:, :NANG], x[:, NANG:]
            acc[k, j : j + ROWS, :NANG] += x_re * re - x_im * im
            acc[k, j : j + ROWS, NANG:] += x_re * im + x_im * re
        volume[pl.ds(k, 1), :] += coef[pl.ds(row, 1), 2 * NANG :]
        weight_ref[pl.ds(k, 1), :] += post_sum[pl.ds(row, 1), :]
        return carry

    lax.fori_loop(0, listed(ids_ref, chosen, step, classes), entry, 0)

    @pl.when(step == pl.num_programs(0) - 1)
    def _():
        def finish(k, carry):
            vol = volume[pl.ds(k, 1), :]
            for j in range(0, NSHELL, ROWS):
                for half in (slice(0, NANG), slice(NANG, 2 * NANG)):
                    part_ref[k, j : j + ROWS, half] = (
                        acc[k, j : j + ROWS, half]
                        - vol * rh_ref[k, j : j + ROWS, half].astype(jnp.float32)
                    ).astype(jnp.bfloat16)
            return carry

        lax.fori_loop(0, classes, finish, 0)


def reduce_kernel(
    lines, groups, p_ref, weight_ref, evid_ref, slots_ref, out_ref, log_ref,
    held, from_left, from_right, weights, evids,
    pair_send, pair_recv, right_send, right_recv, left_send, left_recv,
    weight_send, weight_recv, evid_send, evid_recv,
):
    me = lax.axis_index("dp")
    x = lax.rem(me, 2)
    z = lax.div(me, 2)
    partner = me + 1 - 2 * x
    has_left = z > 0
    has_right = z < lines - 1
    per_group = p_ref.shape[3]

    weight_start, weight_arrive, weight_sent = share(
        "dp", lambda d: weight_ref.at[d], weights, weight_send, weight_recv
    )
    evid_start, evid_arrive, evid_sent = share(
        "dp", lambda _: evid_ref, evids, evid_send, evid_recv
    )
    greet("dp")
    greeted("dp")

    def where_is(t):
        g, i = lax.div(t, lines), lax.rem(t, lines)
        odd, half = lax.rem(i, 2), lax.div(i, 2)
        return (1 - odd) * (lines - 1 - half) + odd * half, g

    def pair(b, g):
        return pltpu.make_async_remote_copy(
            src_ref=p_ref.at[b, 1 - x, g], dst_ref=held.at[b, g],
            send_sem=pair_send.at[b, g], recv_sem=pair_recv.at[b, g],
            device_id={"dp": partner}, device_id_type=MESH,
        )

    def right(b, g):
        return pltpu.make_async_remote_copy(
            src_ref=held.at[b, g], dst_ref=from_left.at[b, g],
            send_sem=right_send.at[b, g], recv_sem=right_recv.at[b, g],
            device_id={"dp": me + 2}, device_id_type=MESH,
        )

    def left(b, g):
        return pltpu.make_async_remote_copy(
            src_ref=held.at[b, g], dst_ref=from_right.at[b, g],
            send_sem=left_send.at[b, g], recv_sem=left_recv.at[b, g],
            device_id={"dp": me - 2}, device_id_type=MESH,
        )

    def add(b, g, other):
        def one(c, carry):
            held[b, g, c] = (
                held[b, g, c].astype(jnp.float32) + other(c).astype(jnp.float32)
            ).astype(jnp.bfloat16)
            return carry

        lax.fori_loop(0, per_group, one, 0)

    def begin(t, carry):
        pair(*where_is(t)).start()
        return carry

    def relay(t, carry):
        b, g = where_is(t)
        pair(b, g).wait_recv()
        add(b, g, lambda c: p_ref[b, x, g, c])

        @pl.when(z < b)
        def _():
            @pl.when(has_left)
            def _():
                right(b, g).wait_recv()
                add(b, g, lambda c: from_left[b, g, c])

            right(b, g).start()

        @pl.when(z > b)
        def _():
            @pl.when(has_right)
            def _():
                left(b, g).wait_recv()
                add(b, g, lambda c: from_right[b, g, c])

            left(b, g).start()

        return carry

    def finish(g, carry):
        @pl.when(has_left)
        def _():
            right(z, g).wait_recv()

        @pl.when(has_right)
        def _():
            left(z, g).wait_recv()

        def own(c, inner):
            out_ref[g, c] = held[z, g, c].astype(jnp.float32)

            @pl.when(has_left)
            def _():
                out_ref[g, c] += from_left[z, g, c].astype(jnp.float32)

            @pl.when(has_right)
            def _():
                out_ref[g, c] += from_right[z, g, c].astype(jnp.float32)

            return inner

        lax.fori_loop(0, per_group, own, 0)
        return carry

    def small():
        count = weights.shape[0]
        weight_arrive()
        evid_arrive()
        weights[me] = weight_ref[me]
        evids[me] = evid_ref[...]
        block = evid_ref.shape[1]
        mine = me * block + lax.broadcasted_iota(jnp.int32, (block, block), 0)

        def look(d, total):
            return total + jnp.where(slots_ref[pl.ds(d, 1), :] == mine, evids[d], 0.0)

        found = lax.fori_loop(0, count, look, jnp.zeros((block, block), jnp.float32))
        summed = jnp.sum(found, axis=1, keepdims=True)
        log_ref[...] = jnp.transpose(jnp.broadcast_to(summed, (block, LANES)))[0:1]
        denom = 1.0 + jnp.sum(weights[...], axis=0)
        for n in range(weights.shape[1]):
            g, c = n // per_group, n % per_group
            row = denom[n : n + 1, :]
            out_ref[g, c] = out_ref[g, c] / jnp.concatenate([row] * (2 * NANG // LANES), axis=1)
        weight_sent()
        evid_sent()

    def drain(t, carry):
        b, g = where_is(t)
        pair(b, g).wait_send()

        @pl.when(z < b)
        def _():
            right(b, g).wait_send()

        @pl.when(z > b)
        def _():
            left(b, g).wait_send()

        return carry

    lax.fori_loop(0, lines * groups, begin, 0)
    weight_start()
    evid_start()
    lax.fori_loop(0, lines * groups, relay, 0)
    lax.fori_loop(0, groups, finish, 0)
    small()
    lax.fori_loop(0, lines * groups, drain, 0)


def vmem():
    return pl.BlockSpec(memory_space=pltpu.VMEM)


def remote(collective_id):
    return pltpu.CompilerParams(
        collective_id=collective_id, has_side_effects=True, vmem_limit_bytes=VMEM_LIMIT
    )


def reduce_scatter(part, weight, evidence, slots, dp_count):
    classes = part.shape[0]
    block = evidence.shape[1]
    lines = dp_count // 2
    owned = classes // dp_count
    groups = math.gcd(4, owned)
    shape = (owned // groups,) + part.shape[1:]
    whole = pltpu.VMEM((lines, groups) + shape, jnp.bfloat16)
    sems = pltpu.SemaphoreType.DMA((lines, groups))
    row_sems = pltpu.SemaphoreType.DMA((dp_count,))
    out, log_evidence = pl.pallas_call(
        functools.partial(reduce_kernel, lines, groups),
        out_shape=[
            jax.ShapeDtypeStruct((groups,) + shape, jnp.float32),
            jax.ShapeDtypeStruct((1, block), jnp.float32),
        ],
        in_specs=[vmem()] * 4,
        out_specs=[vmem()] * 2,
        scratch_shapes=[
            whole, whole, whole,
            pltpu.VMEM((dp_count, owned, LANES), jnp.float32),
            pltpu.VMEM((dp_count, 1, block), jnp.float32),
        ]
        + [sems] * 6
        + [row_sems] * 4,
        compiler_params=remote(2),
        name="reduce_over_dp",
    )(
        part.reshape((lines, 2, groups) + shape),
        weight.reshape(dp_count, owned, LANES),
        evidence,
        slots,
    )
    return out.reshape((owned,) + part.shape[1:]), log_evidence[0]


def local(
    images, pose_slot, references, rotation_response, shell_weight, class_lists, class_counts
):
    dp_count = lax.axis_size("dp")
    columns = lax.axis_size("cls")
    block = images.shape[0]
    classes = references.shape[0]
    width = 2 * NANG
    entries = block * LIST
    rotations = rotation_response.shape[0]
    full_table = angular_tables(NANG)
    forward = jnp.asarray(full_table.astype(jnp.bfloat16))
    inverse = jnp.asarray(np.ascontiguousarray(full_table.T))
    tags = jnp.concatenate(
        [pose_slot[None, :], class_lists.T, jnp.zeros((7 - LIST, block), jnp.int32)], axis=0
    )
    prior = jnp.broadcast_to(
        jnp.log1p(class_counts.astype(jnp.float32))[:, None], (classes, LANES)
    )
    spread = jnp.broadcast_to(shell_weight[:, None], (NSHELL, NANG))

    image_steps = block // ROWS
    ref_steps = classes // ROWS
    cube = (ROWS, NSHELL, width)

    def fixed(shape):
        return pl.BlockSpec(shape, lambda i: (0,) * len(shape))

    def image_block():
        return pl.BlockSpec(cube, lambda i: (jnp.minimum(i, image_steps - 1), 0, 0))

    def ref_block():
        return pl.BlockSpec(cube, lambda i: (jnp.maximum(i - image_steps, 0), 0, 0))

    image_hat, ref_hat, ids, slots = pl.pallas_call(
        functools.partial(transform_kernel, image_steps, classes),
        grid=(image_steps + ref_steps,),
        in_specs=[image_block(), ref_block(), fixed((width, width)), fixed((8, block))],
        out_specs=[image_block(), ref_block(), fixed((8, block)), fixed((dp_count, block))],
        out_shape=[
            jax.ShapeDtypeStruct(images.shape, jnp.bfloat16),
            jax.ShapeDtypeStruct(references.shape, jnp.bfloat16),
            jax.ShapeDtypeStruct((8, block), jnp.int32),
            jax.ShapeDtypeStruct((dp_count, block), jnp.int32),
        ],
        scratch_shapes=[
            pltpu.VMEM((dp_count, 8, block), jnp.int32),
            pltpu.SemaphoreType.DMA((dp_count,)),
            pltpu.SemaphoreType.DMA((dp_count,)),
        ],
        compiler_params=remote(0),
        name="transform",
    )(images, references, forward, tags)

    def whole(shape):
        return pl.BlockSpec(shape, lambda i, c: (0,) * len(shape))

    image_spec = pl.BlockSpec(cube, lambda i, c: (i, 0, 0))
    params = pltpu.CompilerParams(
        dimension_semantics=("arbitrary",), vmem_limit_bytes=VMEM_LIMIT
    )
    chosen = pltpu.SMEM((ROWS * LIST + 1,), jnp.int32)
    scores, stats = pl.pallas_call(
        score_kernel,
        grid_spec=pltpu.PrefetchScalarGridSpec(
            num_scalar_prefetch=1,
            grid=(image_steps,),
            in_specs=[
                image_spec,
                whole((classes, NSHELL, width)),
                whole((NSHELL, NANG)),
                whole((rotations, width)),
                whole((classes, LANES)),
            ],
            out_specs=[whole((entries, LANES)), whole((8, block))],
            scratch_shapes=[
                pltpu.VMEM((entries, width), jnp.float32),
                pltpu.VMEM((entries, LANES), jnp.float32),
                pltpu.VMEM((LANES, width), jnp.float32),
                chosen,
            ],
        ),
        out_shape=[
            jax.ShapeDtypeStruct((entries, LANES), jnp.float32),
            jax.ShapeDtypeStruct((8, block), jnp.float32),
        ],
        compiler_params=params,
        name="scores",
    )(ids, image_hat, ref_hat, spread, rotation_response, prior)

    coef, post_sum, evidence = pl.pallas_call(
        posterior_kernel,
        in_specs=[vmem()] * 3,
        out_specs=[vmem()] * 3,
        out_shape=[
            jax.ShapeDtypeStruct((entries, 3 * NANG), jnp.float32),
            jax.ShapeDtypeStruct((entries, LANES), jnp.float32),
            jax.ShapeDtypeStruct((1, block), jnp.float32),
        ],
        scratch_shapes=[
            pltpu.VMEM((columns, 8, block), jnp.float32),
            pltpu.VMEM((LANES, 3 * NANG), jnp.float32),
            pltpu.SemaphoreType.DMA((columns,)),
            pltpu.SemaphoreType.DMA((columns,)),
        ],
        compiler_params=remote(1),
        name="posterior",
    )(scores, stats, rotation_response)

    part, weight = pl.pallas_call(
        grad_kernel,
        grid_spec=pltpu.PrefetchScalarGridSpec(
            num_scalar_prefetch=1,
            grid=(image_steps,),
            in_specs=[
                image_spec,
                whole((classes, NSHELL, width)),
                whole((entries, 3 * NANG)),
                whole((entries, LANES)),
            ],
            out_specs=[whole((classes, NSHELL, width)), whole((classes, LANES))],
            scratch_shapes=[
                pltpu.VMEM((classes, NSHELL, width), jnp.float32),
                pltpu.VMEM((classes, NANG), jnp.float32),
                chosen,
            ],
        ),
        out_shape=[
            jax.ShapeDtypeStruct((classes, NSHELL, width), jnp.bfloat16),
            jax.ShapeDtypeStruct((classes, LANES), jnp.float32),
        ],
        compiler_params=params,
        name="gradient",
    )(ids, image_hat, ref_hat, coef, post_sum)

    scaled, log_evidence = reduce_scatter(part, weight, evidence, slots, dp_count)
    result = jnp.dot(scaled.reshape(-1, width), inverse, precision=HIGHEST)
    return (result.reshape((1,) + scaled.shape), log_evidence)


def solution(mesh):
    return jax.shard_map(
        local,
        mesh=mesh,
        in_specs=(
            P("dp", None, None),
            P("dp"),
            P("cls", None, None),
            P(),
            P(),
            P("dp", None),
            P("cls"),
        ),
        out_specs=(P("cls", "dp", None, None), P("dp")),
        check_vma=False,
    )
```

time: 200 us -> 130 us (0.65)
  blocking collectives: 54.5 us -> 0 us
  Pallas kernels: 93.3 us -> 120 us
  local copies, waits for them, and re-layouts: 21.5 us -> 3.22 us
  matrix products: 20.8 us -> 4.04 us
  other arithmetic: 6.93 us -> 2.01 us
    all_gather x2 -> x0, blocking collectives: 34.8 us -> none  [the longest x1 27.8 us: local(): all_tags = lax.all_gather(tags, 'dp', axis=1, tiled=True)]
    pallas_call x0 -> x2, Pallas kernels: none -> 27.5 us  [the longest x1 20.6 us: local(): pl.pallas_call(functools.partial(transform_kernel, image_steps, classes),...]
    unnamed x1 -> x0, blocking collectives: 19.7 us -> none
    convert_element_type x2 -> x0, local copies, waits for them, and re-layouts: 18.5 us -> none  [transform(): return out.astype(jnp.bfloat16).reshape(rows.shape)]
    dot_general x2 -> x0, matrix products: 18 us -> none  [transform(): jnp.dot(rows.reshape(-1, width), forward, preferred_element_type=jnp.floa...]
    pallas_call x1, Pallas kernels: 63 us -> 67.1 us  [reduce_scatter(): pl.pallas_call(functools.partial(reduce_kernel, lines, groups), out_shape...]
    pallas_call x1, Pallas kernels: 16.3 us -> 13.4 us  [local(): pl.pallas_call(grad_kernel, grid_spec=pltpu.PrefetchScalarGridSpec(num_sc...]
where the time goes in v2:
time: 130 us
  Pallas kernels  120 us (92%)
  matrix products  4.04 us (3%)
  local copies, waits for them, and re-layouts  3.22 us (2%)
  other arithmetic  2.01 us (2%)
    pallas_call x1, Pallas kernels, reduce_scatter(): pl.pallas_call(functools.partial(reduce_kernel, lines, groups), out_shape...  67.1 us
    pallas_call x1, Pallas kernels, local(): pl.pallas_call(functools.partial(transform_kernel, image_steps, classes),...  20.6 us
    pallas_call x1, Pallas kernels, local(): pl.pallas_call(grad_kernel, grid_spec=pltpu.PrefetchScalarGridSpec(num_sc...  13.4 us
    pallas_call x1, Pallas kernels, local(): pl.pallas_call(score_kernel, grid_spec=pltpu.PrefetchScalarGridSpec(num_s...  12.1 us
    pallas_call x1, Pallas kernels, local(): pl.pallas_call(posterior_kernel, in_specs=[vmem()] * 3, out_specs=[vmem()...  6.92 us
    dot_general x1, matrix products, local(): result = jnp.dot(scaled.reshape(-1, width), inverse, precision=HIGHEST)  4.04 us

profile of v2, /device:TPU:0, one launch (start us, length us, event | category | flops | bytes accessed | tf_op | source)
XLA Modules:
  0.0 130.0 jit_solution(6632333675271072161)
XLA Ops:
  0.6 0.7 convert_log-plus-one_fusion
  1.3 0.1 pad.2.clone
  1.4 1.3 %add_add_fusion.tags_ref = s32[8,128]{1,0:T(8,128)} fusion(s32[2,128]{1,0:T(2,128)} %bitcast.14, s32[1,128]{1,0:T(1,128)} %bitcast.15, s32[8]{0:T(128)S(1)} %pad.2.clone), kind=kLoop, calls=%fused_computation.1 | loop fusion | flops 2048 | bytes 5664 | tf_op jit(solution)/shard_map/concatenate | solution.py:531
  2.7 0.7 broadcast_in_dim.21.prior_ref
  3.4 1.3 %broadcast_in_dim.20.sw_ref = f32[64,256]{1,0:T(8,128)} broadcast(f32[64]{0:T(128)} %param.13), dimensions={0} | broadcast | bytes 65792 | tf_op jit(solution)/shard_map/broadcast_in_dim | solution.py:537
  4.7 20.6 %transform.1 = (bf16[128,64,512]{2,1,0:T(8,128)(2,1)}, bf16[64,64,512]{2,1,0:T(8,128)(2,1)}, s32[8,128]{1,0:T(8,128)}, s32[8,128]{1,0:T(8,128)}) custom-call(bf16[128,64,512]{2,1,0:T(8,128)(2,1)} %image_ref.1, bf16[64,64,512]{2,1,0:T(8,128)(2,1)} %refs_ref.1, bf16[512,512]{1,0:T(8,128)(2,1)} %constant.6.clone.table_ref, s32[8,128]{1,0:T(8,128)} %add_add_fusion.tags_ref), custom_call_target="tpu_custom_call" | custom-call | tf_op jit(solution)/shard_map/transform/pallas_call | solution.py:552
  25.4 12.1 %scores.1 = (f32[256,128]{1,0:T(8,128)}, f32[8,128]{1,0:T(8,128)}) custom-call(s32[8,128]{1,0:T(8,128)} %get-tuple-element.15.ids_ref, bf16[128,64,512]{2,1,0:T(8,128)(2,1)} %get-tuple-element.16.xh_ref, bf16[64,64,512]{2,1,0:T(8,128)(2,1)} %get-tuple-element.17.rh_ref, f32[64,256]{1,0:T(8,128)} %broadcast_in_dim.20.sw_ref, f32[36,512]{1,0:T(8,128)} %rr_ref.3, ...), custom_call_target="tpu_custom_call" | custom-call | tf_op jit(solution)/shard_map/scores/pallas_call | solution.py:580
  37.4 6.9 %posterior.1 = (f32[256,768]{1,0:T(8,128)}, f32[256,128]{1,0:T(8,128)}, f32[1,128]{1,0:T(1,128)}) custom-call(f32[256,128]{1,0:T(8,128)} %get-tuple-element.18.scores_ref, f32[8,128]{1,0:T(8,128)} %get-tuple-element.19.stats_ref, f32[36,512]{1,0:T(8,128)} %rr_ref.3), custom_call_target="tpu_custom_call" | custom-call | tf_op jit(solution)/shard_map/posterior/pallas_call | solution.py:608
  44.4 13.4 %gradient.1 = (bf16[64,64,512]{2,1,0:T(8,128)(2,1)}, f32[64,128]{1,0:T(8,128)}) custom-call(s32[8,128]{1,0:T(8,128)} %get-tuple-element.15.ids_ref, bf16[128,64,512]{2,1,0:T(8,128)(2,1)} %get-tuple-element.16.xh_ref, bf16[64,64,512]{2,1,0:T(8,128)(2,1)} %get-tuple-element.17.rh_ref, f32[256,768]{1,0:T(8,128)} %get-tuple-element.20.coef, ...), custom_call_target="tpu_custom_call" | custom-call | tf_op jit(solution)/shard_map/gradient/pallas_call | solution.py:627
  57.8 0.0 copy-start
  57.8 67.1 %reduce_over_dp.1 = (f32[4,2,64,512]{3,2,1,0:T(8,128)}, f32[1,128]{1,0:T(1,128)}) custom-call(bf16[4,2,4,2,64,512]{5,4,3,2,1,0:T(8,128)(2,1)} %bitcast.11, f32[8,8,128]{2,1,0:T(8,128)} %bitcast.13, f32[1,128]{1,0:T(1,128)} %get-tuple-element.24.evid_ref, s32[8,128]{1,0:T(8,128)} %get-tuple-element.25.slots_ref), custom_call_target="tpu_custom_call" | custom-call | tf_op jit(solution)/shard_map/reduce_over_dp/pallas_call | solution.py:492
  124.8 0.0 copy-done
  124.8 4.0 %convolution_bitcast_fusion = f32[1,8,64,512]{3,2,1,0:T(8,128)} fusion(f32[8,64,512]{2,1,0:T(8,128)} %bitcast.12, f32[512,512,1]{1,0,2:T(8,128)S(1)} %copy-done), kind=kOutput, calls=%fused_computation | convolution fusion | flops 1610612736 | bytes 3145728 | tf_op jit(solution)/shard_map/dot_general | solution.py:654
  128.9 1.1 copy.12
  (1 shorter events, 0.0 us)
Async XLA Ops:
  57.8 67.1 %copy-start = (f32[512,512,1]{1,0,2:T(8,128)S(1)}, f32[512,512,1]{1,0,2:T(8,128)}, u32[]{:S(2)}) copy-start(f32[512,512,1]{1,0,2:T(8,128)} %constant.8) | copy-start | bytes 3145732

commit v3 on v2

--- a/solution.py
+++ b/solution.py
@@ -17,6 +17,7 @@
 MESH = pl.DeviceIdType.MESH
 HIGHEST = lax.Precision.HIGHEST
 VMEM_LIMIT = 56 * 1024 * 1024
+WINDOW = 4
 
 
 def angular_tables(points):
@@ -87,8 +88,8 @@
 
 
 def transform_kernel(
-    image_steps, classes, image_ref, refs_ref, table_ref, tags_ref,
-    image_out, refs_out, ids_out, slots_out, all_tags, send, recv,
+    image_steps, classes, image_ref, refs_ref, table_ref, slot_ref, lists_ref,
+    image_out, refs_out, ids_out, slots_out, tags_ref, all_tags, send, recv,
 ):
     step = pl.program_id(0)
     start, arrive, sent = share("dp", lambda _: tags_ref, all_tags, send, recv)
@@ -99,6 +100,12 @@
     @pl.when(step == 0)
     def _():
         greet("dp")
+        tags_ref[...] = jnp.zeros_like(tags_ref)
+        tags_ref[0:1, :] = slot_ref[...]
+        for a in range(LIST):
+            own = lists_ref[:, a : a + 1].astype(jnp.float32)
+            row = jnp.transpose(jnp.broadcast_to(own, (block, LANES)))[0:1]
+            tags_ref[1 + a : 2 + a, :] = row.astype(jnp.int32)
 
     @pl.when(step == image_steps // 2)
     def _():
@@ -106,17 +113,12 @@
         start()
 
     def multiply(source, target):
-        def one(i, carry):
-            some = pl.ds(i * 4, 4)
-            out = jnp.dot(
-                source[some].reshape(4 * NSHELL, 2 * NANG),
-                table_ref[...],
-                preferred_element_type=jnp.float32,
-            )
-            target[some] = out.astype(jnp.bfloat16).reshape(4, NSHELL, 2 * NANG)
-            return carry
-
-        lax.fori_loop(0, ROWS // 4, one, 0)
+        out = jnp.dot(
+            source[...].reshape(ROWS * NSHELL, 2 * NANG),
+            table_ref[...],
+            preferred_element_type=jnp.float32,
+        )
+        target[...] = out.astype(jnp.bfloat16).reshape(ROWS, NSHELL, 2 * NANG)
 
     @pl.when(step < image_steps)
     def _():
@@ -164,8 +166,8 @@
 
 
 def score_kernel(
-    ids_ref, xh_ref, rh_ref, sw_ref, rr_ref, prior_ref,
-    scores_ref, stats_ref, cross, bias, response, chosen,
+    ids_ref, xh_ref, rh_ref, shells_ref, rr_ref, counts_ref,
+    scores_ref, stats_ref, cross, bias, response, prior_ref, sw_ref, chosen,
 ):
     step = pl.program_id(0)
     block = ids_ref.shape[1]
@@ -178,6 +180,9 @@
         bias[...] = jnp.full_like(bias, -1e30)
         response[...] = jnp.zeros_like(response)
         response[:rotations] = rr_ref[...]
+        row = jnp.log1p(counts_ref[...].astype(jnp.float32))
+        prior_ref[...] = jnp.transpose(jnp.broadcast_to(row, (LANES, classes)))
+        sw_ref[...] = jnp.transpose(jnp.broadcast_to(shells_ref[...], (NANG, NSHELL)))
 
     def entry(n, carry):
         i = chosen[n]
@@ -260,61 +265,86 @@
 
 
 def grad_kernel(
-    ids_ref, xh_ref, rh_ref, coef, post_sum, part_ref, weight_ref, acc, volume, chosen
+    ids_ref, images_ref, rh_ref, coef, post_sum, part_ref, weight_ref, xh_ref, head, nxt, sem
 ):
     step = pl.program_id(0)
     block = ids_ref.shape[1]
-    classes = rh_ref.shape[0]
+    per_step = rh_ref.shape[0]
+    classes = per_step * pl.num_programs(0)
+    fetch = pltpu.make_async_copy(images_ref, xh_ref, sem)
 
     @pl.when(step == 0)
     def _():
-        volume[...] = jnp.zeros_like(volume)
-        weight_ref[...] = jnp.zeros_like(weight_ref)
+        fetch.start()
 
         def clear(k, carry):
-            acc[k] = jnp.zeros(acc.shape[1:], jnp.float32)
+            head[k] = -1
             return carry
 
-        lax.fori_loop(0, classes, clear, 0)
-
-    def entry(n, carry):
-        i = chosen[n]
-        p = lax.div(i, LIST)
-        a = lax.rem(i, LIST)
-        row = a * block + step * ROWS + p
-        k = ids_ref[a, step * ROWS + p]
-        re = coef[pl.ds(row, 1), :NANG]
-        im = coef[pl.ds(row, 1), NANG : 2 * NANG]
-        for j in range(0, NSHELL, ROWS):
-            x = xh_ref[p, j : j + ROWS].astype(jnp.float32)
-            x_re, x_im = x[:, :NANG], x[:, NANG:]
-            acc[k, j : j + ROWS, :NANG] += x_re * re - x_im * im
-            acc[k, j : j + ROWS, NANG:] += x_re * im + x_im * re
-        volume[pl.ds(k, 1), :] += coef[pl.ds(row, 1), 2 * NANG :]
-        weight_ref[pl.ds(k, 1), :] += post_sum[pl.ds(row, 1), :]
+        lax.fori_loop(0, classes + 1, clear, 0)
+
+        def link(n, carry):
+            for i in range(ROWS):
+                for a in range(LIST):
+                    p = n * ROWS + i
+                    k = ids_ref[a, p]
+                    slot = jnp.where((k >= 0) & (k < classes), k, classes)
+                    nxt[a * block + p] = head[slot]
+                    head[slot] = a * block + p
+            return carry
+
+        lax.fori_loop(0, block // ROWS, link, 0)
+        fetch.wait()
+
+    def one_class(c, carry):
+        first = head[step * per_step + c]
+
+        def more(state):
+            return state[0] >= 0
+
+        def tally(state):
+            row, vol, weight = state
+            return (
+                nxt[row],
+                vol + coef[pl.ds(row, 1), 2 * NANG :],
+                weight + post_sum[pl.ds(row, 1), :],
+            )
+
+        _, vol, weight = lax.while_loop(
+            more, tally, (first, jnp.zeros((1, NANG), jnp.float32), jnp.zeros((1, LANES), jnp.float32))
+        )
+        weight_ref[pl.ds(c, 1), :] = weight
+        for j in range(0, NSHELL, 2 * ROWS):
+            rows = slice(j, j + 2 * ROWS)
+
+            def add(state):
+                row, g_re, g_im = state
+                p = lax.rem(row, block)
+                re = coef[pl.ds(row, 1), :NANG]
+                im = coef[pl.ds(row, 1), NANG : 2 * NANG]
+                x_re = xh_ref[p, rows, :NANG].astype(jnp.float32)
+                x_im = xh_ref[p, rows, NANG:].astype(jnp.float32)
+                return (
+                    nxt[row], g_re + (x_re * re - x_im * im), g_im + (x_re * im + x_im * re)
+                )
+
+            start = (
+                first,
+                -vol * rh_ref[c, rows, :NANG].astype(jnp.float32),
+                -vol * rh_ref[c, rows, NANG:].astype(jnp.float32),
+            )
+            _, g_re, g_im = lax.while_loop(more, add, start)
+            part_ref[c, rows, :NANG] = g_re.astype(jnp.bfloat16)
+            part_ref[c, rows, NANG:] = g_im.astype(jnp.bfloat16)
         return carry
 
-    lax.fori_loop(0, listed(ids_ref, chosen, step, classes), entry, 0)
-
-    @pl.when(step == pl.num_programs(0) - 1)
-    def _():
-        def finish(k, carry):
-            vol = volume[pl.ds(k, 1), :]
-            for j in range(0, NSHELL, ROWS):
-                for half in (slice(0, NANG), slice(NANG, 2 * NANG)):
-                    part_ref[k, j : j + ROWS, half] = (
-                        acc[k, j : j + ROWS, half]
-                        - vol * rh_ref[k, j : j + ROWS, half].astype(jnp.float32)
-                    ).astype(jnp.bfloat16)
-            return carry
-
-        lax.fori_loop(0, classes, finish, 0)
+    lax.fori_loop(0, per_step, one_class, 0)
 
 
 def reduce_kernel(
-    lines, groups, p_ref, weight_ref, evid_ref, slots_ref, out_ref, log_ref,
-    held, from_left, from_right, weights, evids,
-    pair_send, pair_recv, right_send, right_recv, left_send, left_recv,
+    lines, groups, p_ref, weight_ref, evid_ref, slots_ref, table_ref, out_ref, log_ref,
+    held, own, from_left, from_right, weights, evids, scale,
+    own_sem, pair_send, pair_recv, right_send, right_recv, left_send, left_recv,
     weight_send, weight_recv, evid_send, evid_recv,
 ):
     me = lax.axis_index("dp")
@@ -323,7 +353,7 @@
     partner = me + 1 - 2 * x
     has_left = z > 0
     has_right = z < lines - 1
-    per_group = p_ref.shape[3]
+    chunks = lines * groups
 
     weight_start, weight_arrive, weight_sent = share(
         "dp", lambda d: weight_ref.at[d], weights, weight_send, weight_recv
@@ -331,13 +361,14 @@
     evid_start, evid_arrive, evid_sent = share(
         "dp", lambda _: evid_ref, evids, evid_send, evid_recv
     )
-    greet("dp")
-    greeted("dp")
 
     def where_is(t):
         g, i = lax.div(t, lines), lax.rem(t, lines)
         odd, half = lax.rem(i, 2), lax.div(i, 2)
         return (1 - odd) * (lines - 1 - half) + odd * half, g
+
+    def keep(b, g):
+        return pltpu.make_async_copy(p_ref.at[b, x, g], own.at[b, g], own_sem.at[b, g])
 
     def pair(b, g):
         return pltpu.make_async_remote_copy(
@@ -361,29 +392,34 @@
         )
 
     def add(b, g, other):
-        def one(c, carry):
-            held[b, g, c] = (
-                held[b, g, c].astype(jnp.float32) + other(c).astype(jnp.float32)
-            ).astype(jnp.bfloat16)
+        held[b, g] = (
+            held[b, g].astype(jnp.float32) + other[b, g].astype(jnp.float32)
+        ).astype(jnp.bfloat16)
+
+    def each(act):
+        def one(t, carry):
+            act(*where_is(t))
             return carry
 
-        lax.fori_loop(0, per_group, one, 0)
-
-    def begin(t, carry):
-        pair(*where_is(t)).start()
-        return carry
-
-    def relay(t, carry):
+        lax.fori_loop(0, chunks, one, 0)
+
+    def relay(t):
         b, g = where_is(t)
+        keep(b, g).wait()
         pair(b, g).wait_recv()
-        add(b, g, lambda c: p_ref[b, x, g, c])
+
+        @pl.when(t + WINDOW < chunks)
+        def _():
+            pair(*where_is(t + WINDOW)).start()
+
+        add(b, g, own)
 
         @pl.when(z < b)
         def _():
             @pl.when(has_left)
             def _():
                 right(b, g).wait_recv()
-                add(b, g, lambda c: from_left[b, g, c])
+                add(b, g, from_left)
 
             right(b, g).start()
 
@@ -392,36 +428,9 @@
             @pl.when(has_right)
             def _():
                 left(b, g).wait_recv()
-                add(b, g, lambda c: from_right[b, g, c])
+                add(b, g, from_right)
 
             left(b, g).start()
-
-        return carry
-
-    def finish(g, carry):
-        @pl.when(has_left)
-        def _():
-            right(z, g).wait_recv()
-
-        @pl.when(has_right)
-        def _():
-            left(z, g).wait_recv()
-
-        def own(c, inner):
-            out_ref[g, c] = held[z, g, c].astype(jnp.float32)
-
-            @pl.when(has_left)
-            def _():
-                out_ref[g, c] += from_left[z, g, c].astype(jnp.float32)
-
-            @pl.when(has_right)
-            def _():
-                out_ref[g, c] += from_right[z, g, c].astype(jnp.float32)
-
-            return inner
-
-        lax.fori_loop(0, per_group, own, 0)
-        return carry
 
     def small():
         count = weights.shape[0]
@@ -438,35 +447,74 @@
         found = lax.fori_loop(0, count, look, jnp.zeros((block, block), jnp.float32))
         summed = jnp.sum(found, axis=1, keepdims=True)
         log_ref[...] = jnp.transpose(jnp.broadcast_to(summed, (block, LANES)))[0:1]
-        denom = 1.0 + jnp.sum(weights[...], axis=0)
-        for n in range(weights.shape[1]):
-            g, c = n // per_group, n % per_group
-            row = denom[n : n + 1, :]
-            out_ref[g, c] = out_ref[g, c] / jnp.concatenate([row] * (2 * NANG // LANES), axis=1)
-        weight_sent()
-        evid_sent()
-
-    def drain(t, carry):
-        b, g = where_is(t)
-        pair(b, g).wait_send()
-
-        @pl.when(z < b)
-        def _():
-            right(b, g).wait_send()
-
-        @pl.when(z > b)
-        def _():
-            left(b, g).wait_send()
-
+        inverse = 1.0 / (1.0 + jnp.sum(weights[...], axis=0))
+        for n in range(2 * NANG // LANES):
+            scale[:, n * LANES : (n + 1) * LANES] = inverse
+
+    def finish(g):
+        out_ref[g] = held[z, g].astype(jnp.float32)
+
+        @pl.when(has_left)
+        def _():
+            right(z, g).wait_recv()
+            out_ref[g] += from_left[z, g].astype(jnp.float32)
+
+        @pl.when(has_right)
+        def _():
+            left(z, g).wait_recv()
+            out_ref[g] += from_right[z, g].astype(jnp.float32)
+
+        scaled = out_ref[g] * scale[pl.ds(g, 1), :]
+        out_ref[g] = jnp.dot(
+            scaled.astype(jnp.bfloat16), table_ref[...], preferred_element_type=jnp.float32
+        )
+
+    each(lambda b, g: keep(b, g).start())
+    greet("dp")
+    greeted("dp")
+
+    def begin(t, carry):
+        pair(*where_is(t)).start()
         return carry
 
-    lax.fori_loop(0, lines * groups, begin, 0)
+    lax.fori_loop(0, min(WINDOW, chunks), begin, 0)
     weight_start()
     evid_start()
-    lax.fori_loop(0, lines * groups, relay, 0)
-    lax.fori_loop(0, groups, finish, 0)
-    small()
-    lax.fori_loop(0, lines * groups, drain, 0)
+
+    def round_of(g, carry):
+        def one(i, inner):
+            relay(g * lines + i)
+            return inner
+
+        lax.fori_loop(0, lines, one, 0)
+
+        @pl.when(g == 0)
+        def _():
+            small()
+
+        @pl.when(g > 0)
+        def _():
+            finish(g - 1)
+
+        return carry
+
+    lax.fori_loop(0, groups, round_of, 0)
+    finish(groups - 1)
+
+    def drain(b, g):
+        pair(b, g).wait_send()
+
+        @pl.when(z < b)
+        def _():
+            right(b, g).wait_send()
+
+        @pl.when(z > b)
+        def _():
+            left(b, g).wait_send()
+
+    each(drain)
+    weight_sent()
+    evid_sent()
 
 
 def vmem():
@@ -479,40 +527,41 @@
     )
 
 
-def reduce_scatter(part, weight, evidence, slots, dp_count):
+def reduce_scatter(part, weight, evidence, slots, table, dp_count):
     classes = part.shape[0]
     block = evidence.shape[1]
     lines = dp_count // 2
     owned = classes // dp_count
-    groups = math.gcd(4, owned)
-    shape = (owned // groups,) + part.shape[1:]
-    whole = pltpu.VMEM((lines, groups) + shape, jnp.bfloat16)
-    sems = pltpu.SemaphoreType.DMA((lines, groups))
+    shape = part.shape[1:]
+    whole = pltpu.VMEM((lines, owned) + shape, jnp.bfloat16)
+    sems = pltpu.SemaphoreType.DMA((lines, owned))
     row_sems = pltpu.SemaphoreType.DMA((dp_count,))
     out, log_evidence = pl.pallas_call(
-        functools.partial(reduce_kernel, lines, groups),
+        functools.partial(reduce_kernel, lines, owned),
         out_shape=[
-            jax.ShapeDtypeStruct((groups,) + shape, jnp.float32),
+            jax.ShapeDtypeStruct((owned,) + shape, jnp.float32),
             jax.ShapeDtypeStruct((1, block), jnp.float32),
         ],
-        in_specs=[vmem()] * 4,
+        in_specs=[pl.BlockSpec(memory_space=pl.ANY)] + [vmem()] * 4,
         out_specs=[vmem()] * 2,
         scratch_shapes=[
-            whole, whole, whole,
+            whole, whole, whole, whole,
             pltpu.VMEM((dp_count, owned, LANES), jnp.float32),
             pltpu.VMEM((dp_count, 1, block), jnp.float32),
+            pltpu.VMEM((owned, 2 * NANG), jnp.float32),
         ]
-        + [sems] * 6
+        + [sems] * 7
         + [row_sems] * 4,
         compiler_params=remote(2),
         name="reduce_over_dp",
     )(
-        part.reshape((lines, 2, groups) + shape),
+        part.reshape((lines, 2, owned) + shape),
         weight.reshape(dp_count, owned, LANES),
         evidence,
         slots,
+        table,
     )
-    return out.reshape((owned,) + part.shape[1:]), log_evidence[0]
+    return out, log_evidence[0]
 
 
 def local(
@@ -527,14 +576,7 @@
     rotations = rotation_response.shape[0]
     full_table = angular_tables(NANG)
     forward = jnp.asarray(full_table.astype(jnp.bfloat16))
-    inverse = jnp.asarray(np.ascontiguousarray(full_table.T))
-    tags = jnp.concatenate(
-        [pose_slot[None, :], class_lists.T, jnp.zeros((7 - LIST, block), jnp.int32)], axis=0
-    )
-    prior = jnp.broadcast_to(
-        jnp.log1p(class_counts.astype(jnp.float32))[:, None], (classes, LANES)
-    )
-    spread = jnp.broadcast_to(shell_weight[:, None], (NSHELL, NANG))
+    inverse = jnp.asarray(np.ascontiguousarray(full_table.T).astype(jnp.bfloat16))
 
     image_steps = block // ROWS
     ref_steps = classes // ROWS
@@ -552,7 +594,13 @@
     image_hat, ref_hat, ids, slots = pl.pallas_call(
         functools.partial(transform_kernel, image_steps, classes),
         grid=(image_steps + ref_steps,),
-        in_specs=[image_block(), ref_block(), fixed((width, width)), fixed((8, block))],
+        in_specs=[
+            image_block(),
+            ref_block(),
+            fixed((width, width)),
+            fixed((1, block)),
+            fixed((block, LIST)),
+        ],
         out_specs=[image_block(), ref_block(), fixed((8, block)), fixed((dp_count, block))],
         out_shape=[
             jax.ShapeDtypeStruct(images.shape, jnp.bfloat16),
@@ -561,13 +609,14 @@
             jax.ShapeDtypeStruct((dp_count, block), jnp.int32),
         ],
         scratch_shapes=[
+            pltpu.VMEM((8, block), jnp.int32),
             pltpu.VMEM((dp_count, 8, block), jnp.int32),
             pltpu.SemaphoreType.DMA((dp_count,)),
             pltpu.SemaphoreType.DMA((dp_count,)),
         ],
         compiler_params=remote(0),
         name="transform",
-    )(images, references, forward, tags)
+    )(images, references, forward, pose_slot[None, :], class_lists)
 
     def whole(shape):
         return pl.BlockSpec(shape, lambda i, c: (0,) * len(shape))
@@ -576,7 +625,6 @@
     params = pltpu.CompilerParams(
         dimension_semantics=("arbitrary",), vmem_limit_bytes=VMEM_LIMIT
     )
-    chosen = pltpu.SMEM((ROWS * LIST + 1,), jnp.int32)
     scores, stats = pl.pallas_call(
         score_kernel,
         grid_spec=pltpu.PrefetchScalarGridSpec(
@@ -585,16 +633,18 @@
             in_specs=[
                 image_spec,
                 whole((classes, NSHELL, width)),
-                whole((NSHELL, NANG)),
+                whole((1, NSHELL)),
                 whole((rotations, width)),
-                whole((classes, LANES)),
+                whole((1, classes)),
             ],
             out_specs=[whole((entries, LANES)), whole((8, block))],
             scratch_shapes=[
                 pltpu.VMEM((entries, width), jnp.float32),
                 pltpu.VMEM((entries, LANES), jnp.float32),
                 pltpu.VMEM((LANES, width), jnp.float32),
-                chosen,
+                pltpu.VMEM((classes, LANES), jnp.float32),
+                pltpu.VMEM((NSHELL, NANG), jnp.float32),
+                pltpu.SMEM((ROWS * LIST + 1,), jnp.int32),
             ],
         ),
         out_shape=[
@@ -603,7 +653,7 @@
         ],
         compiler_params=params,
         name="scores",
-    )(ids, image_hat, ref_hat, spread, rotation_response, prior)
+    )(ids, image_hat, ref_hat, shell_weight[None, :], rotation_response, class_counts[None, :])
 
     coef, post_sum, evidence = pl.pallas_call(
         posterior_kernel,
@@ -624,22 +674,27 @@
         name="posterior",
     )(scores, stats, rotation_response)
 
+    some = (8, NSHELL, width)
     part, weight = pl.pallas_call(
         grad_kernel,
         grid_spec=pltpu.PrefetchScalarGridSpec(
             num_scalar_prefetch=1,
-            grid=(image_steps,),
+            grid=(classes // 8,),
             in_specs=[
-                image_spec,
-                whole((classes, NSHELL, width)),
+                pl.BlockSpec(memory_space=pl.ANY),
+                pl.BlockSpec(some, lambda i, c: (i, 0, 0)),
                 whole((entries, 3 * NANG)),
                 whole((entries, LANES)),
             ],
-            out_specs=[whole((classes, NSHELL, width)), whole((classes, LANES))],
+            out_specs=[
+                pl.BlockSpec(some, lambda i, c: (i, 0, 0)),
+                pl.BlockSpec((8, LANES), lambda i, c: (i, 0)),
+            ],
             scratch_shapes=[
-                pltpu.VMEM((classes, NSHELL, width), jnp.float32),
-                pltpu.VMEM((classes, NANG), jnp.float32),
-                chosen,
+                pltpu.VMEM((block, NSHELL, width), jnp.bfloat16),
+                pltpu.SMEM((classes + 1,), jnp.int32),
+                pltpu.SMEM((entries,), jnp.int32),
+                pltpu.SemaphoreType.DMA(()),
             ],
         ),
         out_shape=[
@@ -650,9 +705,8 @@
         name="gradient",
     )(ids, image_hat, ref_hat, coef, post_sum)
 
-    scaled, log_evidence = reduce_scatter(part, weight, evidence, slots, dp_count)
-    result = jnp.dot(scaled.reshape(-1, width), inverse, precision=HIGHEST)
-    return (result.reshape((1,) + scaled.shape), log_evidence)
+    gradient, log_evidence = reduce_scatter(part, weight, evidence, slots, inverse, dp_count)
+    return (gradient[None], log_evidence)
 
 
 def solution(mesh):

time: 130 us -> 139 us (1.069); the launches traced: 130 us -> 138 us
  Pallas kernels: 120 us -> 132 us
  matrix products: 4.04 us -> 0 us
  other arithmetic: 2.01 us -> 0 us
  local copies, waits for them, and re-layouts: 3.22 us -> 4.86 us
    pallas_call x1, Pallas kernels: 67.1 us -> 82.8 us  [reduce_scatter(): pl.pallas_call(functools.partial(reduce_kernel, lines, owned), out_shape=...]
    dot_general x1 -> x0, matrix products: 4.04 us -> none  [local(): result = jnp.dot(scaled.reshape(-1, width), inverse, precision=HIGHEST)]
    unnamed x3, local copies, waits for them, and re-layouts: 1.12 us -> 4.86 us
    pallas_call x1, Pallas kernels: 20.6 us -> 18.1 us  [local(): pl.pallas_call(functools.partial(transform_kernel, image_steps, classes),...]
    broadcast_in_dim x3 -> x0, local copies, waits for them, and re-layouts: 2.03 us -> none  [the longest x1 1.35 us: local(): spread = jnp.broadcast_to(shell_weight[:, None], (NSHELL, NANG))]
where the time goes in v3:
time: 139 us; the launch traced here: 138 us
  Pallas kernels  132 us (95%)
  local copies, waits for them, and re-layouts  4.86 us (3%)
    pallas_call x1, Pallas kernels, reduce_scatter(): pl.pallas_call(functools.partial(reduce_kernel, lines, owned), out_shape=...  82.8 us
    pallas_call x1, Pallas kernels, local(): pl.pallas_call(functools.partial(transform_kernel, image_steps, classes),...  18.1 us
    pallas_call x1, Pallas kernels, local(): pl.pallas_call(grad_kernel, grid_spec=pltpu.PrefetchScalarGridSpec(num_sc...  13.3 us
    pallas_call x1, Pallas kernels, local(): pl.pallas_call(score_kernel, grid_spec=pltpu.PrefetchScalarGridSpec(num_s...  11.5 us
    pallas_call x1, Pallas kernels, local(): pl.pallas_call(posterior_kernel, in_specs=[vmem()] * 3, out_specs=[vmem()...  6.43 us
    unnamed x3, local copies, waits for them, and re-layouts  4.86 us

profile of v3, /device:TPU:0, one launch (start us, length us, event | category | flops | bytes accessed | tf_op | source)
XLA Modules:
  0.0 137.6 jit_solution(1217218320816245861)
XLA Ops:
  0.6 1.4 %copy.11.lists_ref = s32[128,2]{1,0:T(8,128)} copy(s32[128,2]{0,1:T(2,128)} %param.14) | data formatting | bytes 2048 | tf_op args[5]
  2.0 18.1 %transform.1 = (bf16[128,64,512]{2,1,0:T(8,128)(2,1)}, bf16[64,64,512]{2,1,0:T(8,128)(2,1)}, s32[8,128]{1,0:T(8,128)}, s32[8,128]{1,0:T(8,128)}) custom-call(bf16[128,64,512]{2,1,0:T(8,128)(2,1)} %image_ref.1, bf16[64,64,512]{2,1,0:T(8,128)(2,1)} %refs_ref.1, bf16[512,512]{1,0:T(8,128)(2,1)} %constant.4.clone.table_ref, s32[1,128]{1,0:T(1,128)} %bitcast.10, ...), custom_call_target="tpu_custom_call" | custom-call | tf_op jit(solution)/shard_map/transform/pallas_call | solution.py:594
  20.2 11.5 %scores.1 = (f32[256,128]{1,0:T(8,128)}, f32[8,128]{1,0:T(8,128)}) custom-call(s32[8,128]{1,0:T(8,128)} %get-tuple-element.15.ids_ref, bf16[128,64,512]{2,1,0:T(8,128)(2,1)} %get-tuple-element.16.xh_ref.images_ref, bf16[64,64,512]{2,1,0:T(8,128)(2,1)} %get-tuple-element.17.rh_ref, f32[1,64]{1,0:T(1,128)} %bitcast.11, f32[36,512]{1,0:T(8,128)} %rr_ref.3, ...), custom_call_target="tpu_custom_call" | custom-call | tf_op jit(solution)/shard_map/scores/pallas_call | solution.py:628
  31.6 6.4 %posterior.1 = (f32[256,768]{1,0:T(8,128)}, f32[256,128]{1,0:T(8,128)}, f32[1,128]{1,0:T(1,128)}) custom-call(f32[256,128]{1,0:T(8,128)} %get-tuple-element.18.scores_ref, f32[8,128]{1,0:T(8,128)} %get-tuple-element.19.stats_ref, f32[36,512]{1,0:T(8,128)} %rr_ref.3), custom_call_target="tpu_custom_call" | custom-call | tf_op jit(solution)/shard_map/posterior/pallas_call | solution.py:658
  38.1 13.3 %gradient.1 = (bf16[64,64,512]{2,1,0:T(8,128)(2,1)}, f32[64,128]{1,0:T(8,128)}) custom-call(s32[8,128]{1,0:T(8,128)} %get-tuple-element.15.ids_ref, bf16[128,64,512]{2,1,0:T(8,128)(2,1)} %get-tuple-element.16.xh_ref.images_ref, bf16[64,64,512]{2,1,0:T(8,128)(2,1)} %get-tuple-element.17.rh_ref, f32[256,768]{1,0:T(8,128)} %get-tuple-element.20.coef, ...), custom_call_target="tpu_custom_call" | custom-call | tf_op jit(solution)/shard_map/gradient/pallas_call | solution.py:678
  51.3 82.8 %reduce_over_dp.1 = (f32[8,64,512]{2,1,0:T(8,128)}, f32[1,128]{1,0:T(1,128)}) custom-call(bf16[4,2,8,64,512]{4,3,2,1,0:T(8,128)(2,1)} %bitcast.7, f32[8,8,128]{2,1,0:T(8,128)} %bitcast.9, f32[1,128]{1,0:T(1,128)} %get-tuple-element.24.evid_ref, s32[8,128]{1,0:T(8,128)} %get-tuple-element.25.slots_ref, bf16[512,512]{1,0:T(8,128)(2,1)} %constant.5.clone.table_ref), custom_call_target="tpu_custom_call" | custom-call | tf_op jit(solution)/shard_map/reduce_over_dp/pallas_call | solution.py:539
  134.1 2.3 %copy.14 = f32[1,8,64,512]{3,2,1,0:T(8,128)} copy(f32[1,8,64,512]{3,2,1,0:T(8,128)} %bitcast.8) | data formatting | bytes 2097152
  136.4 1.2 copy.15

commit v4 on v3

--- a/solution.py
+++ b/solution.py
@@ -16,8 +16,8 @@
 ROWS = 16
 MESH = pl.DeviceIdType.MESH
 HIGHEST = lax.Precision.HIGHEST
-VMEM_LIMIT = 56 * 1024 * 1024
-WINDOW = 4
+FIRST = 4
+MIB = 1024 * 1024
 
 
 def angular_tables(points):
@@ -88,7 +88,7 @@
 
 
 def transform_kernel(
-    image_steps, classes, image_ref, refs_ref, table_ref, slot_ref, lists_ref,
+    image_steps, classes, image_ref, refs_ref, even_ref, odd_ref, slot_ref, lists_ref,
     image_out, refs_out, ids_out, slots_out, tags_ref, all_tags, send, recv,
 ):
     step = pl.program_id(0)
@@ -102,10 +102,7 @@
         greet("dp")
         tags_ref[...] = jnp.zeros_like(tags_ref)
         tags_ref[0:1, :] = slot_ref[...]
-        for a in range(LIST):
-            own = lists_ref[:, a : a + 1].astype(jnp.float32)
-            row = jnp.transpose(jnp.broadcast_to(own, (block, LANES)))[0:1]
-            tags_ref[1 + a : 2 + a, :] = row.astype(jnp.int32)
+        tags_ref[1 : 1 + LIST, :] = lists_ref[...]
 
     @pl.when(step == image_steps // 2)
     def _():
@@ -113,12 +110,16 @@
         start()
 
     def multiply(source, target):
-        out = jnp.dot(
-            source[...].reshape(ROWS * NSHELL, 2 * NANG),
-            table_ref[...],
-            preferred_element_type=jnp.float32,
-        )
-        target[...] = out.astype(jnp.bfloat16).reshape(ROWS, NSHELL, 2 * NANG)
+        rows = source[...].reshape(ROWS * NSHELL, 2 * NANG)
+        half = NANG // 2
+        re_low, re_high, im_low, im_high = (rows[:, i * half : (i + 1) * half] for i in range(4))
+        plus = jnp.concatenate([re_low + re_high, im_low + im_high], axis=1)
+        minus = jnp.concatenate([re_low - re_high, im_low - im_high], axis=1)
+        for n, (mixed, table) in enumerate(((plus, even_ref), (minus, odd_ref))):
+            out = jnp.dot(mixed, table[...], preferred_element_type=jnp.float32)
+            out = out.astype(jnp.bfloat16).reshape(ROWS, NSHELL, NANG)
+            target[:, :, n * half : (n + 1) * half] = out[:, :, :half]
+            target[:, :, NANG + n * half : NANG + (n + 1) * half] = out[:, :, half:]
 
     @pl.when(step < image_steps)
     def _():
@@ -167,7 +168,7 @@
 
 def score_kernel(
     ids_ref, xh_ref, rh_ref, shells_ref, rr_ref, counts_ref,
-    scores_ref, stats_ref, cross, bias, response, prior_ref, sw_ref, chosen,
+    scores_ref, stats_ref, head, nxt, cross, bias, response, prior_ref, sw_ref, chosen,
 ):
     step = pl.program_id(0)
     block = ids_ref.shape[1]
@@ -184,12 +185,20 @@
         prior_ref[...] = jnp.transpose(jnp.broadcast_to(row, (LANES, classes)))
         sw_ref[...] = jnp.transpose(jnp.broadcast_to(shells_ref[...], (NANG, NSHELL)))
 
+        def clear(k, carry):
+            head[k] = -1
+            return carry
+
+        lax.fori_loop(0, classes, clear, 0, unroll=True)
+
     def entry(n, carry):
         i = chosen[n]
         p = lax.div(i, LIST)
         a = lax.rem(i, LIST)
         row = a * block + step * ROWS + p
         k = ids_ref[a, step * ROWS + p]
+        nxt[row] = head[k]
+        head[k] = row
         bias[pl.ds(row, 1), :] = prior_ref[pl.ds(k, 1), :]
         re = jnp.zeros((8, NANG), jnp.float32)
         im = jnp.zeros((8, NANG), jnp.float32)
@@ -264,85 +273,60 @@
     sent()
 
 
-def grad_kernel(
-    ids_ref, images_ref, rh_ref, coef, post_sum, part_ref, weight_ref, xh_ref, head, nxt, sem
-):
+def grad_kernel(head, nxt, xh_ref, rh_ref, coef, post_sum, part_ref, weight_ref):
     step = pl.program_id(0)
-    block = ids_ref.shape[1]
+    block = xh_ref.shape[0]
     per_step = rh_ref.shape[0]
-    classes = per_step * pl.num_programs(0)
-    fetch = pltpu.make_async_copy(images_ref, xh_ref, sem)
-
-    @pl.when(step == 0)
-    def _():
-        fetch.start()
-
-        def clear(k, carry):
-            head[k] = -1
-            return carry
-
-        lax.fori_loop(0, classes + 1, clear, 0)
-
-        def link(n, carry):
-            for i in range(ROWS):
-                for a in range(LIST):
-                    p = n * ROWS + i
-                    k = ids_ref[a, p]
-                    slot = jnp.where((k >= 0) & (k < classes), k, classes)
-                    nxt[a * block + p] = head[slot]
-                    head[slot] = a * block + p
-            return carry
-
-        lax.fori_loop(0, block // ROWS, link, 0)
-        fetch.wait()
+    pieces = [slice(j, j + ROWS) for j in range(0, NSHELL, ROWS)]
 
     def one_class(c, carry):
-        first = head[step * per_step + c]
-
         def more(state):
             return state[0] >= 0
 
-        def tally(state):
-            row, vol, weight = state
+        def add(state):
+            row, vol, weight, g_re, g_im = state
+            p = lax.rem(row, block)
+            re = coef[pl.ds(row, 1), :NANG]
+            im = coef[pl.ds(row, 1), NANG : 2 * NANG]
+            new_re, new_im = [], []
+            for rows, one, two in zip(pieces, g_re, g_im):
+                x_re = xh_ref[p, rows, :NANG].astype(jnp.float32)
+                x_im = xh_ref[p, rows, NANG:].astype(jnp.float32)
+                new_re.append(one + (x_re * re - x_im * im))
+                new_im.append(two + (x_re * im + x_im * re))
             return (
                 nxt[row],
                 vol + coef[pl.ds(row, 1), 2 * NANG :],
                 weight + post_sum[pl.ds(row, 1), :],
+                tuple(new_re),
+                tuple(new_im),
             )
 
-        _, vol, weight = lax.while_loop(
-            more, tally, (first, jnp.zeros((1, NANG), jnp.float32), jnp.zeros((1, LANES), jnp.float32))
+        zeros = (jnp.zeros((ROWS, NANG), jnp.float32),) * len(pieces)
+        _, vol, weight, g_re, g_im = lax.while_loop(
+            more,
+            add,
+            (
+                head[step * per_step + c],
+                jnp.zeros((1, NANG), jnp.float32),
+                jnp.zeros((1, LANES), jnp.float32),
+                zeros,
+                zeros,
+            ),
         )
         weight_ref[pl.ds(c, 1), :] = weight
-        for j in range(0, NSHELL, 2 * ROWS):
-            rows = slice(j, j + 2 * ROWS)
-
-            def add(state):
-                row, g_re, g_im = state
-                p = lax.rem(row, block)
-                re = coef[pl.ds(row, 1), :NANG]
-                im = coef[pl.ds(row, 1), NANG : 2 * NANG]
-                x_re = xh_ref[p, rows, :NANG].astype(jnp.float32)
-                x_im = xh_ref[p, rows, NANG:].astype(jnp.float32)
-                return (
-                    nxt[row], g_re + (x_re * re - x_im * im), g_im + (x_re * im + x_im * re)
-                )
-
-            start = (
-                first,
-                -vol * rh_ref[c, rows, :NANG].astype(jnp.float32),
-                -vol * rh_ref[c, rows, NANG:].astype(jnp.float32),
-            )
-            _, g_re, g_im = lax.while_loop(more, add, start)
-            part_ref[c, rows, :NANG] = g_re.astype(jnp.bfloat16)
-            part_ref[c, rows, NANG:] = g_im.astype(jnp.bfloat16)
+        for rows, one, two in zip(pieces, g_re, g_im):
+            c_re = rh_ref[c, rows, :NANG].astype(jnp.float32)
+            c_im = rh_ref[c, rows, NANG:].astype(jnp.float32)
+            part_ref[c, rows, :NANG] = (one - vol * c_re).astype(jnp.bfloat16)
+            part_ref[c, rows, NANG:] = (two - vol * c_im).astype(jnp.bfloat16)
         return carry
 
     lax.fori_loop(0, per_step, one_class, 0)
 
 
 def reduce_kernel(
-    lines, groups, p_ref, weight_ref, evid_ref, slots_ref, table_ref, out_ref, log_ref,
+    lines, groups, p_ref, weight_ref, evid_ref, slots_ref, out_ref, log_ref,
     held, own, from_left, from_right, weights, evids, scale,
     own_sem, pair_send, pair_recv, right_send, right_recv, left_send, left_recv,
     weight_send, weight_recv, evid_send, evid_recv,
@@ -363,9 +347,9 @@
     )
 
     def where_is(t):
-        g, i = lax.div(t, lines), lax.rem(t, lines)
-        odd, half = lax.rem(i, 2), lax.div(i, 2)
-        return (1 - odd) * (lines - 1 - half) + odd * half, g
+        layer, i = lax.div(t, 2 * groups), lax.rem(t, 2 * groups)
+        low = lax.rem(i, 2)
+        return (1 - low) * (lines - 1 - layer) + low * layer, lax.div(i, 2)
 
     def keep(b, g):
         return pltpu.make_async_copy(p_ref.at[b, x, g], own.at[b, g], own_sem.at[b, g])
@@ -407,10 +391,6 @@
         b, g = where_is(t)
         keep(b, g).wait()
         pair(b, g).wait_recv()
-
-        @pl.when(t + WINDOW < chunks)
-        def _():
-            pair(*where_is(t + WINDOW)).start()
 
         add(b, g, own)
 
@@ -451,23 +431,23 @@
         for n in range(2 * NANG // LANES):
             scale[:, n * LANES : (n + 1) * LANES] = inverse
 
-    def finish(g):
-        out_ref[g] = held[z, g].astype(jnp.float32)
-
+    def finish(g, carry):
         @pl.when(has_left)
         def _():
             right(z, g).wait_recv()
-            out_ref[g] += from_left[z, g].astype(jnp.float32)
+            held[z, g] = (
+                held[z, g].astype(jnp.float32) + from_left[z, g].astype(jnp.float32)
+            ).astype(jnp.bfloat16)
 
         @pl.when(has_right)
         def _():
             left(z, g).wait_recv()
-            out_ref[g] += from_right[z, g].astype(jnp.float32)
-
-        scaled = out_ref[g] * scale[pl.ds(g, 1), :]
-        out_ref[g] = jnp.dot(
-            scaled.astype(jnp.bfloat16), table_ref[...], preferred_element_type=jnp.float32
-        )
+            held[z, g] = (
+                held[z, g].astype(jnp.float32) + from_right[z, g].astype(jnp.float32)
+            ).astype(jnp.bfloat16)
+
+        out_ref[g] = (held[z, g].astype(jnp.float32) * scale[pl.ds(g, 1), :]).astype(jnp.bfloat16)
+        return carry
 
     each(lambda b, g: keep(b, g).start())
     greet("dp")
@@ -477,29 +457,18 @@
         pair(*where_is(t)).start()
         return carry
 
-    lax.fori_loop(0, min(WINDOW, chunks), begin, 0)
+    lax.fori_loop(0, FIRST, begin, 0)
     weight_start()
     evid_start()
-
-    def round_of(g, carry):
-        def one(i, inner):
-            relay(g * lines + i)
-            return inner
-
-        lax.fori_loop(0, lines, one, 0)
-
-        @pl.when(g == 0)
-        def _():
-            small()
-
-        @pl.when(g > 0)
-        def _():
-            finish(g - 1)
-
+    lax.fori_loop(FIRST, chunks, begin, 0)
+
+    def passing(t, carry):
+        relay(t)
         return carry
 
-    lax.fori_loop(0, groups, round_of, 0)
-    finish(groups - 1)
+    lax.fori_loop(0, chunks, passing, 0)
+    small()
+    lax.fori_loop(0, groups, finish, 0)
 
     def drain(b, g):
         pair(b, g).wait_send()
@@ -521,13 +490,13 @@
     return pl.BlockSpec(memory_space=pltpu.VMEM)
 
 
-def remote(collective_id):
+def remote(collective_id, mebibytes):
     return pltpu.CompilerParams(
-        collective_id=collective_id, has_side_effects=True, vmem_limit_bytes=VMEM_LIMIT
+        collective_id=collective_id, has_side_effects=True, vmem_limit_bytes=mebibytes * MIB
     )
 
 
-def reduce_scatter(part, weight, evidence, slots, table, dp_count):
+def reduce_scatter(part, weight, evidence, slots, dp_count):
     classes = part.shape[0]
     block = evidence.shape[1]
     lines = dp_count // 2
@@ -539,10 +508,10 @@
     out, log_evidence = pl.pallas_call(
         functools.partial(reduce_kernel, lines, owned),
         out_shape=[
-            jax.ShapeDtypeStruct((owned,) + shape, jnp.float32),
+            jax.ShapeDtypeStruct((owned,) + shape, jnp.bfloat16),
             jax.ShapeDtypeStruct((1, block), jnp.float32),
         ],
-        in_specs=[pl.BlockSpec(memory_space=pl.ANY)] + [vmem()] * 4,
+        in_specs=[pl.BlockSpec(memory_space=pl.ANY)] + [vmem()] * 3,
         out_specs=[vmem()] * 2,
         scratch_shapes=[
             whole, whole, whole, whole,
@@ -552,14 +521,13 @@
         ]
         + [sems] * 7
         + [row_sems] * 4,
-        compiler_params=remote(2),
+        compiler_params=remote(2, 20),
         name="reduce_over_dp",
     )(
         part.reshape((lines, 2, owned) + shape),
         weight.reshape(dp_count, owned, LANES),
         evidence,
         slots,
-        table,
     )
     return out, log_evidence[0]
 
@@ -575,8 +543,16 @@
     entries = block * LIST
     rotations = rotation_response.shape[0]
     full_table = angular_tables(NANG)
-    forward = jnp.asarray(full_table.astype(jnp.bfloat16))
-    inverse = jnp.asarray(np.ascontiguousarray(full_table.T).astype(jnp.bfloat16))
+    parity = np.concatenate([np.arange(0, NANG, 2), np.arange(1, NANG, 2)])
+    order = np.concatenate([parity, NANG + parity])
+    low = np.concatenate([np.arange(NANG // 2), NANG + np.arange(NANG // 2)])
+    evens = np.concatenate([np.arange(0, NANG, 2), NANG + np.arange(0, NANG, 2)])
+    even = jnp.asarray(full_table[np.ix_(low, evens)].astype(jnp.bfloat16))
+    odd = jnp.asarray(full_table[np.ix_(low, evens + 1)].astype(jnp.bfloat16))
+    inverse = jnp.asarray(np.ascontiguousarray(full_table.T[order]).astype(jnp.bfloat16))
+    rotation_response = jnp.transpose(
+        rotation_response.reshape(rotations, 2, NANG // 2, 2), (0, 1, 3, 2)
+    ).reshape(rotations, width)
 
     image_steps = block // ROWS
     ref_steps = classes // ROWS
@@ -597,9 +573,10 @@
         in_specs=[
             image_block(),
             ref_block(),
-            fixed((width, width)),
+            fixed((NANG, NANG)),
+            fixed((NANG, NANG)),
             fixed((1, block)),
-            fixed((block, LIST)),
+            fixed((LIST, block)),
         ],
         out_specs=[image_block(), ref_block(), fixed((8, block)), fixed((dp_count, block))],
         out_shape=[
@@ -614,18 +591,21 @@
             pltpu.SemaphoreType.DMA((dp_count,)),
             pltpu.SemaphoreType.DMA((dp_count,)),
         ],
-        compiler_params=remote(0),
+        compiler_params=remote(0, 24),
         name="transform",
-    )(images, references, forward, pose_slot[None, :], class_lists)
+    )(images, references, even, odd, pose_slot[None, :], class_lists.T)
 
     def whole(shape):
         return pl.BlockSpec(shape, lambda i, c: (0,) * len(shape))
 
     image_spec = pl.BlockSpec(cube, lambda i, c: (i, 0, 0))
-    params = pltpu.CompilerParams(
-        dimension_semantics=("arbitrary",), vmem_limit_bytes=VMEM_LIMIT
-    )
-    scores, stats = pl.pallas_call(
+
+    def plain(mebibytes):
+        return pltpu.CompilerParams(
+            dimension_semantics=("arbitrary",), vmem_limit_bytes=mebibytes * MIB
+        )
+
+    scores, stats, head, nxt = pl.pallas_call(
         score_kernel,
         grid_spec=pltpu.PrefetchScalarGridSpec(
             num_scalar_prefetch=1,
@@ -637,7 +617,12 @@
                 whole((rotations, width)),
                 whole((1, classes)),
             ],
-            out_specs=[whole((entries, LANES)), whole((8, block))],
+            out_specs=[
+                whole((entries, LANES)),
+                whole((8, block)),
+                pl.BlockSpec(memory_space=pltpu.SMEM),
+                pl.BlockSpec(memory_space=pltpu.SMEM),
+            ],
             scratch_shapes=[
                 pltpu.VMEM((entries, width), jnp.float32),
                 pltpu.VMEM((entries, LANES), jnp.float32),
@@ -650,8 +635,10 @@
         out_shape=[
             jax.ShapeDtypeStruct((entries, LANES), jnp.float32),
             jax.ShapeDtypeStruct((8, block), jnp.float32),
+            jax.ShapeDtypeStruct((classes,), jnp.int32),
+            jax.ShapeDtypeStruct((entries,), jnp.int32),
         ],
-        compiler_params=params,
+        compiler_params=plain(24),
         name="scores",
     )(ids, image_hat, ref_hat, shell_weight[None, :], rotation_response, class_counts[None, :])
 
@@ -670,43 +657,44 @@
             pltpu.SemaphoreType.DMA((columns,)),
             pltpu.SemaphoreType.DMA((columns,)),
         ],
-        compiler_params=remote(1),
+        compiler_params=remote(1, 8),
         name="posterior",
     )(scores, stats, rotation_response)
 
     some = (8, NSHELL, width)
+
+    def listed_whole(shape):
+        return pl.BlockSpec(shape, lambda i, h, n: (0,) * len(shape))
+
     part, weight = pl.pallas_call(
         grad_kernel,
         grid_spec=pltpu.PrefetchScalarGridSpec(
-            num_scalar_prefetch=1,
+            num_scalar_prefetch=2,
             grid=(classes // 8,),
             in_specs=[
-                pl.BlockSpec(memory_space=pl.ANY),
-                pl.BlockSpec(some, lambda i, c: (i, 0, 0)),
-                whole((entries, 3 * NANG)),
-                whole((entries, LANES)),
+                vmem(),
+                pl.BlockSpec(some, lambda i, h, n: (i, 0, 0)),
+                listed_whole((entries, 3 * NANG)),
+                listed_whole((entries, LANES)),
             ],
             out_specs=[
-                pl.BlockSpec(some, lambda i, c: (i, 0, 0)),
-                pl.BlockSpec((8, LANES), lambda i, c: (i, 0)),
-            ],
-            scratch_shapes=[
-                pltpu.VMEM((block, NSHELL, width), jnp.bfloat16),
-                pltpu.SMEM((classes + 1,), jnp.int32),
-                pltpu.SMEM((entries,), jnp.int32),
-                pltpu.SemaphoreType.DMA(()),
+                pl.BlockSpec(some, lambda i, h, n: (i, 0, 0)),
+                pl.BlockSpec((8, LANES), lambda i, h, n: (i, 0)),
             ],
         ),
         out_shape=[
             jax.ShapeDtypeStruct((classes, NSHELL, width), jnp.bfloat16),
             jax.ShapeDtypeStruct((classes, LANES), jnp.float32),
         ],
-        compiler_params=params,
+        compiler_params=plain(24),
         name="gradient",
-    )(ids, image_hat, ref_hat, coef, post_sum)
-
-    gradient, log_evidence = reduce_scatter(part, weight, evidence, slots, inverse, dp_count)
-    return (gradient[None], log_evidence)
+    )(head, nxt, image_hat, ref_hat, coef, post_sum)
+
+    scaled, log_evidence = reduce_scatter(part, weight, evidence, slots, dp_count)
+    result = jnp.dot(
+        scaled.reshape(-1, width), inverse, preferred_element_type=jnp.float32
+    )
+    return (result.reshape((1,) + scaled.shape), log_evidence)
 
 
 def solution(mesh):

time: 139 us -> 118 us (0.85)
  the two profiles are of different devices: /device:TPU:0 before, /device:TPU:20 now
where the time goes in v4:
time: 118 us; the launch traced here: 117 us
  Pallas kernels  105 us (89%)
  local copies, waits for them, and re-layouts  10.5 us (9%)
  matrix products  1.41 us (1%)
    pallas_call x1, Pallas kernels, reduce_scatter(): pl.pallas_call(functools.partial(reduce_kernel, lines, owned), out_shape=...  80 us
    unnamed x20, local copies, waits for them, and re-layouts  10.3 us
    pallas_call x1, Pallas kernels, local(): pl.pallas_call(score_kernel, grid_spec=pltpu.PrefetchScalarGridSpec(num_s...  7.82 us
    pallas_call x1, Pallas kernels, local(): pl.pallas_call(functools.partial(transform_kernel, image_steps, classes),...  7.19 us
    pallas_call x1, Pallas kernels, local(): pl.pallas_call(grad_kernel, grid_spec=pltpu.PrefetchScalarGridSpec(num_sc...  5.07 us
    pallas_call x1, Pallas kernels, local(): pl.pallas_call(posterior_kernel, in_specs=[vmem()] * 3, out_specs=[vmem()...  4.6 us

profile of v4, /device:TPU:20, one launch (start us, length us, event | category | flops | bytes accessed | tf_op | source)
XLA Modules:
  0.0 117.3 jit_solution(15404724276763239145)
XLA Ops:
  0.6 1.0 copy.13
  1.7 0.1 copy.14
  1.8 0.1 reshape.24.rr_ref
  1.9 0.0 copy-start
  1.9 3.4 %copy-done = bf16[128,64,512]{2,1,0:T(8,128)(2,1)S(1)} copy-done((bf16[128,64,512]{2,1,0:T(8,128)(2,1)S(1)}, bf16[128,64,512]{2,1,0:T(8,128)(2,1)}, u32[]{:S(2)}) %copy-start) | copy-done | bytes 8388632
  5.3 0.0 copy-start.1
  5.3 2.2 %copy-done.1 = bf16[64,64,512]{2,1,0:T(8,128)(2,1)S(1)} copy-done((bf16[64,64,512]{2,1,0:T(8,128)(2,1)S(1)}, bf16[64,64,512]{2,1,0:T(8,128)(2,1)}, u32[]{:S(2)}) %copy-start.1) | copy-done | bytes 4194328
  7.4 0.0 copy-start.2
  7.4 0.9 copy-done.2
  8.3 0.0 copy-start.3
  8.3 0.9 copy-done.3
  9.3 0.0 copy-start.4
  9.3 0.7 copy-done.4
  9.9 0.0 copy-start.7
  9.9 0.7 copy-done.7
  10.6 0.0 copy-start.5
  10.6 0.0 copy-start.6
  10.6 7.2 %transform.1 = (bf16[128,64,512]{2,1,0:T(8,128)(2,1)S(1)}, bf16[64,64,512]{2,1,0:T(8,128)(2,1)S(1)}, s32[8,128]{1,0:T(8,128)S(1)}, s32[8,128]{1,0:T(8,128)S(1)}) custom-call(bf16[128,64,512]{2,1,0:T(8,128)(2,1)S(1)} %copy-done, bf16[64,64,512]{2,1,0:T(8,128)(2,1)S(1)} %copy-done.1, bf16[256,256]{1,0:T(8,128)(2,1)S(1)} %copy-done.3, ...), custom_call_target="tpu_custom_call" | custom-call | tf_op jit(solution)/shard_map/transform/pallas_call | solution.py:570
  17.8 0.0 copy-done.5
  17.8 0.0 copy-done.6
  17.8 7.8 %scores.1 = (f32[256,128]{1,0:T(8,128)S(1)}, f32[8,128]{1,0:T(8,128)S(1)}, s32[64]{0:T(128)S(1)}, s32[256]{0:T(256)S(1)}) custom-call(s32[8,128]{1,0:T(8,128)S(1)} %get-tuple-element.17.ids_ref, bf16[128,64,512]{2,1,0:T(8,128)(2,1)S(1)} %get-tuple-element.18.xh_ref, bf16[64,64,512]{2,1,0:T(8,128)(2,1)S(1)} %get-tuple-element.19.rh_ref, ...), custom_call_target="tpu_custom_call" | custom-call | tf_op jit(solution)/shard_map/scores/pallas_call | solution.py:608
  25.6 4.6 %posterior.1 = (f32[256,768]{1,0:T(8,128)S(1)}, f32[256,128]{1,0:T(8,128)S(1)}, f32[1,128]{1,0:T(1,128)S(1)}) custom-call(f32[256,128]{1,0:T(8,128)S(1)} %get-tuple-element.22.scores_ref, f32[8,128]{1,0:T(8,128)S(1)} %get-tuple-element.23.stats_ref, f32[36,512]{1,0:T(8,128)S(1)} %reshape.24.rr_ref), custom_call_target="tpu_custom_call" | custom-call | tf_op jit(solution)/shard_map/posterior/pallas_call | solution.py:645
  30.2 5.1 %gradient.1 = (bf16[64,64,512]{2,1,0:T(8,128)(2,1)S(1)}, f32[64,128]{1,0:T(8,128)S(1)}) custom-call(s32[64]{0:T(128)S(1)} %get-tuple-element.20.head, s32[256]{0:T(256)S(1)} %get-tuple-element.21.nxt, bf16[128,64,512]{2,1,0:T(8,128)(2,1)S(1)} %get-tuple-element.18.xh_ref, bf16[64,64,512]{2,1,0:T(8,128)(2,1)S(1)} %get-tuple-element.19.rh_ref, ...), custom_call_target="tpu_custom_call" | custom-call | tf_op jit(solution)/shard_map/gradient/pallas_call | solution.py:669
  35.3 0.0 copy-start.8
  35.3 80.0 %reduce_over_dp.1 = (bf16[8,64,512]{2,1,0:T(8,128)(2,1)S(1)}, f32[1,128]{1,0:T(1,128)S(1)}) custom-call(bf16[4,2,8,64,512]{4,3,2,1,0:T(8,128)(2,1)S(1)} %bitcast.15, f32[8,8,128]{2,1,0:T(8,128)S(1)} %bitcast.16, f32[1,128]{1,0:T(1,128)S(1)} %get-tuple-element.28.evid_ref, s32[8,128]{1,0:T(8,128)S(1)} %get-tuple-element.29.slots_ref), custom_call_target="tpu_custom_call" | custom-call | tf_op jit(solution)/shard_map/reduce_over_dp/pallas_call | solution.py:508
  115.3 0.0 copy-done.8
  115.3 1.4 %convolution_bitcast_fusion = f32[1,8,64,512]{3,2,1,0:T(8,128)} fusion(bf16[8,64,512]{2,1,0:T(8,128)(2,1)S(1)} %get-tuple-element.30, bf16[512,512,1]{1,0,2:T(8,128)(2,1)S(1)} %copy-done.8), kind=kOutput, calls=%fused_computation | convolution fusion | flops 268435456 | bytes 2097152 | tf_op jit(solution)/shard_map/dot_general | solution.py:694
  116.8 0.5 copy.16
Async XLA Ops:
  1.9 3.4 %copy-start = (bf16[128,64,512]{2,1,0:T(8,128)(2,1)S(1)}, bf16[128,64,512]{2,1,0:T(8,128)(2,1)}, u32[]{:S(2)}) copy-start(bf16[128,64,512]{2,1,0:T(8,128)(2,1)} %image_ref.1) | copy-start | bytes 25165828
  5.3 2.2 %copy-start.1 = (bf16[64,64,512]{2,1,0:T(8,128)(2,1)S(1)}, bf16[64,64,512]{2,1,0:T(8,128)(2,1)}, u32[]{:S(2)}) copy-start(bf16[64,64,512]{2,1,0:T(8,128)(2,1)} %refs_ref.1) | copy-start | bytes 12582916
  7.4 0.9 copy-start.2
  8.3 0.9 copy-start.3
  9.3 0.7 copy-start.4
  9.9 0.7 copy-start.7
  10.6 7.2 %copy-start.5 = (f32[64]{0:T(128)S(1)}, f32[64]{0:T(128)}, u32[]{:S(2)}) copy-start(f32[64]{0:T(128)} %param.14) | copy-start | bytes 772
  10.6 7.2 %copy-start.6 = (s32[64]{0:T(128)S(1)}, s32[64]{0:T(128)}, u32[]{:S(2)}) copy-start(s32[64]{0:T(128)} %param.16) | copy-start | bytes 772
  35.3 80.0 %copy-start.8 = (bf16[512,512,1]{1,0,2:T(8,128)(2,1)S(1)}, bf16[512,512,1]{1,0,2:T(8,128)(2,1)}, u32[]{:S(2)}) copy-start(bf16[512,512,1]{1,0,2:T(8,128)(2,1)} %constant.9) | copy-start | bytes 1572868

commit v5 on v4

--- a/solution.py
+++ b/solution.py
@@ -16,7 +16,6 @@
 ROWS = 16
 MESH = pl.DeviceIdType.MESH
 HIGHEST = lax.Precision.HIGHEST
-FIRST = 4
 MIB = 1024 * 1024
 
 
@@ -88,73 +87,103 @@
 
 
 def transform_kernel(
-    image_steps, classes, image_ref, refs_ref, even_ref, odd_ref, slot_ref, lists_ref,
-    image_out, refs_out, ids_out, slots_out, tags_ref, all_tags, send, recv,
+    image_ref, refs_ref, table_hbm, slot_ref, lists_ref,
+    image_out, refs_out, ids_out, slots_out,
+    image_in, refs_in, table_ref, tags_ref, all_tags, block_sems, small_sems, send, recv,
 ):
-    step = pl.program_id(0)
     start, arrive, sent = share("dp", lambda _: tags_ref, all_tags, send, recv)
     me = lax.axis_index("dp")
     count = lax.axis_size("dp")
     block = tags_ref.shape[1]
-
-    @pl.when(step == 0)
-    def _():
-        greet("dp")
-        tags_ref[...] = jnp.zeros_like(tags_ref)
-        tags_ref[0:1, :] = slot_ref[...]
-        tags_ref[1 : 1 + LIST, :] = lists_ref[...]
-
-    @pl.when(step == image_steps // 2)
-    def _():
-        greeted("dp")
-        start()
-
-    def multiply(source, target):
-        rows = source[...].reshape(ROWS * NSHELL, 2 * NANG)
-        half = NANG // 2
-        re_low, re_high, im_low, im_high = (rows[:, i * half : (i + 1) * half] for i in range(4))
+    classes = refs_ref.shape[0]
+    image_steps = image_ref.shape[0] // ROWS
+    half = NANG // 2
+
+    def rows_of(i):
+        return pl.ds(pl.multiple_of(i * ROWS, ROWS), ROWS)
+
+    def fetch_image(i):
+        return pltpu.make_async_copy(
+            image_ref.at[rows_of(i)], image_in.at[rows_of(i)], block_sems.at[i]
+        )
+
+    def fetch_refs(i):
+        return pltpu.make_async_copy(
+            refs_ref.at[rows_of(i)], refs_in.at[rows_of(i)], block_sems.at[image_steps + i]
+        )
+
+    small = (
+        pltpu.make_async_copy(table_hbm, table_ref, small_sems.at[0]),
+        pltpu.make_async_copy(slot_ref, tags_ref.at[pl.ds(0, 1)], small_sems.at[1]),
+        pltpu.make_async_copy(lists_ref, tags_ref.at[pl.ds(1, LIST)], small_sems.at[2]),
+    )
+
+    def multiply(source, target, i):
+        block_rows = source[rows_of(i)].reshape(ROWS * NSHELL, 2 * NANG)
+        re_low, re_high, im_low, im_high = (
+            block_rows[:, n * half : (n + 1) * half] for n in range(4)
+        )
         plus = jnp.concatenate([re_low + re_high, im_low + im_high], axis=1)
         minus = jnp.concatenate([re_low - re_high, im_low - im_high], axis=1)
-        for n, (mixed, table) in enumerate(((plus, even_ref), (minus, odd_ref))):
-            out = jnp.dot(mixed, table[...], preferred_element_type=jnp.float32)
+        for n, mixed in enumerate((plus, minus)):
+            out = jnp.dot(mixed, table_ref[n], preferred_element_type=jnp.float32)
             out = out.astype(jnp.bfloat16).reshape(ROWS, NSHELL, NANG)
-            target[:, :, n * half : (n + 1) * half] = out[:, :, :half]
-            target[:, :, NANG + n * half : NANG + (n + 1) * half] = out[:, :, half:]
-
-    @pl.when(step < image_steps)
-    def _():
-        multiply(image_ref, image_out)
-
-    @pl.when(step >= image_steps)
-    def _():
-        multiply(refs_ref, refs_out)
-
-    @pl.when(step == pl.num_programs(0) - 1)
-    def _():
-        arrive()
-        all_tags[me] = tags_ref[...]
-        own = tags_ref[0:1, :].astype(jnp.float32)
-        slot = jnp.transpose(jnp.broadcast_to(own, (LANES, block))).astype(jnp.int32)
-        lane = lax.broadcasted_iota(jnp.int32, (block, block), 1)
-
-        def look(d, found):
-            rows = all_tags[d]
-            hit = slot == lane + d * block
-            slots_out[pl.ds(d, 1), :] = rows[0:1]
-            return tuple(
-                total + jnp.where(hit, rows[1 + a : 2 + a], 0) for a, total in enumerate(found)
-            )
-
-        found = lax.fori_loop(
-            0, count, look, (jnp.zeros((block, block), jnp.int32),) * LIST
-        )
-        column = lax.axis_index("cls")
-        ids_out[...] = jnp.zeros_like(ids_out)
-        for a in range(LIST):
-            total = jnp.sum(found[a].astype(jnp.float32), axis=1, keepdims=True)
-            row = jnp.transpose(jnp.broadcast_to(total, (block, LANES)))[0:1]
-            ids_out[a : a + 1, :] = row.astype(jnp.int32) - column * classes
-        sent()
+            target[rows_of(i), :, n * half : (n + 1) * half] = out[:, :, :half]
+            target[rows_of(i), :, NANG + n * half : NANG + (n + 1) * half] = out[:, :, half:]
+
+    def loop(low, high, act):
+        def one(i, carry):
+            act(i)
+            return carry
+
+        lax.fori_loop(low, high, one, 0)
+
+    def image_step(i):
+        fetch_image(i).wait()
+        multiply(image_in, image_out, i)
+
+    def refs_step(i):
+        fetch_refs(i).wait()
+        multiply(refs_in, refs_out, i)
+
+    small[0].start()
+    loop(0, 2, lambda i: fetch_image(i).start())
+    small[1].start()
+    small[2].start()
+    loop(2, image_steps, lambda i: fetch_image(i).start())
+    loop(0, classes // ROWS, lambda i: fetch_refs(i).start())
+    greet("dp")
+    small[0].wait()
+    loop(0, image_steps // 2, image_step)
+    small[1].wait()
+    small[2].wait()
+    greeted("dp")
+    start()
+    loop(image_steps // 2, image_steps, image_step)
+    loop(0, classes // ROWS, refs_step)
+
+    arrive()
+    all_tags[me] = tags_ref[...]
+    own = tags_ref[0:1, :].astype(jnp.float32)
+    slot = jnp.transpose(jnp.broadcast_to(own, (LANES, block))).astype(jnp.int32)
+    lane = lax.broadcasted_iota(jnp.int32, (block, block), 1)
+
+    def look(d, found):
+        rows = all_tags[d]
+        hit = slot == lane + d * block
+        slots_out[pl.ds(d, 1), :] = rows[0:1]
+        return tuple(
+            total + jnp.where(hit, rows[1 + a : 2 + a], 0) for a, total in enumerate(found)
+        )
+
+    found = lax.fori_loop(0, count, look, (jnp.zeros((block, block), jnp.int32),) * LIST)
+    column = lax.axis_index("cls")
+    ids_out[...] = jnp.zeros_like(ids_out)
+    for a in range(LIST):
+        total = jnp.sum(found[a].astype(jnp.float32), axis=1, keepdims=True)
+        row = jnp.transpose(jnp.broadcast_to(total, (block, LANES)))[0:1]
+        ids_out[a : a + 1, :] = row.astype(jnp.int32) - column * classes
+    sent()
 
 
 def listed(ids_ref, chosen, step, classes):
@@ -327,8 +356,8 @@
 
 def reduce_kernel(
     lines, groups, p_ref, weight_ref, evid_ref, slots_ref, out_ref, log_ref,
-    held, own, from_left, from_right, weights, evids, scale,
-    own_sem, pair_send, pair_recv, right_send, right_recv, left_send, left_recv,
+    held, from_left, from_right, weights, evids, scale,
+    pair_send, pair_recv, right_send, right_recv, left_send, left_recv,
     weight_send, weight_recv, evid_send, evid_recv,
 ):
     me = lax.axis_index("dp")
@@ -337,7 +366,6 @@
     partner = me + 1 - 2 * x
     has_left = z > 0
     has_right = z < lines - 1
-    chunks = lines * groups
 
     weight_start, weight_arrive, weight_sent = share(
         "dp", lambda d: weight_ref.at[d], weights, weight_send, weight_recv
@@ -346,60 +374,56 @@
         "dp", lambda _: evid_ref, evids, evid_send, evid_recv
     )
 
-    def where_is(t):
-        layer, i = lax.div(t, 2 * groups), lax.rem(t, 2 * groups)
-        low = lax.rem(i, 2)
-        return (1 - low) * (lines - 1 - layer) + low * layer, lax.div(i, 2)
-
-    def keep(b, g):
-        return pltpu.make_async_copy(p_ref.at[b, x, g], own.at[b, g], own_sem.at[b, g])
+    def some(g):
+        first, size = groups[g]
+        return pl.ds(first, size)
 
     def pair(b, g):
         return pltpu.make_async_remote_copy(
-            src_ref=p_ref.at[b, 1 - x, g], dst_ref=held.at[b, g],
+            src_ref=p_ref.at[b, 1 - x, some(g)], dst_ref=held.at[b, some(g)],
             send_sem=pair_send.at[b, g], recv_sem=pair_recv.at[b, g],
             device_id={"dp": partner}, device_id_type=MESH,
         )
 
     def right(b, g):
         return pltpu.make_async_remote_copy(
-            src_ref=held.at[b, g], dst_ref=from_left.at[b, g],
+            src_ref=held.at[b, some(g)], dst_ref=from_left.at[b, some(g)],
             send_sem=right_send.at[b, g], recv_sem=right_recv.at[b, g],
             device_id={"dp": me + 2}, device_id_type=MESH,
         )
 
     def left(b, g):
         return pltpu.make_async_remote_copy(
-            src_ref=held.at[b, g], dst_ref=from_right.at[b, g],
+            src_ref=held.at[b, some(g)], dst_ref=from_right.at[b, some(g)],
             send_sem=left_send.at[b, g], recv_sem=left_recv.at[b, g],
             device_id={"dp": me - 2}, device_id_type=MESH,
         )
 
     def add(b, g, other):
-        held[b, g] = (
-            held[b, g].astype(jnp.float32) + other[b, g].astype(jnp.float32)
-        ).astype(jnp.bfloat16)
-
-    def each(act):
-        def one(t, carry):
-            act(*where_is(t))
+        first, size = groups[g]
+        for c in range(first, first + size):
+            held[b, c] = (
+                held[b, c].astype(jnp.float32) + other(c).astype(jnp.float32)
+            ).astype(jnp.bfloat16)
+
+    def each(g, act):
+        def one(i, carry):
+            odd, half = lax.rem(i, 2), lax.div(i, 2)
+            act((1 - odd) * (lines - 1 - half) + odd * half, g)
             return carry
 
-        lax.fori_loop(0, chunks, one, 0)
-
-    def relay(t):
-        b, g = where_is(t)
-        keep(b, g).wait()
+        lax.fori_loop(0, lines, one, 0)
+
+    def relay(b, g):
         pair(b, g).wait_recv()
-
-        add(b, g, own)
+        add(b, g, lambda c: p_ref[b, x, c])
 
         @pl.when(z < b)
         def _():
             @pl.when(has_left)
             def _():
                 right(b, g).wait_recv()
-                add(b, g, from_left)
+                add(b, g, lambda c: from_left[b, c])
 
             right(b, g).start()
 
@@ -408,7 +432,7 @@
             @pl.when(has_right)
             def _():
                 left(b, g).wait_recv()
-                add(b, g, from_right)
+                add(b, g, lambda c: from_right[b, c])
 
             left(b, g).start()
 
@@ -431,44 +455,37 @@
         for n in range(2 * NANG // LANES):
             scale[:, n * LANES : (n + 1) * LANES] = inverse
 
-    def finish(g, carry):
+    def finish(g):
         @pl.when(has_left)
         def _():
             right(z, g).wait_recv()
-            held[z, g] = (
-                held[z, g].astype(jnp.float32) + from_left[z, g].astype(jnp.float32)
-            ).astype(jnp.bfloat16)
+            add(z, g, lambda c: from_left[z, c])
 
         @pl.when(has_right)
         def _():
             left(z, g).wait_recv()
-            held[z, g] = (
-                held[z, g].astype(jnp.float32) + from_right[z, g].astype(jnp.float32)
-            ).astype(jnp.bfloat16)
-
-        out_ref[g] = (held[z, g].astype(jnp.float32) * scale[pl.ds(g, 1), :]).astype(jnp.bfloat16)
-        return carry
-
-    each(lambda b, g: keep(b, g).start())
+            add(z, g, lambda c: from_right[z, c])
+
+        first, size = groups[g]
+        for c in range(first, first + size):
+            out_ref[c] = (held[z, c].astype(jnp.float32) * scale[c : c + 1, :]).astype(
+                jnp.bfloat16
+            )
+
     greet("dp")
     greeted("dp")
-
-    def begin(t, carry):
-        pair(*where_is(t)).start()
-        return carry
-
-    lax.fori_loop(0, FIRST, begin, 0)
+    last = len(groups) - 1
+    each(0, lambda b, g: pair(b, g).start())
     weight_start()
     evid_start()
-    lax.fori_loop(FIRST, chunks, begin, 0)
-
-    def passing(t, carry):
-        relay(t)
-        return carry
-
-    lax.fori_loop(0, chunks, passing, 0)
+    for n in range(1, len(groups)):
+        each(n, lambda b, g: pair(b, g).start())
+    for n in range(last):
+        each(n, relay)
     small()
-    lax.fori_loop(0, groups, finish, 0)
+    each(last, relay)
+    for n in range(len(groups)):
+        finish(n)
 
     def drain(b, g):
         pair(b, g).wait_send()
@@ -481,7 +498,8 @@
         def _():
             left(b, g).wait_send()
 
-    each(drain)
+    for n in range(len(groups)):
+        each(n, drain)
     weight_sent()
     evid_sent()
 
@@ -503,23 +521,28 @@
     owned = classes // dp_count
     shape = part.shape[1:]
     whole = pltpu.VMEM((lines, owned) + shape, jnp.bfloat16)
-    sems = pltpu.SemaphoreType.DMA((lines, owned))
+    groups, first = [], 0
+    while first < owned:
+        size = 2 if owned - first > 2 else 1
+        groups.append((first, size))
+        first += size
+    sems = pltpu.SemaphoreType.DMA((lines, len(groups)))
     row_sems = pltpu.SemaphoreType.DMA((dp_count,))
     out, log_evidence = pl.pallas_call(
-        functools.partial(reduce_kernel, lines, owned),
+        functools.partial(reduce_kernel, lines, tuple(groups)),
         out_shape=[
             jax.ShapeDtypeStruct((owned,) + shape, jnp.bfloat16),
             jax.ShapeDtypeStruct((1, block), jnp.float32),
         ],
-        in_specs=[pl.BlockSpec(memory_space=pl.ANY)] + [vmem()] * 3,
+        in_specs=[vmem()] * 4,
         out_specs=[vmem()] * 2,
         scratch_shapes=[
-            whole, whole, whole, whole,
+            whole, whole, whole,
             pltpu.VMEM((dp_count, owned, LANES), jnp.float32),
             pltpu.VMEM((dp_count, 1, block), jnp.float32),
             pltpu.VMEM((owned, 2 * NANG), jnp.float32),
         ]
-        + [sems] * 7
+        + [sems] * 6
         + [row_sems] * 4,
         compiler_params=remote(2, 20),
         name="reduce_over_dp",
@@ -547,8 +570,9 @@
     order = np.concatenate([parity, NANG + parity])
     low = np.concatenate([np.arange(NANG // 2), NANG + np.arange(NANG // 2)])
     evens = np.concatenate([np.arange(0, NANG, 2), NANG + np.arange(0, NANG, 2)])
-    even = jnp.asarray(full_table[np.ix_(low, evens)].astype(jnp.bfloat16))
-    odd = jnp.asarray(full_table[np.ix_(low, evens + 1)].astype(jnp.bfloat16))
+    table = jnp.asarray(
+        np.stack([full_table[np.ix_(low, evens + n)] for n in range(2)]).astype(jnp.bfloat16)
+    )
     inverse = jnp.asarray(np.ascontiguousarray(full_table.T[order]).astype(jnp.bfloat16))
     rotation_response = jnp.transpose(
         rotation_response.reshape(rotations, 2, NANG // 2, 2), (0, 1, 3, 2)
@@ -558,27 +582,10 @@
     ref_steps = classes // ROWS
     cube = (ROWS, NSHELL, width)
 
-    def fixed(shape):
-        return pl.BlockSpec(shape, lambda i: (0,) * len(shape))
-
-    def image_block():
-        return pl.BlockSpec(cube, lambda i: (jnp.minimum(i, image_steps - 1), 0, 0))
-
-    def ref_block():
-        return pl.BlockSpec(cube, lambda i: (jnp.maximum(i - image_steps, 0), 0, 0))
-
     image_hat, ref_hat, ids, slots = pl.pallas_call(
-        functools.partial(transform_kernel, image_steps, classes),
-        grid=(image_steps + ref_steps,),
-        in_specs=[
-            image_block(),
-            ref_block(),
-            fixed((NANG, NANG)),
-            fixed((NANG, NANG)),
-            fixed((1, block)),
-            fixed((LIST, block)),
-        ],
-        out_specs=[image_block(), ref_block(), fixed((8, block)), fixed((dp_count, block))],
+        transform_kernel,
+        in_specs=[pl.BlockSpec(memory_space=pltpu.HBM)] * 5,
+        out_specs=[vmem()] * 4,
         out_shape=[
             jax.ShapeDtypeStruct(images.shape, jnp.bfloat16),
             jax.ShapeDtypeStruct(references.shape, jnp.bfloat16),
@@ -586,14 +593,19 @@
             jax.ShapeDtypeStruct((dp_count, block), jnp.int32),
         ],
         scratch_shapes=[
+            pltpu.VMEM(images.shape, jnp.bfloat16),
+            pltpu.VMEM(references.shape, jnp.bfloat16),
+            pltpu.VMEM((2, NANG, NANG), jnp.bfloat16),
             pltpu.VMEM((8, block), jnp.int32),
             pltpu.VMEM((dp_count, 8, block), jnp.int32),
+            pltpu.SemaphoreType.DMA((image_steps + ref_steps,)),
+            pltpu.SemaphoreType.DMA((3,)),
             pltpu.SemaphoreType.DMA((dp_count,)),
             pltpu.SemaphoreType.DMA((dp_count,)),
         ],
-        compiler_params=remote(0, 24),
+        compiler_params=remote(0, 36),
         name="transform",
-    )(images, references, even, odd, pose_slot[None, :], class_lists.T)
+    )(images, references, table, pose_slot[None, :], class_lists.T)
 
     def whole(shape):
         return pl.BlockSpec(shape, lambda i, c: (0,) * len(shape))

time: 118 us -> 100 us (0.85)
  the two profiles are of different devices: /device:TPU:20 before, /device:TPU:0 now
where the time goes in v5:
time: 100 us
  Pallas kernels  91.9 us (92%)
  local copies, waits for them, and re-layouts  6.21 us (6%)
  matrix products  1.41 us (1%)
    pallas_call x1, Pallas kernels, reduce_scatter(): pl.pallas_call(functools.partial(reduce_kernel, lines, tuple(groups)), ou...  63.4 us
    pallas_call x1, Pallas kernels, local(): pl.pallas_call(transform_kernel, in_specs=[pl.BlockSpec(memory_space=pltp...  11.3 us
    pallas_call x1, Pallas kernels, local(): pl.pallas_call(score_kernel, grid_spec=pltpu.PrefetchScalarGridSpec(num_s...  7.63 us
    unnamed x16, local copies, waits for them, and re-layouts  6.01 us
    pallas_call x1, Pallas kernels, local(): pl.pallas_call(grad_kernel, grid_spec=pltpu.PrefetchScalarGridSpec(num_sc...  4.93 us
    pallas_call x1, Pallas kernels, local(): pl.pallas_call(posterior_kernel, in_specs=[vmem()] * 3, out_specs=[vmem()...  4.6 us

profile of v5, /device:TPU:0, one launch (start us, length us, event | category | flops | bytes accessed | tf_op | source)
XLA Modules:
  0.0 100.3 jit_solution(7163473928097323370)
XLA Ops:
  0.6 1.0 %copy.12 = f32[36,512]{0,1:T(8,128)S(1)} copy(f32[36,512]{1,0:T(8,128)} %param.12) | data formatting | bytes 147456 | tf_op args[3]
  1.7 0.1 copy.13
  1.8 0.1 reshape.24.rr_ref
  1.9 0.0 copy-start
  1.9 2.2 %copy-done = bf16[64,64,512]{2,1,0:T(8,128)(2,1)S(1)} copy-done((bf16[64,64,512]{2,1,0:T(8,128)(2,1)S(1)}, bf16[64,64,512]{2,1,0:T(8,128)(2,1)}, u32[]{:S(2)}) %copy-start) | copy-done | bytes 4194328
  4.1 0.0 copy-start.1
  4.1 0.9 copy-done.1
  5.0 0.0 copy-start.2
  5.0 0.7 copy-done.2
  5.7 0.0 copy-start.5
  5.7 0.7 copy-done.5
  6.3 0.0 copy-start.3
  6.3 0.0 copy-start.4
  6.3 11.3 %transform.1 = (bf16[128,64,512]{2,1,0:T(8,128)(2,1)S(1)}, bf16[64,64,512]{2,1,0:T(8,128)(2,1)S(1)}, s32[8,128]{1,0:T(8,128)S(1)}, s32[8,128]{1,0:T(8,128)S(1)}) custom-call(bf16[128,64,512]{2,1,0:T(8,128)(2,1)} %image_ref.1, bf16[64,64,512]{2,1,0:T(8,128)(2,1)S(1)} %copy-done, bf16[2,256,256]{2,1,0:T(8,128)(2,1)S(1)} %copy-done.1, s32[1,128]{1,0:T(1,128)S(1)} %bitcast.20, ...), custom_call_target="tpu_custom_call" | custom-call | tf_op jit(solution)/shard_map/transform/pallas_call | solution.py:585
  17.7 0.0 copy-done.3
  17.7 0.0 copy-done.4
  17.7 7.6 %scores.1 = (f32[256,128]{1,0:T(8,128)S(1)}, f32[8,128]{1,0:T(8,128)S(1)}, s32[64]{0:T(128)S(1)}, s32[256]{0:T(256)S(1)}) custom-call(s32[8,128]{1,0:T(8,128)S(1)} %get-tuple-element.17.ids_ref, bf16[128,64,512]{2,1,0:T(8,128)(2,1)S(1)} %get-tuple-element.18.xh_ref, bf16[64,64,512]{2,1,0:T(8,128)(2,1)S(1)} %get-tuple-element.19.rh_ref, ...), custom_call_target="tpu_custom_call" | custom-call | tf_op jit(solution)/shard_map/scores/pallas_call | solution.py:620
  25.3 4.6 %posterior.1 = (f32[256,768]{1,0:T(8,128)S(1)}, f32[256,128]{1,0:T(8,128)S(1)}, f32[1,128]{1,0:T(1,128)S(1)}) custom-call(f32[256,128]{1,0:T(8,128)S(1)} %get-tuple-element.22.scores_ref, f32[8,128]{1,0:T(8,128)S(1)} %get-tuple-element.23.stats_ref, f32[36,512]{1,0:T(8,128)S(1)} %reshape.24.rr_ref), custom_call_target="tpu_custom_call" | custom-call | tf_op jit(solution)/shard_map/posterior/pallas_call | solution.py:657
  30.0 4.9 %gradient.1 = (bf16[64,64,512]{2,1,0:T(8,128)(2,1)S(1)}, f32[64,128]{1,0:T(8,128)S(1)}) custom-call(s32[64]{0:T(128)S(1)} %get-tuple-element.20.head, s32[256]{0:T(256)S(1)} %get-tuple-element.21.nxt, bf16[128,64,512]{2,1,0:T(8,128)(2,1)S(1)} %get-tuple-element.18.xh_ref, bf16[64,64,512]{2,1,0:T(8,128)(2,1)S(1)} %get-tuple-element.19.rh_ref, ...), custom_call_target="tpu_custom_call" | custom-call | tf_op jit(solution)/shard_map/gradient/pallas_call | solution.py:681
  34.9 0.0 copy-start.6
  34.9 63.4 %reduce_over_dp.1 = (bf16[8,64,512]{2,1,0:T(8,128)(2,1)S(1)}, f32[1,128]{1,0:T(1,128)S(1)}) custom-call(bf16[4,2,8,64,512]{4,3,2,1,0:T(8,128)(2,1)S(1)} %bitcast.15, f32[8,8,128]{2,1,0:T(8,128)S(1)} %bitcast.16, f32[1,128]{1,0:T(1,128)S(1)} %get-tuple-element.28.evid_ref, s32[8,128]{1,0:T(8,128)S(1)} %get-tuple-element.29.slots_ref), custom_call_target="tpu_custom_call" | custom-call | tf_op jit(solution)/shard_map/reduce_over_dp/pallas_call | solution.py:531
  98.3 0.0 copy-done.6
  98.4 1.4 %convolution_bitcast_fusion = f32[1,8,64,512]{3,2,1,0:T(8,128)} fusion(bf16[8,64,512]{2,1,0:T(8,128)(2,1)S(1)} %get-tuple-element.30, bf16[512,512,1]{1,0,2:T(8,128)(2,1)S(1)} %copy-done.6), kind=kOutput, calls=%fused_computation | convolution fusion | flops 268435456 | bytes 2097152 | tf_op jit(solution)/shard_map/dot_general | solution.py:706
  99.8 0.5 copy.15
Async XLA Ops:
  1.9 2.2 %copy-start = (bf16[64,64,512]{2,1,0:T(8,128)(2,1)S(1)}, bf16[64,64,512]{2,1,0:T(8,128)(2,1)}, u32[]{:S(2)}) copy-start(bf16[64,64,512]{2,1,0:T(8,128)(2,1)} %refs_ref.1) | copy-start | bytes 12582916
  4.1 0.9 copy-start.1
  5.0 0.7 copy-start.2
  5.7 0.7 copy-start.5
  6.3 11.3 %copy-start.3 = (f32[64]{0:T(128)S(1)}, f32[64]{0:T(128)}, u32[]{:S(2)}) copy-start(f32[64]{0:T(128)} %param.13) | copy-start | bytes 772
  6.3 11.4 %copy-start.4 = (s32[64]{0:T(128)S(1)}, s32[64]{0:T(128)}, u32[]{:S(2)}) copy-start(s32[64]{0:T(128)} %param.15) | copy-start | bytes 772
  34.9 63.5 %copy-start.6 = (bf16[512,512,1]{1,0,2:T(8,128)(2,1)S(1)}, bf16[512,512,1]{1,0,2:T(8,128)(2,1)}, u32[]{:S(2)}) copy-start(bf16[512,512,1]{1,0,2:T(8,128)(2,1)} %constant.6) | copy-start | bytes 1572868

commit v6 on v5

--- a/solution.py
+++ b/solution.py
@@ -355,10 +355,12 @@
 
 
 def reduce_kernel(
-    lines, groups, p_ref, weight_ref, evid_ref, slots_ref, out_ref, log_ref,
+    lines, groups, early, p_ref, weight_ref, evid_ref, slots_ref, out_ref, log_ref,
     held, from_left, from_right, weights, evids, scale,
+    both, both_left, both_right, swapped,
     pair_send, pair_recv, right_send, right_recv, left_send, left_recv,
     weight_send, weight_recv, evid_send, evid_recv,
+    first_sems, swap_sems,
 ):
     me = lax.axis_index("dp")
     x = lax.rem(me, 2)
@@ -398,6 +400,94 @@
             send_sem=left_send.at[b, g], recv_sem=left_recv.at[b, g],
             device_id={"dp": me - 2}, device_id_type=MESH,
         )
+
+    def both_to_right(b):
+        return pltpu.make_async_remote_copy(
+            src_ref=both.at[b], dst_ref=both_left.at[b],
+            send_sem=first_sems.at[0, b], recv_sem=first_sems.at[1, b],
+            device_id={"dp": me + 2}, device_id_type=MESH,
+        )
+
+    def both_to_left(b):
+        return pltpu.make_async_remote_copy(
+            src_ref=both.at[b], dst_ref=both_right.at[b],
+            send_sem=first_sems.at[2, b], recv_sem=first_sems.at[3, b],
+            device_id={"dp": me - 2}, device_id_type=MESH,
+        )
+
+    def swap():
+        return pltpu.make_async_remote_copy(
+            src_ref=both.at[z, 1 - x], dst_ref=swapped,
+            send_sem=swap_sems.at[0], recv_sem=swap_sems.at[1],
+            device_id={"dp": partner}, device_id_type=MESH,
+        )
+
+    def both_own(b):
+        for side in range(2):
+            both[b, side] = p_ref[b, side, early]
+
+    def both_add(b, other):
+        for side in range(2):
+            both[b, side] = (
+                both[b, side].astype(jnp.float32) + other[b, side].astype(jnp.float32)
+            ).astype(jnp.bfloat16)
+
+    def both_ends(b, _):
+        @pl.when((z < b) & jnp.logical_not(has_left))
+        def _():
+            both_own(b)
+            both_to_right(b).start()
+
+        @pl.when((z > b) & jnp.logical_not(has_right))
+        def _():
+            both_own(b)
+            both_to_left(b).start()
+
+    def both_relay(b, _):
+        @pl.when((z < b) & has_left)
+        def _():
+            both_own(b)
+            both_to_right(b).wait_recv()
+            both_add(b, both_left)
+            both_to_right(b).start()
+
+        @pl.when((z > b) & has_right)
+        def _():
+            both_own(b)
+            both_to_left(b).wait_recv()
+            both_add(b, both_right)
+            both_to_left(b).start()
+
+    def both_swap():
+        both_own(z)
+
+        @pl.when(has_left)
+        def _():
+            both_to_right(z).wait_recv()
+            both_add(z, both_left)
+
+        @pl.when(has_right)
+        def _():
+            both_to_left(z).wait_recv()
+            both_add(z, both_right)
+
+        swap().start()
+
+    def both_finish():
+        swap().wait_recv()
+        out_ref[early] = (
+            (both[z, x].astype(jnp.float32) + swapped[...].astype(jnp.float32))
+            * scale[early : early + 1, :]
+        ).astype(jnp.bfloat16)
+
+    def both_drain(b, _):
+        @pl.when(z < b)
+        def _():
+            both_to_right(b).wait_send()
+
+        @pl.when(z > b)
+        def _():
+            both_to_left(b).wait_send()
 
     def add(b, g, other):
         first, size = groups[g]
@@ -476,14 +566,22 @@
     greeted("dp")
     last = len(groups) - 1
     each(0, lambda b, g: pair(b, g).start())
+    if early is not None:
+        each(0, both_ends)
     weight_start()
     evid_start()
     for n in range(1, len(groups)):
         each(n, lambda b, g: pair(b, g).start())
     for n in range(last):
         each(n, relay)
+        if early is not None and n == 0:
+            each(0, both_relay)
+        if early is not None and n == last - 1:
+            both_swap()
     small()
     each(last, relay)
+    if early is not None:
+        both_finish()
     for n in range(len(groups)):
         finish(n)
 
@@ -500,6 +598,9 @@
 
     for n in range(len(groups)):
         each(n, drain)
+    if early is not None:
+        each(0, both_drain)
+        swap().wait_send()
     weight_sent()
     evid_sent()
 
@@ -522,14 +623,16 @@
     shape = part.shape[1:]
     whole = pltpu.VMEM((lines, owned) + shape, jnp.bfloat16)
     groups, first = [], 0
-    while first < owned:
-        size = 2 if owned - first > 2 else 1
+    early = owned - 1 if owned >= 8 and lines > 1 else None
+    stop = owned if early is None else early
+    while first < stop:
+        size = 2 if stop - first > 1 else 1
         groups.append((first, size))
         first += size
     sems = pltpu.SemaphoreType.DMA((lines, len(groups)))
     row_sems = pltpu.SemaphoreType.DMA((dp_count,))
     out, log_evidence = pl.pallas_call(
-        functools.partial(reduce_kernel, lines, tuple(groups)),
+        functools.partial(reduce_kernel, lines, tuple(groups), early),
         out_shape=[
             jax.ShapeDtypeStruct((owned,) + shape, jnp.bfloat16),
             jax.ShapeDtypeStruct((1, block), jnp.float32),
@@ -541,9 +644,14 @@
             pltpu.VMEM((dp_count, owned, LANES), jnp.float32),
             pltpu.VMEM((dp_count, 1, block), jnp.float32),
             pltpu.VMEM((owned, 2 * NANG), jnp.float32),
+            pltpu.VMEM((lines, 2) + shape, jnp.bfloat16),
+            pltpu.VMEM((lines, 2) + shape, jnp.bfloat16),
+            pltpu.VMEM((lines, 2) + shape, jnp.bfloat16),
+            pltpu.VMEM(shape, jnp.bfloat16),
         ]
         + [sems] * 6
-        + [row_sems] * 4,
+        + [row_sems] * 4
+        + [pltpu.SemaphoreType.DMA((4, lines)), pltpu.SemaphoreType.DMA((2,))],
         compiler_params=remote(2, 20),
         name="reduce_over_dp",
     )(

time: 100 us -> 104 us (1.040)
  Pallas kernels: 91.9 us -> 95.4 us
    pallas_call x1, Pallas kernels: 63.4 us -> 68 us  [reduce_scatter(): pl.pallas_call(functools.partial(reduce_kernel, lines, tuple(groups), ear...]
where the time goes in v6:
time: 104 us
  Pallas kernels  95.4 us (92%)
  local copies, waits for them, and re-layouts  6.21 us (6%)
  matrix products  1.41 us (1%)
    pallas_call x1, Pallas kernels, reduce_scatter(): pl.pallas_call(functools.partial(reduce_kernel, lines, tuple(groups), ear...  68 us
    pallas_call x1, Pallas kernels, local(): pl.pallas_call(transform_kernel, in_specs=[pl.BlockSpec(memory_space=pltp...  11.3 us
    pallas_call x1, Pallas kernels, local(): pl.pallas_call(score_kernel, grid_spec=pltpu.PrefetchScalarGridSpec(num_s...  6.94 us
    unnamed x16, local copies, waits for them, and re-layouts  6.01 us
    pallas_call x1, Pallas kernels, local(): pl.pallas_call(posterior_kernel, in_specs=[vmem()] * 3, out_specs=[vmem()...  4.6 us
    pallas_call x1, Pallas kernels, local(): pl.pallas_call(grad_kernel, grid_spec=pltpu.PrefetchScalarGridSpec(num_sc...  4.55 us

profile of v6, /device:TPU:0, one launch (start us, length us, event | category | flops | bytes accessed | tf_op | source)
XLA Modules:
  0.0 103.8 jit_solution(2805459312015694690)
XLA Ops:
  0.6 1.0 copy.12
  1.7 0.1 copy.13
  1.8 0.1 reshape.24.rr_ref
  1.9 0.0 copy-start
  1.9 2.2 %copy-done = bf16[64,64,512]{2,1,0:T(8,128)(2,1)S(1)} copy-done((bf16[64,64,512]{2,1,0:T(8,128)(2,1)S(1)}, bf16[64,64,512]{2,1,0:T(8,128)(2,1)}, u32[]{:S(2)}) %copy-start) | copy-done | bytes 4194328
  4.1 0.0 copy-start.1
  4.1 0.9 copy-done.1
  5.0 0.0 copy-start.2
  5.0 0.7 copy-done.2
  5.7 0.0 copy-start.5
  5.7 0.7 copy-done.5
  6.3 0.0 copy-start.3
  6.3 0.0 copy-start.4
  6.3 11.3 %transform.1 = (bf16[128,64,512]{2,1,0:T(8,128)(2,1)S(1)}, bf16[64,64,512]{2,1,0:T(8,128)(2,1)S(1)}, s32[8,128]{1,0:T(8,128)S(1)}, s32[8,128]{1,0:T(8,128)S(1)}) custom-call(bf16[128,64,512]{2,1,0:T(8,128)(2,1)} %image_ref.1, bf16[64,64,512]{2,1,0:T(8,128)(2,1)S(1)} %copy-done, bf16[2,256,256]{2,1,0:T(8,128)(2,1)S(1)} %copy-done.1, s32[1,128]{1,0:T(1,128)S(1)} %bitcast.20, ...), custom_call_target="tpu_custom_call" | custom-call | tf_op jit(solution)/shard_map/transform/pallas_call | solution.py:693
  17.7 0.0 copy-done.3
  17.7 0.0 copy-done.4
  17.7 6.9 %scores.1 = (f32[256,128]{1,0:T(8,128)S(1)}, f32[8,128]{1,0:T(8,128)S(1)}, s32[64]{0:T(128)S(1)}, s32[256]{0:T(256)S(1)}) custom-call(s32[8,128]{1,0:T(8,128)S(1)} %get-tuple-element.17.ids_ref, bf16[128,64,512]{2,1,0:T(8,128)(2,1)S(1)} %get-tuple-element.18.xh_ref, bf16[64,64,512]{2,1,0:T(8,128)(2,1)S(1)} %get-tuple-element.19.rh_ref, ...), custom_call_target="tpu_custom_call" | custom-call | tf_op jit(solution)/shard_map/scores/pallas_call | solution.py:728
  24.7 4.6 %posterior.1 = (f32[256,768]{1,0:T(8,128)S(1)}, f32[256,128]{1,0:T(8,128)S(1)}, f32[1,128]{1,0:T(1,128)S(1)}) custom-call(f32[256,128]{1,0:T(8,128)S(1)} %get-tuple-element.22.scores_ref, f32[8,128]{1,0:T(8,128)S(1)} %get-tuple-element.23.stats_ref, f32[36,512]{1,0:T(8,128)S(1)} %reshape.24.rr_ref), custom_call_target="tpu_custom_call" | custom-call | tf_op jit(solution)/shard_map/posterior/pallas_call | solution.py:765
  29.3 4.5 %gradient.1 = (bf16[64,64,512]{2,1,0:T(8,128)(2,1)S(1)}, f32[64,128]{1,0:T(8,128)S(1)}) custom-call(s32[64]{0:T(128)S(1)} %get-tuple-element.20.head, s32[256]{0:T(256)S(1)} %get-tuple-element.21.nxt, bf16[128,64,512]{2,1,0:T(8,128)(2,1)S(1)} %get-tuple-element.18.xh_ref, bf16[64,64,512]{2,1,0:T(8,128)(2,1)S(1)} %get-tuple-element.19.rh_ref, ...), custom_call_target="tpu_custom_call" | custom-call | tf_op jit(solution)/shard_map/gradient/pallas_call | solution.py:789
  33.8 0.0 copy-start.6
  33.8 68.0 %reduce_over_dp.1 = (bf16[8,64,512]{2,1,0:T(8,128)(2,1)S(1)}, f32[1,128]{1,0:T(1,128)S(1)}) custom-call(bf16[4,2,8,64,512]{4,3,2,1,0:T(8,128)(2,1)S(1)} %bitcast.15, f32[8,8,128]{2,1,0:T(8,128)S(1)} %bitcast.16, f32[1,128]{1,0:T(1,128)S(1)} %get-tuple-element.28.evid_ref, s32[8,128]{1,0:T(8,128)S(1)} %get-tuple-element.29.slots_ref), custom_call_target="tpu_custom_call" | custom-call | tf_op jit(solution)/shard_map/reduce_over_dp/pallas_call | solution.py:634
  101.8 0.0 copy-done.6
  101.9 1.4 %convolution_bitcast_fusion = f32[1,8,64,512]{3,2,1,0:T(8,128)} fusion(bf16[8,64,512]{2,1,0:T(8,128)(2,1)S(1)} %get-tuple-element.30, bf16[512,512,1]{1,0,2:T(8,128)(2,1)S(1)} %copy-done.6), kind=kOutput, calls=%fused_computation | convolution fusion | flops 268435456 | bytes 2097152 | tf_op jit(solution)/shard_map/dot_general | solution.py:814
  103.3 0.5 copy.15
Async XLA Ops:
  1.9 2.2 %copy-start = (bf16[64,64,512]{2,1,0:T(8,128)(2,1)S(1)}, bf16[64,64,512]{2,1,0:T(8,128)(2,1)}, u32[]{:S(2)}) copy-start(bf16[64,64,512]{2,1,0:T(8,128)(2,1)} %refs_ref.1) | copy-start | bytes 12582916
  4.1 0.9 copy-start.1
  5.0 0.7 copy-start.2
  5.7 0.7 copy-start.5
  6.3 11.3 %copy-start.3 = (f32[64]{0:T(128)S(1)}, f32[64]{0:T(128)}, u32[]{:S(2)}) copy-start(f32[64]{0:T(128)} %param.13) | copy-start | bytes 772
  6.3 11.4 %copy-start.4 = (s32[64]{0:T(128)S(1)}, s32[64]{0:T(128)}, u32[]{:S(2)}) copy-start(s32[64]{0:T(128)} %param.15) | copy-start | bytes 772
  33.8 68.0 %copy-start.6 = (bf16[512,512,1]{1,0,2:T(8,128)(2,1)S(1)}, bf16[512,512,1]{1,0,2:T(8,128)(2,1)}, u32[]{:S(2)}) copy-start(bf16[512,512,1]{1,0,2:T(8,128)(2,1)} %constant.6) | copy-start | bytes 1572868

commit v7 on v5

--- a/solution.py
+++ b/solution.py
@@ -523,7 +523,7 @@
     whole = pltpu.VMEM((lines, owned) + shape, jnp.bfloat16)
     groups, first = [], 0
     while first < owned:
-        size = 2 if owned - first > 2 else 1
+        size = min(2, owned - first)
         groups.append((first, size))
         first += size
     sems = pltpu.SemaphoreType.DMA((lines, len(groups)))

time: 100 us -> 96.2 us (0.962)
  Pallas kernels: 91.9 us -> 87.9 us
    pallas_call x1, Pallas kernels: 63.4 us -> 58.6 us  [reduce_scatter(): pl.pallas_call(functools.partial(reduce_kernel, lines, tuple(groups)), ou...]
where the time goes in v7:
time: 96.2 us; the launch traced here: 96.3 us
  Pallas kernels  87.9 us (91%)
  local copies, waits for them, and re-layouts  6.21 us (6%)
  matrix products  1.41 us (1%)
    pallas_call x1, Pallas kernels, reduce_scatter(): pl.pallas_call(functools.partial(reduce_kernel, lines, tuple(groups)), ou...  58.6 us
    pallas_call x1, Pallas kernels, local(): pl.pallas_call(transform_kernel, in_specs=[pl.BlockSpec(memory_space=pltp...  11.3 us
    pallas_call x1, Pallas kernels, local(): pl.pallas_call(score_kernel, grid_spec=pltpu.PrefetchScalarGridSpec(num_s...  8.13 us
    unnamed x16, local copies, waits for them, and re-layouts  6.01 us
    pallas_call x1, Pallas kernels, local(): pl.pallas_call(grad_kernel, grid_spec=pltpu.PrefetchScalarGridSpec(num_sc...  5.25 us
    pallas_call x1, Pallas kernels, local(): pl.pallas_call(posterior_kernel, in_specs=[vmem()] * 3, out_specs=[vmem()...  4.6 us

profile of v7, /device:TPU:0, one launch (start us, length us, event | category | flops | bytes accessed | tf_op | source)
XLA Modules:
  0.0 96.3 jit_solution(2824011472560405680)
XLA Ops:
  0.6 1.0 %copy.12 = f32[36,512]{0,1:T(8,128)S(1)} copy(f32[36,512]{1,0:T(8,128)} %param.12) | data formatting | bytes 147456 | tf_op args[3]
  1.7 0.1 copy.13
  1.8 0.1 reshape.24.rr_ref
  1.9 0.0 copy-start
  1.9 2.2 %copy-done = bf16[64,64,512]{2,1,0:T(8,128)(2,1)S(1)} copy-done((bf16[64,64,512]{2,1,0:T(8,128)(2,1)S(1)}, bf16[64,64,512]{2,1,0:T(8,128)(2,1)}, u32[]{:S(2)}) %copy-start) | copy-done | bytes 4194328
  4.1 0.0 copy-start.1
  4.1 0.9 copy-done.1
  5.0 0.0 copy-start.2
  5.0 0.7 copy-done.2
  5.7 0.0 copy-start.5
  5.7 0.7 copy-done.5
  6.3 0.0 copy-start.3
  6.3 0.0 copy-start.4
  6.3 11.3 %transform.1 = (bf16[128,64,512]{2,1,0:T(8,128)(2,1)S(1)}, bf16[64,64,512]{2,1,0:T(8,128)(2,1)S(1)}, s32[8,128]{1,0:T(8,128)S(1)}, s32[8,128]{1,0:T(8,128)S(1)}) custom-call(bf16[128,64,512]{2,1,0:T(8,128)(2,1)} %image_ref.1, bf16[64,64,512]{2,1,0:T(8,128)(2,1)S(1)} %copy-done, bf16[2,256,256]{2,1,0:T(8,128)(2,1)S(1)} %copy-done.1, s32[1,128]{1,0:T(1,128)S(1)} %bitcast.20, ...), custom_call_target="tpu_custom_call" | custom-call | tf_op jit(solution)/shard_map/transform/pallas_call | solution.py:585
  17.7 0.0 copy-done.3
  17.7 0.0 copy-done.4
  17.7 8.1 %scores.1 = (f32[256,128]{1,0:T(8,128)S(1)}, f32[8,128]{1,0:T(8,128)S(1)}, s32[64]{0:T(128)S(1)}, s32[256]{0:T(256)S(1)}) custom-call(s32[8,128]{1,0:T(8,128)S(1)} %get-tuple-element.17.ids_ref, bf16[128,64,512]{2,1,0:T(8,128)(2,1)S(1)} %get-tuple-element.18.xh_ref, bf16[64,64,512]{2,1,0:T(8,128)(2,1)S(1)} %get-tuple-element.19.rh_ref, ...), custom_call_target="tpu_custom_call" | custom-call | tf_op jit(solution)/shard_map/scores/pallas_call | solution.py:620
  25.8 4.6 %posterior.1 = (f32[256,768]{1,0:T(8,128)S(1)}, f32[256,128]{1,0:T(8,128)S(1)}, f32[1,128]{1,0:T(1,128)S(1)}) custom-call(f32[256,128]{1,0:T(8,128)S(1)} %get-tuple-element.22.scores_ref, f32[8,128]{1,0:T(8,128)S(1)} %get-tuple-element.23.stats_ref, f32[36,512]{1,0:T(8,128)S(1)} %reshape.24.rr_ref), custom_call_target="tpu_custom_call" | custom-call | tf_op jit(solution)/shard_map/posterior/pallas_call | solution.py:657
  30.5 5.2 %gradient.1 = (bf16[64,64,512]{2,1,0:T(8,128)(2,1)S(1)}, f32[64,128]{1,0:T(8,128)S(1)}) custom-call(s32[64]{0:T(128)S(1)} %get-tuple-element.20.head, s32[256]{0:T(256)S(1)} %get-tuple-element.21.nxt, bf16[128,64,512]{2,1,0:T(8,128)(2,1)S(1)} %get-tuple-element.18.xh_ref, bf16[64,64,512]{2,1,0:T(8,128)(2,1)S(1)} %get-tuple-element.19.rh_ref, ...), custom_call_target="tpu_custom_call" | custom-call | tf_op jit(solution)/shard_map/gradient/pallas_call | solution.py:681
  35.7 0.0 copy-start.6
  35.7 58.6 %reduce_over_dp.1 = (bf16[8,64,512]{2,1,0:T(8,128)(2,1)S(1)}, f32[1,128]{1,0:T(1,128)S(1)}) custom-call(bf16[4,2,8,64,512]{4,3,2,1,0:T(8,128)(2,1)S(1)} %bitcast.15, f32[8,8,128]{2,1,0:T(8,128)S(1)} %bitcast.16, f32[1,128]{1,0:T(1,128)S(1)} %get-tuple-element.28.evid_ref, s32[8,128]{1,0:T(8,128)S(1)} %get-tuple-element.29.slots_ref), custom_call_target="tpu_custom_call" | custom-call | tf_op jit(solution)/shard_map/reduce_over_dp/pallas_call | solution.py:531
  94.4 0.0 copy-done.6
  94.4 1.4 %convolution_bitcast_fusion = f32[1,8,64,512]{3,2,1,0:T(8,128)} fusion(bf16[8,64,512]{2,1,0:T(8,128)(2,1)S(1)} %get-tuple-element.30, bf16[512,512,1]{1,0,2:T(8,128)(2,1)S(1)} %copy-done.6), kind=kOutput, calls=%fused_computation | convolution fusion | flops 268435456 | bytes 2097152 | tf_op jit(solution)/shard_map/dot_general | solution.py:706
  95.8 0.5 copy.15
Async XLA Ops:
  1.9 2.2 %copy-start = (bf16[64,64,512]{2,1,0:T(8,128)(2,1)S(1)}, bf16[64,64,512]{2,1,0:T(8,128)(2,1)}, u32[]{:S(2)}) copy-start(bf16[64,64,512]{2,1,0:T(8,128)(2,1)} %refs_ref.1) | copy-start | bytes 12582916
  4.1 0.9 copy-start.1
  5.0 0.7 copy-start.2
  5.7 0.7 copy-start.5
  6.3 11.3 %copy-start.3 = (f32[64]{0:T(128)S(1)}, f32[64]{0:T(128)}, u32[]{:S(2)}) copy-start(f32[64]{0:T(128)} %param.13) | copy-start | bytes 772
  6.3 11.4 %copy-start.4 = (s32[64]{0:T(128)S(1)}, s32[64]{0:T(128)}, u32[]{:S(2)}) copy-start(s32[64]{0:T(128)} %param.15) | copy-start | bytes 772
  35.7 58.7 %copy-start.6 = (bf16[512,512,1]{1,0,2:T(8,128)(2,1)S(1)}, bf16[512,512,1]{1,0,2:T(8,128)(2,1)}, u32[]{:S(2)}) copy-start(bf16[512,512,1]{1,0,2:T(8,128)(2,1)} %constant.6) | copy-start | bytes 1572868

commit v8 on v7

--- a/solution.py
+++ b/solution.py
@@ -523,7 +523,7 @@
     whole = pltpu.VMEM((lines, owned) + shape, jnp.bfloat16)
     groups, first = [], 0
     while first < owned:
-        size = min(2, owned - first)
+        size = min(3, owned - first)
         groups.append((first, size))
         first += size
     sems = pltpu.SemaphoreType.DMA((lines, len(groups)))

time: 96.2 us -> 97.2 us (1.010)
  Pallas kernels: 87.9 us -> 89.1 us
    pallas_call x1, Pallas kernels: 58.6 us -> 60.7 us  [reduce_scatter(): pl.pallas_call(functools.partial(reduce_kernel, lines, tuple(groups)), ou...]
where the time goes in v8:
time: 97.2 us; the launch traced here: 97.4 us
  Pallas kernels  89.1 us (92%)
  local copies, waits for them, and re-layouts  6.21 us (6%)
  matrix products  1.41 us (1%)
    pallas_call x1, Pallas kernels, reduce_scatter(): pl.pallas_call(functools.partial(reduce_kernel, lines, tuple(groups)), ou...  60.7 us
    pallas_call x1, Pallas kernels, local(): pl.pallas_call(transform_kernel, in_specs=[pl.BlockSpec(memory_space=pltp...  11.3 us
    pallas_call x1, Pallas kernels, local(): pl.pallas_call(score_kernel, grid_spec=pltpu.PrefetchScalarGridSpec(num_s...  7.57 us
    unnamed x16, local copies, waits for them, and re-layouts  6.01 us
    pallas_call x1, Pallas kernels, local(): pl.pallas_call(grad_kernel, grid_spec=pltpu.PrefetchScalarGridSpec(num_sc...  4.92 us
    pallas_call x1, Pallas kernels, local(): pl.pallas_call(posterior_kernel, in_specs=[vmem()] * 3, out_specs=[vmem()...  4.6 us

profile of v8, /device:TPU:0, one launch (start us, length us, event | category | flops | bytes accessed | tf_op | source)
XLA Modules:
  0.0 97.4 jit_solution(16627376859402319070)
XLA Ops:
  0.6 1.0 %copy.12 = f32[36,512]{0,1:T(8,128)S(1)} copy(f32[36,512]{1,0:T(8,128)} %param.12) | data formatting | bytes 147456 | tf_op args[3]
  1.7 0.1 copy.13
  1.8 0.1 reshape.24.rr_ref
  1.9 0.0 copy-start
  1.9 2.2 %copy-done = bf16[64,64,512]{2,1,0:T(8,128)(2,1)S(1)} copy-done((bf16[64,64,512]{2,1,0:T(8,128)(2,1)S(1)}, bf16[64,64,512]{2,1,0:T(8,128)(2,1)}, u32[]{:S(2)}) %copy-start) | copy-done | bytes 4194328
  4.1 0.0 copy-start.1
  4.1 0.9 copy-done.1
  5.0 0.0 copy-start.2
  5.0 0.7 copy-done.2
  5.7 0.0 copy-start.5
  5.7 0.7 copy-done.5
  6.3 0.0 copy-start.3
  6.3 0.0 copy-start.4
  6.3 11.3 %transform.1 = (bf16[128,64,512]{2,1,0:T(8,128)(2,1)S(1)}, bf16[64,64,512]{2,1,0:T(8,128)(2,1)S(1)}, s32[8,128]{1,0:T(8,128)S(1)}, s32[8,128]{1,0:T(8,128)S(1)}) custom-call(bf16[128,64,512]{2,1,0:T(8,128)(2,1)} %image_ref.1, bf16[64,64,512]{2,1,0:T(8,128)(2,1)S(1)} %copy-done, bf16[2,256,256]{2,1,0:T(8,128)(2,1)S(1)} %copy-done.1, s32[1,128]{1,0:T(1,128)S(1)} %bitcast.20, ...), custom_call_target="tpu_custom_call" | custom-call | tf_op jit(solution)/shard_map/transform/pallas_call | solution.py:585
  17.7 0.0 copy-done.3
  17.7 0.0 copy-done.4
  17.7 7.6 %scores.1 = (f32[256,128]{1,0:T(8,128)S(1)}, f32[8,128]{1,0:T(8,128)S(1)}, s32[64]{0:T(128)S(1)}, s32[256]{0:T(256)S(1)}) custom-call(s32[8,128]{1,0:T(8,128)S(1)} %get-tuple-element.17.ids_ref, bf16[128,64,512]{2,1,0:T(8,128)(2,1)S(1)} %get-tuple-element.18.xh_ref, bf16[64,64,512]{2,1,0:T(8,128)(2,1)S(1)} %get-tuple-element.19.rh_ref, ...), custom_call_target="tpu_custom_call" | custom-call | tf_op jit(solution)/shard_map/scores/pallas_call | solution.py:620
  25.3 4.6 %posterior.1 = (f32[256,768]{1,0:T(8,128)S(1)}, f32[256,128]{1,0:T(8,128)S(1)}, f32[1,128]{1,0:T(1,128)S(1)}) custom-call(f32[256,128]{1,0:T(8,128)S(1)} %get-tuple-element.22.scores_ref, f32[8,128]{1,0:T(8,128)S(1)} %get-tuple-element.23.stats_ref, f32[36,512]{1,0:T(8,128)S(1)} %reshape.24.rr_ref), custom_call_target="tpu_custom_call" | custom-call | tf_op jit(solution)/shard_map/posterior/pallas_call | solution.py:657
  29.9 4.9 %gradient.1 = (bf16[64,64,512]{2,1,0:T(8,128)(2,1)S(1)}, f32[64,128]{1,0:T(8,128)S(1)}) custom-call(s32[64]{0:T(128)S(1)} %get-tuple-element.20.head, s32[256]{0:T(256)S(1)} %get-tuple-element.21.nxt, bf16[128,64,512]{2,1,0:T(8,128)(2,1)S(1)} %get-tuple-element.18.xh_ref, bf16[64,64,512]{2,1,0:T(8,128)(2,1)S(1)} %get-tuple-element.19.rh_ref, ...), custom_call_target="tpu_custom_call" | custom-call | tf_op jit(solution)/shard_map/gradient/pallas_call | solution.py:681
  34.8 0.0 copy-start.6
  34.8 60.7 %reduce_over_dp.1 = (bf16[8,64,512]{2,1,0:T(8,128)(2,1)S(1)}, f32[1,128]{1,0:T(1,128)S(1)}) custom-call(bf16[4,2,8,64,512]{4,3,2,1,0:T(8,128)(2,1)S(1)} %bitcast.15, f32[8,8,128]{2,1,0:T(8,128)S(1)} %bitcast.16, f32[1,128]{1,0:T(1,128)S(1)} %get-tuple-element.28.evid_ref, s32[8,128]{1,0:T(8,128)S(1)} %get-tuple-element.29.slots_ref), custom_call_target="tpu_custom_call" | custom-call | tf_op jit(solution)/shard_map/reduce_over_dp/pallas_call | solution.py:531
  95.5 0.0 copy-done.6
  95.5 1.4 %convolution_bitcast_fusion = f32[1,8,64,512]{3,2,1,0:T(8,128)} fusion(bf16[8,64,512]{2,1,0:T(8,128)(2,1)S(1)} %get-tuple-element.30, bf16[512,512,1]{1,0,2:T(8,128)(2,1)S(1)} %copy-done.6), kind=kOutput, calls=%fused_computation | convolution fusion | flops 268435456 | bytes 2097152 | tf_op jit(solution)/shard_map/dot_general | solution.py:706
  96.9 0.5 copy.15
Async XLA Ops:
  1.9 2.2 %copy-start = (bf16[64,64,512]{2,1,0:T(8,128)(2,1)S(1)}, bf16[64,64,512]{2,1,0:T(8,128)(2,1)}, u32[]{:S(2)}) copy-start(bf16[64,64,512]{2,1,0:T(8,128)(2,1)} %refs_ref.1) | copy-start | bytes 12582916
  4.1 0.9 copy-start.1
  5.0 0.7 copy-start.2
  5.7 0.7 copy-start.5
  6.3 11.3 %copy-start.3 = (f32[64]{0:T(128)S(1)}, f32[64]{0:T(128)}, u32[]{:S(2)}) copy-start(f32[64]{0:T(128)} %param.13) | copy-start | bytes 772
  6.3 11.4 %copy-start.4 = (s32[64]{0:T(128)S(1)}, s32[64]{0:T(128)}, u32[]{:S(2)}) copy-start(s32[64]{0:T(128)} %param.15) | copy-start | bytes 772
  34.8 60.7 %copy-start.6 = (bf16[512,512,1]{1,0,2:T(8,128)(2,1)S(1)}, bf16[512,512,1]{1,0,2:T(8,128)(2,1)}, u32[]{:S(2)}) copy-start(bf16[512,512,1]{1,0,2:T(8,128)(2,1)} %constant.6) | copy-start | bytes 1572868
